TPU v7x, 256 devices: a whole 4x4x8 slice. The times are simulated.
256 devices in a mesh: tm: 64 (over x, z, core), head: 4 (over y).
Axes of the slice: x: 4, y: 4, z: 8, core: 2. Of those that a mesh axis runs over, the one named last changes fastest.
Arguments:
- queries: bfloat16 [49152, 2560], P(('tm', 'head')), may hold values from -6 to 6
- keys: bfloat16 [49152, 2560], P(('tm', 'head')), may hold values from -6 to 6
- values: bfloat16 [49152, 2560], P(('tm', 'head')), may hold values from -6 to 6
- upstream: bfloat16 [49152, 2560], P(('tm', 'head')), may hold values from -6 to 6
- window: int32 [128, 3], P('tm'), may hold values from -1 to 126, as said below
Outputs:
- grad_queries: bfloat16 [49152, 2560], P(('tm', 'head'))
- grad_keys: bfloat16 [49152, 2560], P(('tm', 'head'))
- grad_values: bfloat16 [49152, 2560], P(('tm', 'head'))
Inputs may be any that keep to these rules, and one draw needn't show every extreme that they name: Entry window[c, t] is either c - 1 - t or -1; slot 0 always holds c - 1 (so -1 for group 0).
All inputs are finite; a program needn't handle non-finite values.
Results may differ from a plain program's by a relative error of at most 0.009.
Values may be sent and summed in bfloat16 or wider, within the bound.
No kernel may reach another device: no remote copies, remote signals or barrier semaphores. Data moves between devices by JAX's collectives and lax.ppermute only.
A program may use at most 128 MiB of HBM per device.

v0:
```python
import math

import jax
import jax.numpy as jnp
from jax import lax
from jax.sharding import PartitionSpec as P

CH_DEV = 2
SPAN = 3
HD = 128


def shifted(block, axis, distance):
    devices = range(lax.axis_size(axis))
    route = [(i - distance, i) for i in devices if i - distance in devices]
    return lax.ppermute(block, axis, route)


def head_pass(q_head, k_head, v_head, g_head, allowed, score_scale):
    scores = jnp.dot(q_head, k_head.T, preferred_element_type=jnp.float32) * score_scale
    scores = jnp.where(allowed, scores, -1e30)
    row_top = jnp.max(scores, axis=1, keepdims=True)
    weights = jnp.exp(scores - row_top)
    row_total = jnp.sum(weights, axis=1, keepdims=True)
    probs = weights / row_total
    probs_b = probs.astype(jnp.bfloat16)
    output = jnp.dot(probs_b, v_head, preferred_element_type=jnp.float32)
    delta = jnp.sum(g_head.astype(jnp.float32) * output, axis=1, keepdims=True)
    dprobs = jnp.dot(g_head, v_head.T, preferred_element_type=jnp.float32)
    dscores = (probs * (dprobs - delta)).astype(jnp.bfloat16)
    grad_q = jnp.dot(dscores, k_head, preferred_element_type=jnp.float32) * score_scale
    part_k = jnp.dot(dscores.T, q_head, preferred_element_type=jnp.float32) * score_scale
    part_v = jnp.dot(probs_b.T, g_head, preferred_element_type=jnp.float32)
    return (grad_q, part_k, part_v, row_top, row_total, delta)


def to_rows(stacked):
    return jnp.transpose(stacked, (1, 0, 2)).reshape(
        stacked.shape[1], stacked.shape[0] * stacked.shape[2]
    )


def local(queries, keys, values, upstream, window):
    local_q, local_k, local_v, local_g = (
        lax.all_to_all(queries, "head", split_axis=1, concat_axis=0, tiled=True),
        lax.all_to_all(keys, "head", split_axis=1, concat_axis=0, tiled=True),
        lax.all_to_all(values, "head", split_axis=1, concat_axis=0, tiled=True),
        lax.all_to_all(upstream, "head", split_axis=1, concat_axis=0, tiled=True),
    )
    row_count = local_q.shape[0]
    group_rows = row_count // CH_DEV
    extra_rows = (SPAN - CH_DEV) * group_rows
    head_count = local_q.shape[1] // HD
    score_scale = 1.0 / math.sqrt(HD)
    near_k, near_v = shifted((local_k, local_v), "tm", 1)
    far_k, far_v = shifted(
        (local_k[row_count - extra_rows :], local_v[row_count - extra_rows :]), "tm", 2
    )
    context_keys = jnp.concatenate([far_k, near_k, local_k], 0)
    context_values = jnp.concatenate([far_v, near_v, local_v], 0)
    first_group = lax.axis_index("tm") * CH_DEV
    key_ids = first_group - SPAN + jnp.arange(SPAN + CH_DEV, dtype=jnp.int32)
    query_ids = first_group + jnp.arange(CH_DEV, dtype=jnp.int32)
    listed = jnp.any(window[:, :, None] == key_ids[None, None, :], axis=1)
    visible = (key_ids[None, :] == query_ids[:, None]) | listed & (key_ids[None, :] >= 0)

    def columns(source, head_index):
        return lax.dynamic_slice_in_dim(source, head_index * HD, HD, 1)

    allowed_all = jnp.repeat(jnp.repeat(visible, group_rows, 0), group_rows, 1)

    def per_head(head_index):
        return head_pass(
            columns(local_q, head_index),
            columns(context_keys, head_index),
            columns(context_values, head_index),
            columns(local_g, head_index),
            allowed_all,
            score_scale,
        )

    stack_q, stack_k, stack_v, tops, totals, deltas = lax.map(
        per_head, jnp.arange(head_count, dtype=jnp.int32)
    )
    grad_q = to_rows(stack_q).astype(jnp.bfloat16)
    context_gk = to_rows(stack_k)
    context_gv = to_rows(stack_v)
    far_gk = context_gk[:extra_rows]
    far_gv = context_gv[:extra_rows]
    near_gk = context_gk[extra_rows : SPAN * group_rows]
    near_gv = context_gv[extra_rows : SPAN * group_rows]
    own_gk = context_gk[SPAN * group_rows :]
    own_gv = context_gv[SPAN * group_rows :]
    back_k, back_v = (
        shifted(near_gk.astype(jnp.bfloat16), "tm", -1).astype(near_gk.dtype),
        shifted(near_gv.astype(jnp.bfloat16), "tm", -1).astype(near_gv.dtype),
    )
    own_gk = own_gk + back_k
    own_gv = own_gv + back_v
    distant_k, distant_v = (
        shifted(far_gk.astype(jnp.bfloat16), "tm", -2).astype(far_gk.dtype),
        shifted(far_gv.astype(jnp.bfloat16), "tm", -2).astype(far_gv.dtype),
    )
    own_gk = jnp.concatenate(
        [own_gk[: row_count - extra_rows], own_gk[row_count - extra_rows :] + distant_k], 0
    )
    own_gv = jnp.concatenate(
        [own_gv[: row_count - extra_rows], own_gv[row_count - extra_rows :] + distant_v], 0
    )
    return (
        lax.all_to_all(grad_q, "head", split_axis=0, concat_axis=1, tiled=True),
        lax.all_to_all(
            own_gk.astype(jnp.bfloat16), "head", split_axis=0, concat_axis=1, tiled=True
        ),
        lax.all_to_all(
            own_gv.astype(jnp.bfloat16), "head", split_axis=0, concat_axis=1, tiled=True
        ),
    )


def solution(mesh):
    return jax.shard_map(
        local,
        mesh=mesh,
        in_specs=(
            P(("tm", "head"), None),
            P(("tm", "head"), None),
            P(("tm", "head"), None),
            P(("tm", "head"), None),
            P("tm", None),
        ),
        out_specs=(P(("tm", "head"), None), P(("tm", "head"), None), P(("tm", "head"), None)),
        check_vma=False,
    )
```

profile of v0, /device:TPU:6, one launch (start us, length us, event | category | flops | bytes accessed | tf_op | source)
XLA Modules:
  0.0 308.3 jit_solution(12660184047404822235)
XLA Ops:
  3.0 4.6 %all-to-all-start.1 = ((bf16[192,4,640]{2,0,1:T(8,128)(2,1)}), bf16[192,4,640]{2,0,1:T(8,128)(2,1)S(1)}, u32[]{:S(2)}, u32[]{:S(2)}) async-start(bf16[192,4,640]{2,0,1:T(8,128)(2,1)} %bitcast.72), calls=%async_computation.1 | async-start | bytes 1966080 | tf_op jit(solution)/shard_map/all_to_all | solution.py:46
  8.6 13.4 %all-to-all-done.1 = bf16[192,4,640]{2,0,1:T(8,128)(2,1)S(1)} async-done(((bf16[192,4,640]{2,0,1:T(8,128)(2,1)}), bf16[192,4,640]{2,0,1:T(8,128)(2,1)S(1)}, u32[]{:S(2)}, u32[]{:S(2)}) %all-to-all-start.1) | async-done | bytes 983072 | tf_op jit(solution)/shard_map/all_to_all | solution.py:46
  28.4 10.5 %all-to-all-done.3 = bf16[192,4,640]{2,0,1:T(8,128)(2,1)S(1)} async-done(((bf16[192,4,640]{2,0,1:T(8,128)(2,1)}), bf16[192,4,640]{2,0,1:T(8,128)(2,1)S(1)}, u32[]{:S(2)}, u32[]{:S(2)}) %all-to-all-start.3) | async-done | bytes 983072 | tf_op jit(solution)/shard_map/all_to_all | solution.py:47
  56.1 4.8 %all-to-all-start.2 = ((bf16[192,4,640]{2,0,1:T(8,128)(2,1)}), bf16[192,4,640]{2,0,1:T(8,128)(2,1)}, u32[]{:S(2)}, u32[]{:S(2)}) async-start(bf16[192,4,640]{2,0,1:T(8,128)(2,1)} %bitcast.104), calls=%async_computation.2 | async-start | bytes 1966080 | tf_op jit(solution)/shard_map/all_to_all | solution.py:48
  60.9 4.8 %collective-permute-done = bf16[384,640]{1,0:T(8,128)(2,1)} collective-permute-done((bf16[384,640]{1,0:T(8,128)(2,1)}, bf16[384,640]{1,0:T(8,128)(2,1)}, u32[]{:S(2)}, u32[]{:S(2)}) %collective-permute-start) | collective-permute-done | bytes 491552 | tf_op jit(solution)/shard_map/ppermute | solution.py:16
  68.6 7.6 %collective-permute-done.2 = bf16[384,640]{1,0:T(8,128)(2,1)} collective-permute-done((bf16[384,640]{1,0:T(8,128)(2,1)}, bf16[384,640]{1,0:T(8,128)(2,1)}, u32[]{:S(2)}, u32[]{:S(2)}) %collective-permute-start.2) | collective-permute-done | bytes 491552 | tf_op jit(solution)/shard_map/ppermute | solution.py:16
  79.2 137.7 %while.15 = (s32[]{:T(128)}, bf16[5,768,128]{2,1,0:T(8,128)(2,1)}, f32[5,1920,128]{1,2,0:T(8,128)}, f32[5,1920,128]{1,2,0:T(8,128)}, s32[5]{0:T(128)S(1)}, /*ind...) while((s32[]{:T(128)}, bf16[5,768,128]{2,1,0:T(8,128)(2,1)}, ...), condition=%wide.region_5.6_spmd.clone, body=%wide.region_1.5_spmd.clone.sunk | while | flops 2283255552 | bytes 97544248 | solution.py:82
  90.6 4.0 %fusion.65 = f32[768]{0:T(1024)S(1)} fusion(f32[768,1920]{1,0:T(8,128)} %fusion.64, bf16[1920,640]{1,0:T(8,128)(2,1)} %get-tuple-element.248, s32[]{:T(128)S(6)} %select_n.14, bf16[768,128]{0,1:T(8,128)(2,1)S(1)} %copy.92), kind=kOutput, calls=%fused_computation.17.clone.1 | convolution fusion | flops 379256064 | bytes 6589444 | tf_op jit(solution)/shard_map/while/body/eval_jaxpr/dot_general | solution.py:27
  102.5 4.2 %fusion.68 = f32[5,1920,128]{1,2,0:T(8,128)} fusion(f32[5,1920,128]{1,2,0:T(8,128)} %get-tuple-element.229, s32[]{:T(128)S(6)} %copy.101, bf16[768,128]{1,0:T(8,128)(2,1)S(1)} %constant_dynamic-slice_fusion.2, f32[768,1920]{1,0:T(8,128)} %fusion.64), kind=kOutput, calls=%fused_computation.9.clone.1 | convolution fusion | flops 378961920 | bytes 7077892 | tf_op jit(solution)/shard_map/while/body/eval_jaxpr/dot_general | solution.py:33
  118.1 4.0 %fusion.65 = f32[768]{0:T(1024)S(1)} fusion(f32[768,1920]{1,0:T(8,128)} %fusion.64, bf16[1920,640]{1,0:T(8,128)(2,1)} %get-tuple-element.248, s32[]{:T(128)S(6)} %select_n.14, bf16[768,128]{0,1:T(8,128)(2,1)S(1)} %copy.92), kind=kOutput, calls=%fused_computation.17.clone.1 | convolution fusion | flops 379256064 | bytes 6589444 | tf_op jit(solution)/shard_map/while/body/eval_jaxpr/dot_general | solution.py:27
  130.0 4.3 %fusion.68 = f32[5,1920,128]{1,2,0:T(8,128)} fusion(f32[5,1920,128]{1,2,0:T(8,128)} %get-tuple-element.229, s32[]{:T(128)S(6)} %copy.101, bf16[768,128]{1,0:T(8,128)(2,1)S(1)} %constant_dynamic-slice_fusion.2, f32[768,1920]{1,0:T(8,128)} %fusion.64), kind=kOutput, calls=%fused_computation.9.clone.1 | convolution fusion | flops 378961920 | bytes 7077892 | tf_op jit(solution)/shard_map/while/body/eval_jaxpr/dot_general | solution.py:33
  145.6 4.0 %fusion.65 = f32[768]{0:T(1024)S(1)} fusion(f32[768,1920]{1,0:T(8,128)} %fusion.64, bf16[1920,640]{1,0:T(8,128)(2,1)} %get-tuple-element.248, s32[]{:T(128)S(6)} %select_n.14, bf16[768,128]{0,1:T(8,128)(2,1)S(1)} %copy.92), kind=kOutput, calls=%fused_computation.17.clone.1 | convolution fusion | flops 379256064 | bytes 6589444 | tf_op jit(solution)/shard_map/while/body/eval_jaxpr/dot_general | solution.py:27
  157.6 4.3 %fusion.68 = f32[5,1920,128]{1,2,0:T(8,128)} fusion(f32[5,1920,128]{1,2,0:T(8,128)} %get-tuple-element.229, s32[]{:T(128)S(6)} %copy.101, bf16[768,128]{1,0:T(8,128)(2,1)S(1)} %constant_dynamic-slice_fusion.2, f32[768,1920]{1,0:T(8,128)} %fusion.64), kind=kOutput, calls=%fused_computation.9.clone.1 | convolution fusion | flops 378961920 | bytes 7077892 | tf_op jit(solution)/shard_map/while/body/eval_jaxpr/dot_general | solution.py:33
  173.2 4.0 %fusion.65 = f32[768]{0:T(1024)S(1)} fusion(f32[768,1920]{1,0:T(8,128)} %fusion.64, bf16[1920,640]{1,0:T(8,128)(2,1)} %get-tuple-element.248, s32[]{:T(128)S(6)} %select_n.14, bf16[768,128]{0,1:T(8,128)(2,1)S(1)} %copy.92), kind=kOutput, calls=%fused_computation.17.clone.1 | convolution fusion | flops 379256064 | bytes 6589444 | tf_op jit(solution)/shard_map/while/body/eval_jaxpr/dot_general | solution.py:27
  185.1 4.3 %fusion.68 = f32[5,1920,128]{1,2,0:T(8,128)} fusion(f32[5,1920,128]{1,2,0:T(8,128)} %get-tuple-element.229, s32[]{:T(128)S(6)} %copy.101, bf16[768,128]{1,0:T(8,128)(2,1)S(1)} %constant_dynamic-slice_fusion.2, f32[768,1920]{1,0:T(8,128)} %fusion.64), kind=kOutput, calls=%fused_computation.9.clone.1 | convolution fusion | flops 378961920 | bytes 7077892 | tf_op jit(solution)/shard_map/while/body/eval_jaxpr/dot_general | solution.py:33
  200.7 4.0 %fusion.65 = f32[768]{0:T(1024)S(1)} fusion(f32[768,1920]{1,0:T(8,128)} %fusion.64, bf16[1920,640]{1,0:T(8,128)(2,1)} %get-tuple-element.248, s32[]{:T(128)S(6)} %select_n.14, bf16[768,128]{0,1:T(8,128)(2,1)S(1)} %copy.92), kind=kOutput, calls=%fused_computation.17.clone.1 | convolution fusion | flops 379256064 | bytes 6589444 | tf_op jit(solution)/shard_map/while/body/eval_jaxpr/dot_general | solution.py:27
  212.7 4.3 %fusion.68 = f32[5,1920,128]{1,2,0:T(8,128)} fusion(f32[5,1920,128]{1,2,0:T(8,128)} %get-tuple-element.229, s32[]{:T(128)S(6)} %copy.101, bf16[768,128]{1,0:T(8,128)(2,1)S(1)} %constant_dynamic-slice_fusion.2, f32[768,1920]{1,0:T(8,128)} %fusion.64), kind=kOutput, calls=%fused_computation.9.clone.1 | convolution fusion | flops 378961920 | bytes 7077892 | tf_op jit(solution)/shard_map/while/body/eval_jaxpr/dot_general | solution.py:33
  216.9 4.6 %bitcast_convert_fusion = (bf16[1920,5,128]{0,2,1:T(8,128)(2,1)S(1)}, bf16[1920,5,128]{0,2,1:T(8,128)(2,1)S(1)}) fusion(f32[5,1920,128]{1,2,0:T(8,128)} %get-tuple-element.59, f32[5,1920,128]{1,2,0:T(8,128)} %get-tuple-element.58), kind=kLoop, calls=%fused_computation.53 | loop fusion | flops 2457600 | bytes 14745600 | tf_op jit(solution)/shard_map/convert.4
  222.6 10.3 %collective-permute-start.4 = (bf16[768,640]{0,1:T(8,128)(2,1)}, bf16[768,640]{0,1:T(8,128)(2,1)}, u32[]{:S(2)}, u32[]{:S(2)}) collective-permute-start(bf16[768,640]{0,1:T(8,128)(2,1)} %bitcast.15), channel_id=1, source_target_pairs={{4,0},{8,4},{12,8},{16,12},{20,16},{24,20},{28,24},{32,28},{36,32}... | collective-permute-start | bytes 2949128 | tf_op jit(solution)/shard_map/ppermute | solution.py:16
  242.5 4.8 %all-to-all-start.4 = ((bf16[4,192,640]{2,1,0:T(8,128)(2,1)}), bf16[4,192,640]{2,1,0:T(8,128)(2,1)S(1)}, u32[]{:S(2)}, u32[]{:S(2)}) async-start(bf16[4,192,640]{2,1,0:T(8,128)(2,1)} %reshape.82), calls=%async_computation.4 | async-start | bytes 1966080 | tf_op jit(solution)/shard_map/all_to_all | solution.py:111
  255.1 16.0 %collective-permute-done.5 = bf16[384,640]{0,1:T(8,128)(2,1)} collective-permute-done((bf16[384,640]{0,1:T(8,128)(2,1)}, bf16[384,640]{0,1:T(8,128)(2,1)}, u32[]{:S(2)}, u32[]{:S(2)}) %collective-permute-start.5) | collective-permute-done | bytes 491552 | tf_op jit(solution)/shard_map/ppermute | solution.py:16
  275.6 4.8 %all-to-all-start.5 = ((bf16[4,192,640]{2,1,0:T(8,128)(2,1)}), bf16[4,192,640]{2,1,0:T(8,128)(2,1)}, u32[]{:S(2)}, u32[]{:S(2)}) async-start(bf16[4,192,640]{2,1,0:T(8,128)(2,1)} %bitcast.105), calls=%async_computation.5 | async-start | bytes 1966080 | tf_op jit(solution)/shard_map/all_to_all | solution.py:112
  284.5 8.7 %all-to-all-done.5 = bf16[4,192,640]{2,1,0:T(8,128)(2,1)} async-done(((bf16[4,192,640]{2,1,0:T(8,128)(2,1)}), bf16[4,192,640]{2,1,0:T(8,128)(2,1)}, u32[]{:S(2)}, u32[]{:S(2)}) %all-to-all-start.5) | async-done | bytes 983072 | tf_op jit(solution)/shard_map/all_to_all | solution.py:112
  300.0 7.2 %all-to-all-done.6 = bf16[4,192,640]{2,1,0:T(8,128)(2,1)S(1)} async-done(((bf16[4,192,640]{2,1,0:T(8,128)(2,1)}), bf16[4,192,640]{2,1,0:T(8,128)(2,1)S(1)}, u32[]{:S(2)}, u32[]{:S(2)}) %all-to-all-start.6) | async-done | bytes 983072 | tf_op jit(solution)/shard_map/all_to_all | solution.py:115
  (160 shorter events, 160.4 us)
Async XLA Ops:
  0.6 6.9 %copy-start.1 = (bf16[192,2560]{1,0:T(8,128)(2,1)S(1)}, bf16[192,2560]{1,0:T(8,128)(2,1)}, u32[]{:S(2)}) copy-start(bf16[192,2560]{1,0:T(8,128)(2,1)} %param.9) | copy-start | bytes 2949124
  3.0 24.4 %copy-start.2 = (bf16[192,2560]{1,0:T(8,128)(2,1)S(1)}, bf16[192,2560]{1,0:T(8,128)(2,1)}, u32[]{:S(2)}) copy-start(bf16[192,2560]{1,0:T(8,128)(2,1)} %param.7) | copy-start | bytes 2949124
  3.0 19.0 %all-to-all-start.1 = ((bf16[192,4,640]{2,0,1:T(8,128)(2,1)}), bf16[192,4,640]{2,0,1:T(8,128)(2,1)S(1)}, u32[]{:S(2)}, u32[]{:S(2)}) async-start(bf16[192,4,640]{2,0,1:T(8,128)(2,1)} %bitcast.72), calls=%async_computation.1 | async-start | bytes 1966080 | tf_op jit(solution)/shard_map/all_to_all | solution.py:46
  21.9 17.0 %all-to-all-start.3 = ((bf16[192,4,640]{2,0,1:T(8,128)(2,1)}), bf16[192,4,640]{2,0,1:T(8,128)(2,1)S(1)}, u32[]{:S(2)}, u32[]{:S(2)}) async-start(bf16[192,4,640]{2,0,1:T(8,128)(2,1)} %bitcast.70), calls=%async_computation.3 | async-start | bytes 1966080 | tf_op jit(solution)/shard_map/all_to_all | solution.py:47
  25.5 40.2 %collective-permute-start.1 = (bf16[768,640]{1,0:T(8,128)(2,1)S(1)}, bf16[768,640]{1,0:T(8,128)(2,1)}, u32[]{:S(2)}, u32[]{:S(2)}) collective-permute-start(bf16[768,640]{1,0:T(8,128)(2,1)S(1)} %bitcast.96), channel_id=1, source_target_pairs={{0,4},{4,8},{8,12},{12,16},{16,20},{20,24},{24,28},{28,32},{32,36}... | collective-permute-start | bytes 2949128 | tf_op jit(solution)/shard_map/ppermute | solution.py:16
  28.4 22.9 %copy-start.6 = (s32[2,3]{1,0:T(2,128)S(1)}, s32[2,3]{1,0:T(2,128)}, u32[]{:S(2)}) copy-start(s32[2,3]{1,0:T(2,128)} %param.11) | copy-start | bytes 76
  38.9 17.2 %all-to-all-start = ((bf16[192,4,640]{2,0,1:T(8,128)(2,1)}), bf16[192,4,640]{2,0,1:T(8,128)(2,1)S(1)}, u32[]{:S(2)}, u32[]{:S(2)}) async-start(bf16[192,4,640]{2,0,1:T(8,128)(2,1)} %bitcast.103), calls=%async_computation | async-start | bytes 1966080 | tf_op jit(solution)/shard_map/all_to_all | solution.py:45
  42.4 33.8 %collective-permute-start.3 = (bf16[768,640]{1,0:T(8,128)(2,1)S(1)}, bf16[768,640]{1,0:T(8,128)(2,1)}, u32[]{:S(2)}, u32[]{:S(2)}) collective-permute-start(bf16[768,640]{1,0:T(8,128)(2,1)S(1)} %bitcast.99), channel_id=1, source_target_pairs={{0,4},{4,8},{8,12},{12,16},{16,20},{20,24},{24,28},{28,32},{32,36}... | collective-permute-start | bytes 2949128 | tf_op jit(solution)/shard_map/ppermute | solution.py:16
  45.2 20.5 %collective-permute-start = (bf16[384,640]{1,0:T(8,128)(2,1)}, bf16[384,640]{1,0:T(8,128)(2,1)}, u32[]{:S(2)}, u32[]{:S(2)}) collective-permute-start(bf16[384,640]{1,0:T(8,128)(2,1)} %bitcast.3), channel_id=1, source_target_pairs={{0,8},{4,12},{8,16},{12,20},{16,24},{20,28},{24,32},{28,36},{32,40... | collective-permute-start | bytes 1474568 | tf_op jit(solution)/shard_map/ppermute | solution.py:16
  52.2 24.0 %collective-permute-start.2 = (bf16[384,640]{1,0:T(8,128)(2,1)}, bf16[384,640]{1,0:T(8,128)(2,1)}, u32[]{:S(2)}, u32[]{:S(2)}) collective-permute-start(bf16[384,640]{1,0:T(8,128)(2,1)} %bitcast.8), channel_id=1, source_target_pairs={{0,8},{4,12},{8,16},{12,20},{16,24},{20,28},{24,32},{28,36},{32,40... | collective-permute-start | bytes 1474568 | tf_op jit(solution)/shard_map/ppermute | solution.py:16
  56.1 23.1 %all-to-all-start.2 = ((bf16[192,4,640]{2,0,1:T(8,128)(2,1)}), bf16[192,4,640]{2,0,1:T(8,128)(2,1)}, u32[]{:S(2)}, u32[]{:S(2)}) async-start(bf16[192,4,640]{2,0,1:T(8,128)(2,1)} %bitcast.104), calls=%async_computation.2 | async-start | bytes 1966080 | tf_op jit(solution)/shard_map/all_to_all | solution.py:48
  90.5 4.5 %copy-start = (f32[768,1920]{1,0:T(8,128)S(1)}, f32[768,1920]{1,0:T(8,128)}, u32[]{:S(2)}) copy-start(f32[768,1920]{1,0:T(8,128)} %fusion.64) | copy-start | bytes 17694724 | tf_op jit(solution)/shard_map/while
  118.1 4.5 %copy-start = (f32[768,1920]{1,0:T(8,128)S(1)}, f32[768,1920]{1,0:T(8,128)}, u32[]{:S(2)}) copy-start(f32[768,1920]{1,0:T(8,128)} %fusion.64) | copy-start | bytes 17694724 | tf_op jit(solution)/shard_map/while
  145.6 4.5 %copy-start = (f32[768,1920]{1,0:T(8,128)S(1)}, f32[768,1920]{1,0:T(8,128)}, u32[]{:S(2)}) copy-start(f32[768,1920]{1,0:T(8,128)} %fusion.64) | copy-start | bytes 17694724 | tf_op jit(solution)/shard_map/while
  173.2 4.5 %copy-start = (f32[768,1920]{1,0:T(8,128)S(1)}, f32[768,1920]{1,0:T(8,128)}, u32[]{:S(2)}) copy-start(f32[768,1920]{1,0:T(8,128)} %fusion.64) | copy-start | bytes 17694724 | tf_op jit(solution)/shard_map/while
  200.7 4.5 %copy-start = (f32[768,1920]{1,0:T(8,128)S(1)}, f32[768,1920]{1,0:T(8,128)}, u32[]{:S(2)}) copy-start(f32[768,1920]{1,0:T(8,128)} %fusion.64) | copy-start | bytes 17694724 | tf_op jit(solution)/shard_map/while
  221.6 18.2 %copy-start.5 = (bf16[5,768,128]{2,1,0:T(8,128)(2,1)S(1)}, bf16[5,768,128]{2,1,0:T(8,128)(2,1)}, u32[]{:S(2)}) copy-start(bf16[5,768,128]{2,1,0:T(8,128)(2,1)} %get-tuple-element.57) | copy-start | bytes 2949124
  222.6 31.0 %collective-permute-start.4 = (bf16[768,640]{0,1:T(8,128)(2,1)}, bf16[768,640]{0,1:T(8,128)(2,1)}, u32[]{:S(2)}, u32[]{:S(2)}) collective-permute-start(bf16[768,640]{0,1:T(8,128)(2,1)} %bitcast.15), channel_id=1, source_target_pairs={{4,0},{8,4},{12,8},{16,12},{20,16},{24,20},{28,24},{32,28},{36,32}... | collective-permute-start | bytes 2949128 | tf_op jit(solution)/shard_map/ppermute | solution.py:16
  233.9 46.5 %collective-permute-start.6 = (bf16[768,640]{0,1:T(8,128)(2,1)}, bf16[768,640]{0,1:T(8,128)(2,1)}, u32[]{:S(2)}, u32[]{:S(2)}) collective-permute-start(bf16[768,640]{0,1:T(8,128)(2,1)} %bitcast.21), channel_id=1, source_target_pairs={{4,0},{8,4},{12,8},{16,12},{20,16},{24,20},{28,24},{32,28},{36,32}... | collective-permute-start | bytes 2949128 | tf_op jit(solution)/shard_map/ppermute | solution.py:16
  236.6 34.5 %collective-permute-start.5 = (bf16[384,640]{0,1:T(8,128)(2,1)}, bf16[384,640]{0,1:T(8,128)(2,1)}, u32[]{:S(2)}, u32[]{:S(2)}) collective-permute-start(bf16[384,640]{0,1:T(8,128)(2,1)} %bitcast.16), channel_id=1, source_target_pairs={{8,0},{12,4},{16,8},{20,12},{24,16},{28,20},{32,24},{36,28},{40,32... | collective-permute-start | bytes 1474568 | tf_op jit(solution)/shard_map/ppermute | solution.py:16
  242.5 33.1 %all-to-all-start.4 = ((bf16[4,192,640]{2,1,0:T(8,128)(2,1)}), bf16[4,192,640]{2,1,0:T(8,128)(2,1)S(1)}, u32[]{:S(2)}, u32[]{:S(2)}) async-start(bf16[4,192,640]{2,1,0:T(8,128)(2,1)} %reshape.82), calls=%async_computation.4 | async-start | bytes 1966080 | tf_op jit(solution)/shard_map/all_to_all | solution.py:111
  250.7 31.3 %collective-permute-start.7 = (bf16[384,640]{0,1:T(8,128)(2,1)S(1)}, bf16[384,640]{0,1:T(8,128)(2,1)}, u32[]{:S(2)}, u32[]{:S(2)}) collective-permute-start(bf16[384,640]{0,1:T(8,128)(2,1)S(1)} %bitcast.115), channel_id=1, source_target_pairs={{8,0},{12,4},{16,8},{20,12},{24,16},{28,20},{32,24},{36,28},{40,32... | collective-permute-start | bytes 1474568 | tf_op jit(solution)/shard_map/ppermute | solution.py:16
  275.6 17.6 %all-to-all-start.5 = ((bf16[4,192,640]{2,1,0:T(8,128)(2,1)}), bf16[4,192,640]{2,1,0:T(8,128)(2,1)}, u32[]{:S(2)}, u32[]{:S(2)}) async-start(bf16[4,192,640]{2,1,0:T(8,128)(2,1)} %bitcast.105), calls=%async_computation.5 | async-start | bytes 1966080 | tf_op jit(solution)/shard_map/all_to_all | solution.py:112
  293.2 14.0 %all-to-all-start.6 = ((bf16[4,192,640]{2,1,0:T(8,128)(2,1)}), bf16[4,192,640]{2,1,0:T(8,128)(2,1)S(1)}, u32[]{:S(2)}, u32[]{:S(2)}) async-start(bf16[4,192,640]{2,1,0:T(8,128)(2,1)} %bitcast.23), calls=%async_computation.6 | async-start | bytes 1966080 | tf_op jit(solution)/shard_map/all_to_all | solution.py:115
  (10 other events, 15.1 us)
where the time goes:
time: 310 us; the launch traced here: 308 us
  matrix products  79.4 us (26%)
  waiting for transfers between devices  68.1 us (22%)
  starting transfers between devices  59 us (19%)
  local copies, waits for them, and re-layouts  57.8 us (19%)
  other arithmetic  39.4 us (13%)
  loops' own time  3.67 us (1%)
    ppermute x8, starting transfers between devices, shifted(): return lax.ppermute(block, axis, route)  29.6 us
    ppermute x8, waiting for transfers between devices, shifted(): return lax.ppermute(block, axis, route)  28.3 us
    dot_general x5, matrix products, head_pass(): part_v = jnp.dot(probs_b.T, g_head, preferred_element_type=jnp.float32)  21.3 us
    dot_general x5, matrix products, head_pass(): output = jnp.dot(probs_b, v_head, preferred_element_type=jnp.float32)  20.1 us
    div x5, other arithmetic, head_pass(): probs = weights / row_total  17.5 us
    all_to_all x1, waiting for transfers between devices, local(): lax.all_to_all(keys, 'head', split_axis=1, concat_axis=0, tiled=True)  13.4 us
    dot_general x5, matrix products, head_pass(): jnp.dot(q_head, k_head.T, preferred_element_type=jnp.float32) * score_scale  12.8 us
    all_to_all x1, waiting for transfers between devices, local(): lax.all_to_all(values, 'head', split_axis=1, concat_axis=0, tiled=True)  10.5 us
  transfers between devices with their start and end apart: 15, of which 7 were waited for; matrix products, arithmetic and copies ran while one was open for 11% of the time, Pallas kernels for 0%

commit v1 on v0

v1 whole, which is shorter than its diff:
```python
import functools
import math

import jax
import jax.numpy as jnp
from jax import lax
from jax.experimental import pallas as pl
from jax.experimental.pallas import tpu as pltpu
from jax.sharding import PartitionSpec as P

HD = 128
GR = 384
PR = 192
HEADS_DEV = 5
CHUNKS = (2, 2, 1)
SCALE = 1.0 / math.sqrt(HD)
SCALE2 = SCALE * math.log2(math.e)
NT = (((1,), (1,)), ((), ()))
TN = (((0,), (0,)), ((), ()))
BF = jnp.bfloat16
F32 = jnp.float32
VM = pl.BlockSpec(memory_space=pltpu.VMEM)


def dot(a, b, dims=(((1,), (0,)), ((), ()))):
    return lax.dot_general(a, b, dims, preferred_element_type=F32)


def cost(flops, nbytes):
    return pl.CostEstimate(flops=int(flops), bytes_accessed=int(nbytes), transcendentals=0)


def head_shift(block, distance):
    n = lax.axis_size("head")
    return lax.ppermute(block, "head", [(i, (i + distance) % n) for i in range(n)])


def tm_shift(block, distance):
    devices = range(lax.axis_size("tm"))
    route = [(i - distance, i) for i in devices if i - distance in devices]
    return lax.ppermute(block, "tm", route)


def head_columns(owner, off, w):
    return pl.ds(pl.multiple_of(owner * (HEADS_DEV * HD) + off, HD), w)


def piece_rows(owner):
    return pl.ds(pl.multiple_of(owner * PR, 64), PR)


def pack_kernel(offsets, k, v, q, g, *outs):
    me = lax.axis_index("head")
    for c, (off, w) in enumerate(offsets):
        for d, out in zip((1, 3, 2), outs[3 * c : 3 * c + 3]):
            cols = head_columns(lax.rem(me + d, 4), off, w)
            for i, src in enumerate((k, v, q, g)):
                out[i] = src[:, cols]


def pack(k, v, q, g, offsets):
    outs = [jax.ShapeDtypeStruct((4, PR, w), BF) for _, w in offsets for _ in range(3)]
    return pl.pallas_call(
        functools.partial(pack_kernel, offsets),
        in_specs=[VM] * 4,
        out_specs=[VM] * len(outs),
        out_shape=outs,
        compiler_params=pltpu.CompilerParams(vmem_limit_bytes=40 << 20),
        cost_estimate=cost(0, 24 * PR * 640 * 2),
        name="pack",
    )(k, v, q, g)


def join_kernel(off, w, k, v, r1, r2, r3, own, last):
    me = lax.axis_index("head")
    cols = head_columns(me, off, w)
    own[0, piece_rows(me), :] = k[:, cols]
    own[1, piece_rows(me), :] = v[:, cols]
    for d, r in ((1, r1), (3, r2), (2, r3)):
        rows = piece_rows(lax.rem(me + 4 - d, 4))
        own[0, rows, :] = r[0]
        own[1, rows, :] = r[1]
    last[...] = own[:, GR:, :]


def join(k, v, r, off, w):
    return pl.pallas_call(
        functools.partial(join_kernel, off, w),
        in_specs=[VM] * 5,
        out_specs=[VM] * 2,
        out_shape=[
            jax.ShapeDtypeStruct((2, 2 * GR, w), BF),
            jax.ShapeDtypeStruct((2, GR, w), BF),
        ],
        compiler_params=pltpu.CompilerParams(vmem_limit_bytes=40 << 20),
        cost_estimate=cost(0, 6 * 2 * GR * w * 2),
        name="join",
    )(k, v, *r)


def attend_kernel(
    win, me_ref, near, far, own, q0, g0, r1, r2, r3,
    dq_ref, nearg, farg, owng, q_ref, g_ref, s_ref, d_ref,
):
    me = me_ref[0]
    q_ref[piece_rows(me), :] = q0[...]
    g_ref[piece_rows(me), :] = g0[...]
    for d, r in ((1, r1), (3, r2), (2, r3)):
        rows = piece_rows(lax.rem(me + 4 - d, 4))
        q_ref[rows, :] = r[0]
        g_ref[rows, :] = r[1]
    q = q_ref[...]
    g = g_ref[...]

    def hidden(c, slot):
        return jnp.where(win[c, slot] >= 0, 0.0, 1e30).astype(F32)

    lane = lax.broadcasted_iota(jnp.int32, (1, 2 * GR), 1)

    def lanes(a, b):
        return jnp.where(lane < GR, a, b)

    blocks = (
        (far, farg, 0, 0, 0, GR, jnp.full((1, GR), 1.0, F32) * hidden(0, 2)),
        (near, nearg, 0, 1, 0, 2 * GR, lanes(hidden(0, 1), hidden(1, 2))),
        (near, nearg, 1, 2, 0, 2 * GR, lanes(hidden(0, 0), hidden(1, 1))),
        (own, owng, 0, 3, 0, 2 * GR, lanes(0.0, hidden(1, 0))),
        (own, owng, 1, 4, GR, 2 * GR, jnp.zeros((1, GR), F32)),
    )

    def rows_of(i):
        return slice(i * GR, (i + 1) * GR)

    def combine(x, op):
        mid = op(op(x[1], x[2]), x[3])
        return jnp.concatenate([op(mid[:, :GR], x[0]), op(mid[:, GR:], x[4])], axis=1)

    tops = []
    for ref, _, i, j, lo, hi, hide in blocks:
        s = dot(ref[0, rows_of(i), :], q[lo:hi], NT)
        s_ref[rows_of(j), lo:hi] = s
        tops.append(jnp.max(s, axis=0, keepdims=True) * SCALE2 - hide)
    top = combine(tops, jnp.maximum)
    totals, deltas = [], []
    for ref, _, i, j, lo, hi, hide in blocks:
        dp = dot(ref[1, rows_of(i), :], g[lo:hi], NT)
        e = jnp.exp2(s_ref[rows_of(j), lo:hi] * SCALE2 - (top[:, lo:hi] + hide))
        s_ref[rows_of(j), lo:hi] = e
        d_ref[rows_of(j), lo:hi] = dp
        totals.append(jnp.sum(e, axis=0, keepdims=True))
        deltas.append(jnp.sum(e * dp, axis=0, keepdims=True))
    inverse = 1.0 / combine(totals, jnp.add)
    delta = combine(deltas, jnp.add) * inverse
    dq = [None, None]
    for ref, out, i, j, lo, hi, hide in blocks:
        p = s_ref[rows_of(j), lo:hi] * inverse[:, lo:hi]
        ds = (p * (d_ref[rows_of(j), lo:hi] - delta[:, lo:hi])).astype(BF)
        out[1, rows_of(i), :] = dot(p.astype(BF), g[lo:hi]).astype(out.dtype)
        out[0, rows_of(i), :] = (dot(ds, q[lo:hi]) * SCALE).astype(out.dtype)
        part = dot(ref[0, rows_of(i), :], ds, TN)
        if lo == 0:
            dq[0] = part[:, :GR] if dq[0] is None else dq[0] + part[:, :GR]
        if hi == 2 * GR:
            dq[1] = part[:, -GR:] if dq[1] is None else dq[1] + part[:, -GR:]
    for i in range(2):
        dq_ref[rows_of(i), :] = (dq[i].T * SCALE).astype(BF)


def attend(window, me, near, far, own, q, g, r, off, w):
    heads = w // HD

    def three(a, rows, first=0):
        return pl.BlockSpec((a, rows, HD), lambda h, win, m: (first, 0, h))

    def flat(rows):
        return pl.BlockSpec((rows, HD), lambda h, win, m: (0, h))

    mine = pl.BlockSpec((PR, HD), lambda h, win, m: (0, m[0] * HEADS_DEV + off // HD + h))
    sd = jax.ShapeDtypeStruct
    return pl.pallas_call(
        attend_kernel,
        grid_spec=pltpu.PrefetchScalarGridSpec(
            num_scalar_prefetch=2,
            grid=(heads,),
            in_specs=[three(2, 2 * GR), three(2, GR), three(2, 2 * GR), mine, mine]
            + [three(2, PR, 1)] * 3,
            out_specs=[flat(2 * GR), three(2, 2 * GR), three(2, GR), three(2, 2 * GR)],
            scratch_shapes=[
                pltpu.VMEM((2 * GR, HD), BF),
                pltpu.VMEM((2 * GR, HD), BF),
                pltpu.VMEM((5 * GR, 2 * GR), F32),
                pltpu.VMEM((5 * GR, 2 * GR), F32),
            ],
        ),
        out_shape=[
            sd((2 * GR, w), BF),
            sd((2, 2 * GR, w), BF),
            sd((2, GR, w), BF),
            sd((2, 2 * GR, w), F32),
        ],
        compiler_params=pltpu.CompilerParams(vmem_limit_bytes=40 << 20),
        cost_estimate=cost(heads * 5.5e9, heads * 3e6),
        name="attend",
    )(window, me, near, far, own, q, g, *r)


def settle_kernel(me_ref, dq, owng, nearg, farg, o0, o1, o2, o3):
    me = me_ref[0]
    for d, out in ((0, o0), (1, o1), (3, o2), (2, o3)):
        owner = lax.rem(me + d, 4)
        rows = piece_rows(owner)
        far_rows = piece_rows(lax.rem(owner, 2))
        out[0] = dq[rows, :]
        for i in range(2):
            late = jnp.where(owner >= 2, farg[i, far_rows, :].astype(F32), 0.0)
            out[1 + i] = (owng[i, rows, :] + nearg[i, rows, :].astype(F32) + late).astype(BF)


def settle(me, dq, owng, nearg, farg, w):
    def three(a, rows):
        return pl.BlockSpec((a, rows, HD), lambda h, m: (0, 0, h))

    return pl.pallas_call(
        settle_kernel,
        grid_spec=pltpu.PrefetchScalarGridSpec(
            num_scalar_prefetch=1,
            grid=(w // HD,),
            in_specs=[
                pl.BlockSpec((2 * GR, HD), lambda h, m: (0, h)),
                three(2, 2 * GR),
                three(2, 2 * GR),
                three(2, GR),
            ],
            out_specs=[three(3, PR)] * 4,
        ),
        out_shape=[jax.ShapeDtypeStruct((3, PR, w), BF)] * 4,
        cost_estimate=cost(0, 10 * 2 * GR * w * 2),
        name="settle",
    )(me, dq, owng, nearg, farg)


def place_kernel(offsets, *refs):
    n = len(offsets)
    outs = refs[4 * n :]
    me = lax.axis_index("head")
    for c, (off, w) in enumerate(offsets):
        for d, r in zip((0, 1, 3, 2), refs[4 * c : 4 * c + 4]):
            cols = head_columns(lax.rem(me + 4 - d, 4), off, w)
            for i in range(3):
                outs[i][:, cols] = r[i]


def place(offsets, pieces):
    out = jax.ShapeDtypeStruct((PR, 4 * HEADS_DEV * HD), BF)
    n = len(pieces)
    return pl.pallas_call(
        functools.partial(place_kernel, offsets),
        in_specs=[VM] * n,
        out_specs=[VM] * 3,
        out_shape=[out] * 3,
        compiler_params=pltpu.CompilerParams(vmem_limit_bytes=40 << 20),
        cost_estimate=cost(0, 6 * PR * 2560 * 2),
        name="place",
    )(*pieces)


def shift_all(pieces):
    a, b, c = pieces
    return head_shift(a, 1), head_shift(b, -1), head_shift(c, 2)


def local(queries, keys, values, upstream, window):
    me = lax.axis_index("head").astype(jnp.int32).reshape(1)
    offsets = []
    off = 0
    for heads in CHUNKS:
        offsets.append((off, heads * HD))
        off += heads * HD
    offsets = tuple(offsets)
    packed = pack(keys, values, queries, upstream, offsets)
    came = [shift_all(packed[3 * c : 3 * c + 3]) for c in range(len(offsets))]
    pieces = []
    for (off, w), r in zip(offsets, came):
        own, last = join(keys, values, r, off, w)
        near = tm_shift(own, 1)
        far = tm_shift(last, 2)
        dq, nearg, farg, owng = attend(
            window, me, near, far, own, queries, upstream, r, off, w
        )
        back_near = tm_shift(nearg, -1)
        back_far = tm_shift(farg, -2)
        o0, *parts = settle(me, dq, owng, back_near, back_far, w)
        pieces += [o0, *shift_all(parts)]
    return place(offsets, pieces)


def solution(mesh):
    rows = P(("tm", "head"), None)
    return jax.shard_map(
        local,
        mesh=mesh,
        in_specs=(rows, rows, rows, rows, P("tm", None)),
        out_specs=(rows, rows, rows),
        check_vma=False,
    )
```

time: 310 us -> 178 us (0.57)
  matrix products: 79.4 us -> 0 us
  Pallas kernels: 0 us -> 42.3 us
  local copies, waits for them, and re-layouts: 57.8 us -> 15.9 us
  other arithmetic: 39.4 us -> 0 us
  waiting for transfers between devices: 68.1 us -> 45.7 us
  starting transfers between devices: 59 us -> 70.7 us
  loops' own time: 3.67 us -> 0 us
    dot_general x30 -> x0, matrix products: 79.4 us -> none  [the longest x5 21.3 us: head_pass(): part_v = jnp.dot(probs_b.T, g_head, preferred_element_type=jnp.float32)]
    pallas_call x0 -> x11, Pallas kernels: none -> 42.3 us  [the longest x3 29 us: attend(): pl.pallas_call(attend_kernel, grid_spec=pltpu.PrefetchScalarGridSpec(num_...]
    ppermute x8 -> x30, starting transfers between devices: 29.6 us -> 70.7 us  [the longest x12 45.2 us: tm_shift(): return lax.ppermute(block, 'tm', route)]
    all_to_all x7 -> x0, waiting for transfers between devices: 39.8 us -> none  [the longest x1 13.4 us: local(): lax.all_to_all(keys, 'head', split_axis=1, concat_axis=0, tiled=True)]
    all_to_all x7 -> x0, starting transfers between devices: 29.4 us -> none  [the longest x1 4.76 us: local(): lax.all_to_all(upstream, 'head', split_axis=1, concat_axis=0, tiled=True)]
    div x5 -> x0, other arithmetic: 17.5 us -> none  [head_pass(): probs = weights / row_total]
    ppermute x8 -> x30, waiting for transfers between devices: 28.3 us -> 45.7 us  [the longest x18 39.1 us: head_shift(): lax.ppermute(block, 'head', [(i, (i + distance) % n) for i in range(n)])]
    unnamed x8 -> x64, local copies, waits for them, and re-layouts: 0.02 us -> 15.9 us
  transfers between devices with their start and end apart: 15 -> 30, of which waited for: 7 -> 10; matrix products, arithmetic and copies ran while one was open for 11% -> 0% of each run, Pallas kernels for 0% -> 22%
where the time goes in v1:
time: 178 us; the launch traced here: 176 us
  starting transfers between devices  70.7 us (40%)
  waiting for transfers between devices  45.7 us (26%)
  Pallas kernels  42.3 us (24%)
  local copies, waits for them, and re-layouts  15.9 us (9%)
    ppermute x12, starting transfers between devices, tm_shift(): return lax.ppermute(block, 'tm', route)  45.2 us
    ppermute x18, waiting for transfers between devices, head_shift(): lax.ppermute(block, 'head', [(i, (i + distance) % n) for i in range(n)])  39.1 us
    pallas_call x3, Pallas kernels, attend(): pl.pallas_call(attend_kernel, grid_spec=pltpu.PrefetchScalarGridSpec(num_...  29 us
    ppermute x18, starting transfers between devices, head_shift(): lax.ppermute(block, 'head', [(i, (i + distance) % n) for i in range(n)])  25.5 us
    unnamed x64, local copies, waits for them, and re-layouts  15.9 us
    pallas_call x3, Pallas kernels, settle(): pl.pallas_call(settle_kernel, grid_spec=pltpu.PrefetchScalarGridSpec(num_...  7.8 us
    ppermute x12, waiting for transfers between devices, tm_shift(): return lax.ppermute(block, 'tm', route)  6.62 us
  transfers between devices with their start and end apart: 30, of which 10 were waited for; matrix products, arithmetic and copies ran while one was open for 0% of the time, Pallas kernels for 22%

profile of v1, /device:TPU:6, one launch (start us, length us, event | category | flops | bytes accessed | tf_op | source)
XLA Modules:
  0.0 175.6 jit_solution(11375692704409473420)
XLA Ops:
  11.8 6.9 %collective-permute-done.10.r1 = bf16[4,192,256]{2,1,0:T(8,128)(2,1)S(1)} collective-permute-done((bf16[4,192,256]{2,1,0:T(8,128)(2,1)S(1)}, bf16[4,192,256]{2,1,0:T(8,128)(2,1)S(1)}, u32[]{:S(2)}, u32[]{:S(2)}) %collective-permute-start.10) | collective-permute-done | bytes 393248 | tf_op jit(solution)/shard_map/ppermute | solution.py:35
  20.2 8.1 %collective-permute-done.12.r3 = bf16[4,192,256]{2,1,0:T(8,128)(2,1)S(1)} collective-permute-done((bf16[4,192,256]{2,1,0:T(8,128)(2,1)S(1)}, bf16[4,192,256]{2,1,0:T(8,128)(2,1)S(1)}, u32[]{:S(2)}, u32[]{:S(2)}) %collective-permute-start.12) | collective-permute-done | bytes 393248 | tf_op jit(solution)/shard_map/ppermute | solution.py:35
  36.0 3.3 %collective-permute-done.20.r1 = bf16[4,192,128]{2,1,0:T(8,128)(2,1)S(1)} collective-permute-done((bf16[4,192,128]{2,1,0:T(8,128)(2,1)S(1)}, bf16[4,192,128]{2,1,0:T(8,128)(2,1)S(1)}, u32[]{:S(2)}, u32[]{:S(2)}) %collective-permute-start.20) | collective-permute-done | bytes 196640 | tf_op jit(solution)/shard_map/ppermute | solution.py:35
  44.7 3.8 %collective-permute-start.14 = (bf16[2,384,256]{2,1,0:T(8,128)(2,1)}, bf16[2,384,256]{2,1,0:T(8,128)(2,1)}, u32[]{:S(2)}, u32[]{:S(2)}) collective-permute-start(bf16[2,384,256]{2,1,0:T(8,128)(2,1)} %get-tuple-element.59), channel_id=1, source_target_pairs={{0,8},{4,12},{8,16},{12,20},{16,24},{20,28},{24,32},{28,36},{32,40... | collective-permute-start | bytes 1179656 | tf_op jit(solution)/shard_map/ppermute | solution.py:41
  52.4 3.8 %collective-permute-start.24 = (bf16[2,384,128]{2,1,0:T(8,128)(2,1)S(1)}, bf16[2,384,128]{2,1,0:T(8,128)(2,1)S(1)}, u32[]{:S(2)}, u32[]{:S(2)}) collective-permute-start(bf16[2,384,128]{2,1,0:T(8,128)(2,1)S(1)} %get-tuple-element.72), channel_id=1, source_target_pairs={{0,8},{4,12},{8,16},{12,20},{16,24},{20,28},{24,32},{28,36},{32,40... | collective-permute-start | bytes 589832 | tf_op jit(solution)/shard_map/ppermute | solution.py:41
  56.2 7.0 %collective-permute-start.23 = (bf16[2,768,128]{2,1,0:T(8,128)(2,1)S(1)}, bf16[2,768,128]{2,1,0:T(8,128)(2,1)S(1)}, u32[]{:S(2)}, u32[]{:S(2)}) collective-permute-start(bf16[2,768,128]{2,1,0:T(8,128)(2,1)S(1)} %get-tuple-element.71.own), channel_id=1, source_target_pairs={{0,4},{4,8},{8,12},{12,16},{16,20},{20,24},{24,28},{28,32},{32,36}... | collective-permute-start | bytes 1179656 | tf_op jit(solution)/shard_map/ppermute | solution.py:41
  64.5 3.8 %collective-permute-start.4 = (bf16[2,384,256]{2,1,0:T(8,128)(2,1)S(1)}, bf16[2,384,256]{2,1,0:T(8,128)(2,1)S(1)}, u32[]{:S(2)}, u32[]{:S(2)}) collective-permute-start(bf16[2,384,256]{2,1,0:T(8,128)(2,1)S(1)} %get-tuple-element.46), channel_id=1, source_target_pairs={{0,8},{4,12},{8,16},{12,20},{16,24},{20,28},{24,32},{28,36},{32,40... | collective-permute-start | bytes 1179656 | tf_op jit(solution)/shard_map/ppermute | solution.py:41
  70.5 11.8 %attend.4 = (bf16[768,256]{1,0:T(8,128)(2,1)S(1)}, bf16[2,768,256]{2,1,0:T(8,128)(2,1)S(1)}, bf16[2,384,256]{2,1,0:T(8,128)(2,1)S(1)}, f32[2,768,256]{2,1,0:T(8,128)S(1)}) custom-call(s32[2,3]{1,0:T(2,128)S(1)} %copy-done.26, s32[1]{0:T(128)} %bitcast.me_ref, bf16[2,768,256]{2,1,0:T(8,128)(2,1)} %collective-permute-done.13.near, ...), custom_call_target="tpu_custom_call" | custom-call | flops 11000000512 | bytes 6000000 | tf_op jit(solution)/shard_map/attend/pallas_call | solution.py:180
  84.2 4.1 %collective-permute-start.16 = (bf16[2,384,256]{2,1,0:T(8,128)(2,1)S(1)}, bf16[2,384,256]{2,1,0:T(8,128)(2,1)S(1)}, u32[]{:S(2)}, u32[]{:S(2)}) collective-permute-start(bf16[2,384,256]{2,1,0:T(8,128)(2,1)S(1)} %get-tuple-element.63), channel_id=1, source_target_pairs={{8,0},{12,4},{16,8},{20,12},{24,16},{28,20},{32,24},{36,28},{40,32... | collective-permute-start | bytes 1179656 | tf_op jit(solution)/shard_map/ppermute | solution.py:41
  88.4 4.3 %collective-permute-start.15 = (bf16[2,768,256]{2,1,0:T(8,128)(2,1)S(1)}, bf16[2,768,256]{2,1,0:T(8,128)(2,1)S(1)}, u32[]{:S(2)}, u32[]{:S(2)}) collective-permute-start(bf16[2,768,256]{2,1,0:T(8,128)(2,1)S(1)} %get-tuple-element.62), channel_id=1, source_target_pairs={{4,0},{8,4},{12,8},{16,12},{20,16},{24,20},{28,24},{32,28},{36,32}... | collective-permute-start | bytes 2359304 | tf_op jit(solution)/shard_map/ppermute | solution.py:41
  92.7 11.8 %attend.3 = (bf16[768,256]{1,0:T(8,128)(2,1)S(1)}, bf16[2,768,256]{2,1,0:T(8,128)(2,1)S(1)}, bf16[2,384,256]{2,1,0:T(8,128)(2,1)S(1)}, f32[2,768,256]{2,1,0:T(8,128)S(1)}) custom-call(s32[2,3]{1,0:T(2,128)S(1)} %copy-done.26, s32[1]{0:T(128)} %bitcast.me_ref, bf16[2,768,256]{2,1,0:T(8,128)(2,1)S(1)} %collective-permute-done.3.near, ...), custom_call_target="tpu_custom_call" | custom-call | flops 11000000512 | bytes 6000000 | tf_op jit(solution)/shard_map/attend/pallas_call | solution.py:180
  104.5 2.9 %collective-permute-start.5 = (bf16[2,768,256]{2,1,0:T(8,128)(2,1)S(1)}, bf16[2,768,256]{2,1,0:T(8,128)(2,1)S(1)}, u32[]{:S(2)}, u32[]{:S(2)}) collective-permute-start(bf16[2,768,256]{2,1,0:T(8,128)(2,1)S(1)} %get-tuple-element.49), channel_id=1, source_target_pairs={{4,0},{8,4},{12,8},{16,12},{20,16},{24,20},{28,24},{32,28},{36,32}... | collective-permute-start | bytes 2359304 | tf_op jit(solution)/shard_map/ppermute | solution.py:41
  107.4 5.4 %attend.5 = (bf16[768,128]{1,0:T(8,128)(2,1)S(1)}, bf16[2,768,128]{2,1,0:T(8,128)(2,1)S(1)}, bf16[2,384,128]{2,1,0:T(8,128)(2,1)S(1)}, f32[2,768,128]{2,1,0:T(8,128)S(1)}) custom-call(s32[2,3]{1,0:T(2,128)S(1)} %copy-done.26, s32[1]{0:T(128)} %bitcast.me_ref, bf16[2,768,128]{2,1,0:T(8,128)(2,1)S(1)} %collective-permute-done.23.near, ...), custom_call_target="tpu_custom_call" | custom-call | flops 5500000256 | bytes 3000000 | tf_op jit(solution)/shard_map/attend/pallas_call | solution.py:180
  114.4 3.3 %collective-permute-start.25 = (bf16[2,768,128]{2,1,0:T(8,128)(2,1)S(1)}, bf16[2,768,128]{2,1,0:T(8,128)(2,1)S(1)}, u32[]{:S(2)}, u32[]{:S(2)}) collective-permute-start(bf16[2,768,128]{2,1,0:T(8,128)(2,1)S(1)} %get-tuple-element.75), channel_id=1, source_target_pairs={{4,0},{8,4},{12,8},{16,12},{20,16},{24,20},{28,24},{32,28},{36,32}... | collective-permute-start | bytes 1179656 | tf_op jit(solution)/shard_map/ppermute | solution.py:41
  117.8 3.9 %collective-permute-start.6 = (bf16[2,384,256]{2,1,0:T(8,128)(2,1)S(1)}, bf16[2,384,256]{2,1,0:T(8,128)(2,1)}, u32[]{:S(2)}, u32[]{:S(2)}) collective-permute-start(bf16[2,384,256]{2,1,0:T(8,128)(2,1)S(1)} %get-tuple-element.50), channel_id=1, source_target_pairs={{8,0},{12,4},{16,8},{20,12},{24,16},{28,20},{32,24},{36,28},{40,32... | collective-permute-start | bytes 1179656 | tf_op jit(solution)/shard_map/ppermute | solution.py:41
  121.7 4.1 %collective-permute-start.26 = (bf16[2,384,128]{2,1,0:T(8,128)(2,1)S(1)}, bf16[2,384,128]{2,1,0:T(8,128)(2,1)}, u32[]{:S(2)}, u32[]{:S(2)}) collective-permute-start(bf16[2,384,128]{2,1,0:T(8,128)(2,1)S(1)} %get-tuple-element.76), channel_id=1, source_target_pairs={{8,0},{12,4},{16,8},{20,12},{24,16},{28,20},{32,24},{36,28},{40,32... | collective-permute-start | bytes 589832 | tf_op jit(solution)/shard_map/ppermute | solution.py:41
  126.8 2.8 %settle.4 = (bf16[3,192,256]{2,1,0:T(8,128)(2,1)}, bf16[3,192,256]{2,1,0:T(8,128)(2,1)}, bf16[3,192,256]{2,1,0:T(8,128)(2,1)}, bf16[3,192,256]{2,1,0:T(8,128)(2,1)}) custom-call(s32[1]{0:T(128)} %bitcast.me_ref, bf16[768,256]{1,0:T(8,128)(2,1)} %copy-done.12, f32[2,768,256]{2,1,0:T(8,128)} %copy-done.5, bf16[2,768,256]{2,1,0:T(8,128)(2,1)} %copy-done.28, ...), custom_call_target="tpu_custom_call" | custom-call | bytes 3932160 | tf_op jit(solution)/shard_map/settle/pallas_call | solution.py:223
  129.6 6.6 %collective-permute-done.26.farg = bf16[2,384,128]{2,1,0:T(8,128)(2,1)} collective-permute-done((bf16[2,384,128]{2,1,0:T(8,128)(2,1)S(1)}, bf16[2,384,128]{2,1,0:T(8,128)(2,1)}, u32[]{:S(2)}, u32[]{:S(2)}) %collective-permute-start.26) | collective-permute-done | bytes 196640 | tf_op jit(solution)/shard_map/ppermute | solution.py:41
  139.2 3.4 %collective-permute-start.28 = (bf16[3,192,128]{2,1,0:T(8,128)(2,1)}, bf16[3,192,128]{2,1,0:T(8,128)(2,1)S(1)}, u32[]{:S(2)}, u32[]{:S(2)}) collective-permute-start(bf16[3,192,128]{2,1,0:T(8,128)(2,1)} %get-tuple-element.79), channel_id=1, source_target_pairs={{0,3},{1,0},{2,1},{3,2},{4,7},{5,4},{6,5},{7,6},{8,11},{9,8},{10,9... | collective-permute-start | bytes 442376 | tf_op jit(solution)/shard_map/ppermute | solution.py:35
  144.9 2.8 %settle.3 = (bf16[3,192,256]{2,1,0:T(8,128)(2,1)}, bf16[3,192,256]{2,1,0:T(8,128)(2,1)}, bf16[3,192,256]{2,1,0:T(8,128)(2,1)}, bf16[3,192,256]{2,1,0:T(8,128)(2,1)}) custom-call(s32[1]{0:T(128)} %bitcast.me_ref, bf16[768,256]{1,0:T(8,128)(2,1)} %copy-done.11, f32[2,768,256]{2,1,0:T(8,128)} %copy-done.4, bf16[2,768,256]{2,1,0:T(8,128)(2,1)} %copy-done.27, ...), custom_call_target="tpu_custom_call" | custom-call | bytes 3932160 | tf_op jit(solution)/shard_map/settle/pallas_call | solution.py:223
  150.4 3.2 %collective-permute-start.8 = (bf16[3,192,256]{2,1,0:T(8,128)(2,1)}, bf16[3,192,256]{2,1,0:T(8,128)(2,1)S(1)}, u32[]{:S(2)}, u32[]{:S(2)}) collective-permute-start(bf16[3,192,256]{2,1,0:T(8,128)(2,1)} %get-tuple-element.53), channel_id=1, source_target_pairs={{0,3},{1,0},{2,1},{3,2},{4,7},{5,4},{6,5},{7,6},{8,11},{9,8},{10,9... | collective-permute-start | bytes 884744 | tf_op jit(solution)/shard_map/ppermute | solution.py:35
  155.7 6.4 %collective-permute-done.18.refs_6_ = bf16[3,192,256]{2,1,0:T(8,128)(2,1)S(1)} collective-permute-done((bf16[3,192,256]{2,1,0:T(8,128)(2,1)}, bf16[3,192,256]{2,1,0:T(8,128)(2,1)S(1)}, u32[]{:S(2)}, u32[]{:S(2)}) %collective-permute-start.18) | collective-permute-done | bytes 294944 | tf_op jit(solution)/shard_map/ppermute | solution.py:35
  162.1 3.1 %collective-permute-done.7.refs_1_ = bf16[3,192,256]{2,1,0:T(8,128)(2,1)S(1)} collective-permute-done((bf16[3,192,256]{2,1,0:T(8,128)(2,1)}, bf16[3,192,256]{2,1,0:T(8,128)(2,1)S(1)}, u32[]{:S(2)}, u32[]{:S(2)}) %collective-permute-start.7) | collective-permute-done | bytes 294944 | tf_op jit(solution)/shard_map/ppermute | solution.py:35
  165.2 7.4 %collective-permute-done.8.refs_2_ = bf16[3,192,256]{2,1,0:T(8,128)(2,1)S(1)} collective-permute-done((bf16[3,192,256]{2,1,0:T(8,128)(2,1)}, bf16[3,192,256]{2,1,0:T(8,128)(2,1)S(1)}, u32[]{:S(2)}, u32[]{:S(2)}) %collective-permute-start.8) | collective-permute-done | bytes 294944 | tf_op jit(solution)/shard_map/ppermute | solution.py:35
  (111 shorter events, 50.3 us)
Async XLA Ops:
  6.6 12.1 %collective-permute-start.10 = (bf16[4,192,256]{2,1,0:T(8,128)(2,1)S(1)}, bf16[4,192,256]{2,1,0:T(8,128)(2,1)S(1)}, u32[]{:S(2)}, u32[]{:S(2)}) collective-permute-start(bf16[4,192,256]{2,1,0:T(8,128)(2,1)S(1)} %get-tuple-element.55), channel_id=1, source_target_pairs={{0,1},{1,2},{2,3},{3,0},{4,5},{5,6},{6,7},{7,4},{8,9},{9,10},{10,1... | collective-permute-start | bytes 1179656 | tf_op jit(solution)/shard_map/ppermute | solution.py:35
  8.1 12.0 %collective-permute-start.11 = (bf16[4,192,256]{2,1,0:T(8,128)(2,1)S(1)}, bf16[4,192,256]{2,1,0:T(8,128)(2,1)S(1)}, u32[]{:S(2)}, u32[]{:S(2)}) collective-permute-start(bf16[4,192,256]{2,1,0:T(8,128)(2,1)S(1)} %get-tuple-element.56), channel_id=1, source_target_pairs={{0,3},{1,0},{2,1},{3,2},{4,7},{5,4},{6,5},{7,6},{8,11},{9,8},{10,9... | collective-permute-start | bytes 1179656 | tf_op jit(solution)/shard_map/ppermute | solution.py:35
  9.8 18.5 %collective-permute-start.12 = (bf16[4,192,256]{2,1,0:T(8,128)(2,1)S(1)}, bf16[4,192,256]{2,1,0:T(8,128)(2,1)S(1)}, u32[]{:S(2)}, u32[]{:S(2)}) collective-permute-start(bf16[4,192,256]{2,1,0:T(8,128)(2,1)S(1)} %get-tuple-element.57), channel_id=1, source_target_pairs={{0,2},{1,3},{2,0},{3,1},{4,6},{5,7},{6,4},{7,5},{8,10},{9,11},{10,... | collective-permute-start | bytes 1179656 | tf_op jit(solution)/shard_map/ppermute | solution.py:35
  29.4 41.1 %collective-permute-start.13 = (bf16[2,768,256]{2,1,0:T(8,128)(2,1)}, bf16[2,768,256]{2,1,0:T(8,128)(2,1)}, u32[]{:S(2)}, u32[]{:S(2)}) collective-permute-start(bf16[2,768,256]{2,1,0:T(8,128)(2,1)} %get-tuple-element.58.own), channel_id=1, source_target_pairs={{0,4},{4,8},{8,12},{12,16},{16,20},{20,24},{24,28},{28,32},{32,36}... | collective-permute-start | bytes 2359304 | tf_op jit(solution)/shard_map/ppermute | solution.py:41
  34.7 17.7 %collective-permute-start = (bf16[4,192,256]{2,1,0:T(8,128)(2,1)}, bf16[4,192,256]{2,1,0:T(8,128)(2,1)S(1)}, u32[]{:S(2)}, u32[]{:S(2)}) collective-permute-start(bf16[4,192,256]{2,1,0:T(8,128)(2,1)} %get-tuple-element.42), channel_id=1, source_target_pairs={{0,1},{1,2},{2,3},{3,0},{4,5},{5,6},{6,7},{7,4},{8,9},{9,10},{10,1... | collective-permute-start | bytes 1179656 | tf_op jit(solution)/shard_map/ppermute | solution.py:35
  40.0 16.2 %collective-permute-start.1 = (bf16[4,192,256]{2,1,0:T(8,128)(2,1)}, bf16[4,192,256]{2,1,0:T(8,128)(2,1)}, u32[]{:S(2)}, u32[]{:S(2)}) collective-permute-start(bf16[4,192,256]{2,1,0:T(8,128)(2,1)} %get-tuple-element.43), channel_id=1, source_target_pairs={{0,3},{1,0},{2,1},{3,2},{4,7},{5,4},{6,5},{7,6},{8,11},{9,8},{10,9... | collective-permute-start | bytes 1179656 | tf_op jit(solution)/shard_map/ppermute | solution.py:35
  41.2 22.0 %collective-permute-start.2 = (bf16[4,192,256]{2,1,0:T(8,128)(2,1)}, bf16[4,192,256]{2,1,0:T(8,128)(2,1)}, u32[]{:S(2)}, u32[]{:S(2)}) collective-permute-start(bf16[4,192,256]{2,1,0:T(8,128)(2,1)} %get-tuple-element.44), channel_id=1, source_target_pairs={{0,2},{1,3},{2,0},{3,1},{4,6},{5,7},{6,4},{7,5},{8,10},{9,11},{10,... | collective-permute-start | bytes 1179656 | tf_op jit(solution)/shard_map/ppermute | solution.py:35
  44.7 23.6 %collective-permute-start.14 = (bf16[2,384,256]{2,1,0:T(8,128)(2,1)}, bf16[2,384,256]{2,1,0:T(8,128)(2,1)}, u32[]{:S(2)}, u32[]{:S(2)}) collective-permute-start(bf16[2,384,256]{2,1,0:T(8,128)(2,1)} %get-tuple-element.59), channel_id=1, source_target_pairs={{0,8},{4,12},{8,16},{12,20},{16,24},{20,28},{24,32},{28,36},{32,40... | collective-permute-start | bytes 1179656 | tf_op jit(solution)/shard_map/ppermute | solution.py:41
  52.4 55.0 %collective-permute-start.24 = (bf16[2,384,128]{2,1,0:T(8,128)(2,1)S(1)}, bf16[2,384,128]{2,1,0:T(8,128)(2,1)S(1)}, u32[]{:S(2)}, u32[]{:S(2)}) collective-permute-start(bf16[2,384,128]{2,1,0:T(8,128)(2,1)S(1)} %get-tuple-element.72), channel_id=1, source_target_pairs={{0,8},{4,12},{8,16},{12,20},{16,24},{20,28},{24,32},{28,36},{32,40... | collective-permute-start | bytes 589832 | tf_op jit(solution)/shard_map/ppermute | solution.py:41
  56.2 51.2 %collective-permute-start.23 = (bf16[2,768,128]{2,1,0:T(8,128)(2,1)S(1)}, bf16[2,768,128]{2,1,0:T(8,128)(2,1)S(1)}, u32[]{:S(2)}, u32[]{:S(2)}) collective-permute-start(bf16[2,768,128]{2,1,0:T(8,128)(2,1)S(1)} %get-tuple-element.71.own), channel_id=1, source_target_pairs={{0,4},{4,8},{8,12},{12,16},{16,20},{20,24},{24,28},{28,32},{32,36}... | collective-permute-start | bytes 1179656 | tf_op jit(solution)/shard_map/ppermute | solution.py:41
  64.5 23.9 %collective-permute-start.4 = (bf16[2,384,256]{2,1,0:T(8,128)(2,1)S(1)}, bf16[2,384,256]{2,1,0:T(8,128)(2,1)S(1)}, u32[]{:S(2)}, u32[]{:S(2)}) collective-permute-start(bf16[2,384,256]{2,1,0:T(8,128)(2,1)S(1)} %get-tuple-element.46), channel_id=1, source_target_pairs={{0,8},{4,12},{8,16},{12,20},{16,24},{20,28},{24,32},{28,36},{32,40... | collective-permute-start | bytes 1179656 | tf_op jit(solution)/shard_map/ppermute | solution.py:41
  68.3 24.3 %collective-permute-start.3 = (bf16[2,768,256]{2,1,0:T(8,128)(2,1)S(1)}, bf16[2,768,256]{2,1,0:T(8,128)(2,1)S(1)}, u32[]{:S(2)}, u32[]{:S(2)}) collective-permute-start(bf16[2,768,256]{2,1,0:T(8,128)(2,1)S(1)} %get-tuple-element.45.own), channel_id=1, source_target_pairs={{0,4},{4,8},{8,12},{12,16},{16,20},{20,24},{24,28},{28,32},{32,36}... | collective-permute-start | bytes 2359304 | tf_op jit(solution)/shard_map/ppermute | solution.py:41
  84.2 37.5 %collective-permute-start.16 = (bf16[2,384,256]{2,1,0:T(8,128)(2,1)S(1)}, bf16[2,384,256]{2,1,0:T(8,128)(2,1)S(1)}, u32[]{:S(2)}, u32[]{:S(2)}) collective-permute-start(bf16[2,384,256]{2,1,0:T(8,128)(2,1)S(1)} %get-tuple-element.63), channel_id=1, source_target_pairs={{8,0},{12,4},{16,8},{20,12},{24,16},{28,20},{32,24},{36,28},{40,32... | collective-permute-start | bytes 1179656 | tf_op jit(solution)/shard_map/ppermute | solution.py:41
  88.4 37.5 %collective-permute-start.15 = (bf16[2,768,256]{2,1,0:T(8,128)(2,1)S(1)}, bf16[2,768,256]{2,1,0:T(8,128)(2,1)S(1)}, u32[]{:S(2)}, u32[]{:S(2)}) collective-permute-start(bf16[2,768,256]{2,1,0:T(8,128)(2,1)S(1)} %get-tuple-element.62), channel_id=1, source_target_pairs={{4,0},{8,4},{12,8},{16,12},{20,16},{24,20},{28,24},{32,28},{36,32}... | collective-permute-start | bytes 2359304 | tf_op jit(solution)/shard_map/ppermute | solution.py:41
  104.5 39.5 %collective-permute-start.5 = (bf16[2,768,256]{2,1,0:T(8,128)(2,1)S(1)}, bf16[2,768,256]{2,1,0:T(8,128)(2,1)S(1)}, u32[]{:S(2)}, u32[]{:S(2)}) collective-permute-start(bf16[2,768,256]{2,1,0:T(8,128)(2,1)S(1)} %get-tuple-element.49), channel_id=1, source_target_pairs={{4,0},{8,4},{12,8},{16,12},{20,16},{24,20},{28,24},{32,28},{36,32}... | collective-permute-start | bytes 2359304 | tf_op jit(solution)/shard_map/ppermute | solution.py:41
  114.4 21.7 %collective-permute-start.25 = (bf16[2,768,128]{2,1,0:T(8,128)(2,1)S(1)}, bf16[2,768,128]{2,1,0:T(8,128)(2,1)S(1)}, u32[]{:S(2)}, u32[]{:S(2)}) collective-permute-start(bf16[2,768,128]{2,1,0:T(8,128)(2,1)S(1)} %get-tuple-element.75), channel_id=1, source_target_pairs={{4,0},{8,4},{12,8},{16,12},{20,16},{24,20},{28,24},{32,28},{36,32}... | collective-permute-start | bytes 1179656 | tf_op jit(solution)/shard_map/ppermute | solution.py:41
  117.8 24.7 %collective-permute-start.6 = (bf16[2,384,256]{2,1,0:T(8,128)(2,1)S(1)}, bf16[2,384,256]{2,1,0:T(8,128)(2,1)}, u32[]{:S(2)}, u32[]{:S(2)}) collective-permute-start(bf16[2,384,256]{2,1,0:T(8,128)(2,1)S(1)} %get-tuple-element.50), channel_id=1, source_target_pairs={{8,0},{12,4},{16,8},{20,12},{24,16},{28,20},{32,24},{36,28},{40,32... | collective-permute-start | bytes 1179656 | tf_op jit(solution)/shard_map/ppermute | solution.py:41
  121.7 14.4 %collective-permute-start.26 = (bf16[2,384,128]{2,1,0:T(8,128)(2,1)S(1)}, bf16[2,384,128]{2,1,0:T(8,128)(2,1)}, u32[]{:S(2)}, u32[]{:S(2)}) collective-permute-start(bf16[2,384,128]{2,1,0:T(8,128)(2,1)S(1)} %get-tuple-element.76), channel_id=1, source_target_pairs={{8,0},{12,4},{16,8},{20,12},{24,16},{28,20},{32,24},{36,28},{40,32... | collective-permute-start | bytes 589832 | tf_op jit(solution)/shard_map/ppermute | solution.py:41
  129.6 24.1 %collective-permute-start.17 = (bf16[3,192,256]{2,1,0:T(8,128)(2,1)}, bf16[3,192,256]{2,1,0:T(8,128)(2,1)S(1)}, u32[]{:S(2)}, u32[]{:S(2)}) collective-permute-start(bf16[3,192,256]{2,1,0:T(8,128)(2,1)} %get-tuple-element.65), channel_id=1, source_target_pairs={{0,1},{1,2},{2,3},{3,0},{4,5},{5,6},{6,7},{7,4},{8,9},{9,10},{10,1... | collective-permute-start | bytes 884744 | tf_op jit(solution)/shard_map/ppermute | solution.py:35
  144.0 18.1 %collective-permute-start.18 = (bf16[3,192,256]{2,1,0:T(8,128)(2,1)}, bf16[3,192,256]{2,1,0:T(8,128)(2,1)S(1)}, u32[]{:S(2)}, u32[]{:S(2)}) collective-permute-start(bf16[3,192,256]{2,1,0:T(8,128)(2,1)} %get-tuple-element.66), channel_id=1, source_target_pairs={{0,3},{1,0},{2,1},{3,2},{4,7},{5,4},{6,5},{7,6},{8,11},{9,8},{10,9... | collective-permute-start | bytes 884744 | tf_op jit(solution)/shard_map/ppermute | solution.py:35
  147.7 14.4 %collective-permute-start.19 = (bf16[3,192,256]{2,1,0:T(8,128)(2,1)S(1)}, bf16[3,192,256]{2,1,0:T(8,128)(2,1)S(1)}, u32[]{:S(2)}, u32[]{:S(2)}) collective-permute-start(bf16[3,192,256]{2,1,0:T(8,128)(2,1)S(1)} %copy-done.31), channel_id=1, source_target_pairs={{0,2},{1,3},{2,0},{3,1},{4,6},{5,7},{6,4},{7,5},{8,10},{9,11},{10,... | collective-permute-start | bytes 884744 | tf_op jit(solution)/shard_map/ppermute | solution.py:35
  150.4 14.8 %collective-permute-start.7 = (bf16[3,192,256]{2,1,0:T(8,128)(2,1)}, bf16[3,192,256]{2,1,0:T(8,128)(2,1)S(1)}, u32[]{:S(2)}, u32[]{:S(2)}) collective-permute-start(bf16[3,192,256]{2,1,0:T(8,128)(2,1)} %get-tuple-element.52), channel_id=1, source_target_pairs={{0,1},{1,2},{2,3},{3,0},{4,5},{5,6},{6,7},{7,4},{8,9},{9,10},{10,1... | collective-permute-start | bytes 884744 | tf_op jit(solution)/shard_map/ppermute | solution.py:35
  150.4 22.2 %collective-permute-start.8 = (bf16[3,192,256]{2,1,0:T(8,128)(2,1)}, bf16[3,192,256]{2,1,0:T(8,128)(2,1)S(1)}, u32[]{:S(2)}, u32[]{:S(2)}) collective-permute-start(bf16[3,192,256]{2,1,0:T(8,128)(2,1)} %get-tuple-element.53), channel_id=1, source_target_pairs={{0,3},{1,0},{2,1},{3,2},{4,7},{5,4},{6,5},{7,6},{8,11},{9,8},{10,9... | collective-permute-start | bytes 884744 | tf_op jit(solution)/shard_map/ppermute | solution.py:35
  153.7 19.0 %collective-permute-start.9 = (bf16[3,192,256]{2,1,0:T(8,128)(2,1)}, bf16[3,192,256]{2,1,0:T(8,128)(2,1)S(1)}, u32[]{:S(2)}, u32[]{:S(2)}) collective-permute-start(bf16[3,192,256]{2,1,0:T(8,128)(2,1)} %get-tuple-element.54), channel_id=1, source_target_pairs={{0,2},{1,3},{2,0},{3,1},{4,6},{5,7},{6,4},{7,5},{8,10},{9,11},{10,... | collective-permute-start | bytes 884744 | tf_op jit(solution)/shard_map/ppermute | solution.py:35
  (38 other events, 327.5 us)

commit v2 on v0

v2 whole, which is shorter than its diff:
```python
import functools
import math

import jax
import jax.numpy as jnp
from jax import lax
from jax.experimental import pallas as pl
from jax.experimental.pallas import tpu as pltpu
from jax.sharding import PartitionSpec as P

HD = 128
GR = 384
PR = 192
HEADS_DEV = 5
CHUNKS = (2, 3)
IN_STAGES = (
    (("kv", 0),),
    (("qg", 0), ("kv", 1)),
    (("qg", 1),),
)
OUT_STAGES = ((("dq", 0), ("dkv", 0), ("dq", 1)), (("dkv", 1),))
SCALE = 1.0 / math.sqrt(HD)
SCALE2 = SCALE * math.log2(math.e)
NT = (((1,), (1,)), ((), ()))
TN = (((0,), (0,)), ((), ()))
BF = jnp.bfloat16
F32 = jnp.float32
VM = pl.BlockSpec(memory_space=pltpu.VMEM)


def dot(a, b, dims=(((1,), (0,)), ((), ()))):
    return lax.dot_general(a, b, dims, preferred_element_type=F32)


def cost(flops, nbytes):
    return pl.CostEstimate(flops=int(flops * 1), bytes_accessed=int(nbytes * 1), transcendentals=0)


def head_shift(block, distance):
    n = lax.axis_size("head")
    return lax.ppermute(block, "head", [(i, (i + distance) % n) for i in range(n)])


def tm_shift(block, distance):
    devices = range(lax.axis_size("tm"))
    route = [(i - distance, i) for i in devices if i - distance in devices]
    return lax.ppermute(block, "tm", route)


def columns(owner, head):
    return pl.ds(pl.multiple_of((owner * HEADS_DEV + head) * HD, HD), HD)


def piece_rows(owner):
    return pl.ds(pl.multiple_of(owner * PR, 64), PR)


def heads_of(chunk):
    first = sum(CHUNKS[:chunk])
    return range(first, first + CHUNKS[chunk])


def in_units(stage):
    units = []
    for what, chunk in stage:
        for head in heads_of(chunk):
            units += [(what[0], head), (what[1], head)]
    return units


def out_units(stage):
    units = []
    for what, chunk in stage:
        for head in heads_of(chunk):
            units += [(o, head) for o in what[1:]]
    return units


def small():
    return pltpu.CompilerParams(vmem_limit_bytes=24 << 20)


def pack_kernel(units, names, *refs):
    me = lax.axis_index("head")
    srcs = dict(zip(names, refs))
    for d, out in zip((1, 3, 2), refs[len(names) :]):
        owner = lax.rem(me + d, 4)
        for u, (name, head) in enumerate(units):
            out[u] = srcs[name][:, columns(owner, head)]


def pack(args, stage):
    units = in_units(stage)
    names = sorted({name for name, _ in units})
    out = jax.ShapeDtypeStruct((len(units), PR, HD), BF)
    return pl.pallas_call(
        functools.partial(pack_kernel, units, names),
        in_specs=[VM] * len(names),
        out_specs=[VM] * 3,
        out_shape=[out] * 3,
        compiler_params=small(),
        cost_estimate=cost(0, 6 * len(units) * PR * HD * 2),
        name="pack",
    )(*[args[name] for name in names])


def join_kernel(heads, base, k, v, r1, r2, r3, own, last):
    me = lax.axis_index("head")
    for n, head in enumerate(heads):
        own[n, 0, piece_rows(me), :] = k[:, columns(me, head)]
        own[n, 1, piece_rows(me), :] = v[:, columns(me, head)]
        for d, r in ((1, r1), (3, r2), (2, r3)):
            rows = piece_rows(lax.rem(me + 4 - d, 4))
            own[n, 0, rows, :] = r[base + 2 * n]
            own[n, 1, rows, :] = r[base + 2 * n + 1]
    last[...] = own[:, :, GR:, :]


def join(k, v, r, heads, base):
    n = len(heads)
    return pl.pallas_call(
        functools.partial(join_kernel, heads, base),
        in_specs=[VM] * 5,
        out_specs=[VM] * 2,
        out_shape=[
            jax.ShapeDtypeStruct((n, 2, 2 * GR, HD), BF),
            jax.ShapeDtypeStruct((n, 2, GR, HD), BF),
        ],
        compiler_params=small(),
        cost_estimate=cost(0, 6 * 2 * GR * n * HD * 2),
        name="join",
    )(k, v, *r)


def attend_kernel(
    heads, base, win, near_, far_, own_, queries, upstream, r1, r2, r3,
    dq_, nearg_, farg_, owng_, q_ref, g_ref, s_ref, d_ref,
):
    me = lax.axis_index("head")

    def hidden(c, slot):
        return jnp.where(win[c, slot] >= 0, 0.0, 1e30).astype(F32)

    lane = lax.broadcasted_iota(jnp.int32, (1, 2 * GR), 1)

    def lanes(a, b):
        return jnp.where(lane < GR, a, b)

    one = jnp.full((1, GR), 1.0, F32)
    hides = (
        one * hidden(0, 2),
        lanes(hidden(0, 1), hidden(1, 2)),
        lanes(hidden(0, 0), hidden(1, 1)),
        lanes(0.0, hidden(1, 0)),
        one * 0.0,
    )

    def rows_of(i):
        return slice(i * GR, (i + 1) * GR)

    def combine(x, op):
        mid = op(op(x[1], x[2]), x[3])
        return jnp.concatenate([op(mid[:, :GR], x[0]), op(mid[:, GR:], x[4])], axis=1)

    def head(n, carry):
        near, far, own = near_.at[n], far_.at[n], own_.at[n]
        nearg, farg, owng = nearg_.at[n], farg_.at[n], owng_.at[n]
        q_ref[piece_rows(me), :] = queries[:, columns(me, heads[0] + n)]
        g_ref[piece_rows(me), :] = upstream[:, columns(me, heads[0] + n)]
        for d, r in ((1, r1), (3, r2), (2, r3)):
            rows = piece_rows(lax.rem(me + 4 - d, 4))
            q_ref[rows, :] = r[base + 2 * n]
            g_ref[rows, :] = r[base + 2 * n + 1]
        blocks = (
            (far, farg, 0, 0, 0, GR, hides[0]),
            (near, nearg, 0, 1, 0, 2 * GR, hides[1]),
            (near, nearg, 1, 2, 0, 2 * GR, hides[2]),
            (own, owng, 0, 3, 0, 2 * GR, hides[3]),
            (own, owng, 1, 4, GR, 2 * GR, hides[4]),
        )
        tops = []
        for ref, _, i, j, lo, hi, hide in blocks:
            s = dot(ref[0, rows_of(i), :], q_ref[lo:hi, :], NT)
            s_ref[rows_of(j), lo:hi] = s
            tops.append(jnp.max(s, axis=0, keepdims=True) * SCALE2 - hide)
        top = combine(tops, jnp.maximum)
        totals, deltas = [], []
        for ref, _, i, j, lo, hi, hide in blocks:
            dp = dot(ref[1, rows_of(i), :], g_ref[lo:hi, :], NT)
            e = jnp.exp2(s_ref[rows_of(j), lo:hi] * SCALE2 - (top[:, lo:hi] + hide))
            s_ref[rows_of(j), lo:hi] = e
            d_ref[rows_of(j), lo:hi] = dp
            totals.append(jnp.sum(e, axis=0, keepdims=True))
            deltas.append(jnp.sum(e * dp, axis=0, keepdims=True))
        inverse = 1.0 / combine(totals, jnp.add)
        delta = combine(deltas, jnp.add) * inverse
        column = jnp.transpose(jnp.broadcast_to(inverse, (HD, 2 * GR)))
        g = (g_ref[...].astype(F32) * column).astype(BF)
        q = (q_ref[...].astype(F32) * (column * SCALE)).astype(BF)
        dq = [None, None]
        for ref, out, i, j, lo, hi, hide in blocks:
            e = s_ref[rows_of(j), lo:hi]
            ds = (e * (d_ref[rows_of(j), lo:hi] - delta[:, lo:hi])).astype(BF)
            out[1, rows_of(i), :] = dot(e.astype(BF), g[lo:hi]).astype(out.dtype)
            out[0, rows_of(i), :] = dot(ds, q[lo:hi]).astype(out.dtype)
            part = dot(ref[0, rows_of(i), :], ds, TN)
            if lo == 0:
                dq[0] = part[:, :GR] if dq[0] is None else dq[0] + part[:, :GR]
            if hi == 2 * GR:
                dq[1] = part[:, -GR:] if dq[1] is None else dq[1] + part[:, -GR:]
        for i in range(2):
            factor = inverse[:, rows_of(i)] * SCALE
            dq_[n, rows_of(i), :] = (dq[i] * factor).T.astype(BF)
        return carry

    if len(heads) == 1:
        head(0, 0)
    else:
        lax.fori_loop(0, len(heads), head, 0)


def attend(window, near, far, own, queries, upstream, r, heads, base):
    n = len(heads)
    sd = jax.ShapeDtypeStruct
    return pl.pallas_call(
        functools.partial(attend_kernel, heads, base),
        in_specs=[pl.BlockSpec(memory_space=pltpu.SMEM)] + [VM] * 8,
        out_specs=[VM] * 4,
        out_shape=[
            sd((n, 2 * GR, HD), BF),
            sd((n, 2, 2 * GR, HD), BF),
            sd((n, 2, GR, HD), BF),
            sd((n, 2, 2 * GR, HD), F32),
        ],
        scratch_shapes=[
            pltpu.VMEM((2 * GR, HD), BF),
            pltpu.VMEM((2 * GR, HD), BF),
            pltpu.VMEM((5 * GR, 2 * GR), F32),
            pltpu.VMEM((5 * GR, 2 * GR), F32),
        ],
        compiler_params=pltpu.CompilerParams(vmem_limit_bytes=32 << 20),
        cost_estimate=cost(n * 5.5e9, n * 3e6),
        name="attend",
    )(window, near, far, own, queries, upstream, *r)


def settle_kernel(stage, *refs):
    me = lax.axis_index("head")
    outs = refs[-4:]
    refs = list(refs[:-4])
    u = 0
    for what, chunk in stage:
        if what == "dq":
            dq = refs.pop(0)
        else:
            owng, nearg, farg = refs.pop(0), refs.pop(0), refs.pop(0)
        for n in range(CHUNKS[chunk]):
            for d, out in zip((0, 1, 3, 2), outs):
                owner = lax.rem(me + d, 4)
                rows = piece_rows(owner)
                far_rows = piece_rows(lax.rem(owner, 2))
                if what == "dq":
                    out[u] = dq[n, rows, :]
                    continue
                for i in range(2):
                    late = jnp.where(owner >= 2, farg[n, i, far_rows, :].astype(F32), 0.0)
                    total = owng[n, i, rows, :] + nearg[n, i, rows, :].astype(F32) + late
                    out[u + i] = total.astype(BF)
            u += 1 if what == "dq" else 2


def settle(stage, operands):
    out = jax.ShapeDtypeStruct((len(out_units(stage)), PR, HD), BF)
    return pl.pallas_call(
        functools.partial(settle_kernel, stage),
        in_specs=[VM] * len(operands),
        out_specs=[VM] * 4,
        out_shape=[out] * 4,
        compiler_params=small(),
        cost_estimate=cost(0, 16 * len(out_units(stage)) * PR * HD * 2),
        name="settle",
    )(*operands)


def place_kernel(*refs):
    outs = dict(zip("qkv", refs[-3:]))
    me = lax.axis_index("head")
    for c, stage in enumerate(OUT_STAGES):
        for d, r in zip((0, 1, 3, 2), refs[4 * c : 4 * c + 4]):
            owner = lax.rem(me + 4 - d, 4)
            for u, (name, head) in enumerate(out_units(stage)):
                outs[name][:, columns(owner, head)] = r[u]


def place(pieces):
    out = jax.ShapeDtypeStruct((PR, 4 * HEADS_DEV * HD), BF)
    n = len(pieces)
    return pl.pallas_call(
        place_kernel,
        in_specs=[VM] * n,
        out_specs=[VM] * 3,
        out_shape=[out] * 3,
        compiler_params=small(),
        cost_estimate=cost(0, 6 * PR * 2560 * 2),
        name="place",
    )(*pieces)


def shift_all(pieces):
    a, b, c = pieces
    c = head_shift(c, 2)
    return head_shift(a, 1), head_shift(b, -1), c


def after(x, earlier):
    return lax.optimization_barrier((x, earlier))[0]


def local(queries, keys, values, upstream, window):
    args = {"q": queries, "k": keys, "v": values, "g": upstream}
    place_of = {}
    for i, stage in enumerate(IN_STAGES):
        base = 0
        for what, chunk in stage:
            place_of[what, chunk] = (i, base)
            base += 2 * CHUNKS[chunk]
    packed = [pack(args, stage) for stage in IN_STAGES]
    came = {}
    local_of = {}
    other = {}
    back = {}

    def send_in(i):
        came[i] = shift_all(packed[i])

    def join_chunk(c):
        i, base = place_of["kv", c]
        local_of[c] = join(keys, values, came[i], heads_of(c), base)

    def send_near(c):
        own, last = local_of[c]
        other[c] = tm_shift(own, 1), tm_shift(last, 2)

    def attend_chunk(c):
        i, base = place_of["qg", c]
        return attend(
            window, *other[c], local_of[c][0], queries, upstream, came[i], heads_of(c), base
        )

    def send_back(c):
        back[c] = tm_shift(grads[c][1], -1), tm_shift(grads[c][2], -2)

    grads = {}
    pieces = {}
    kept = {}

    def settle_stage(j):
        operands = []
        for what, c in OUT_STAGES[j]:
            operands += [grads[c][0]] if what == "dq" else [grads[c][3], *back[c]]
        own, *parts = settle(OUT_STAGES[j], operands)
        kept[j] = own
        return parts

    def send_out(j, parts):
        pieces[j] = [kept[j], *shift_all(parts)]

    send_in(0)
    send_in(1)
    join_chunk(0)
    send_near(0)
    join_chunk(1)
    local_of[1] = after(local_of[1], other[0])
    send_near(1)
    packed[2] = after(packed[2], local_of[1])
    send_in(2)
    grads[0] = attend_chunk(0)
    came[2] = after(came[2], grads[0][0])
    send_back(0)
    grads[1] = attend_chunk(1)
    grads[1] = after(grads[1], back[0])
    parts0 = settle_stage(0)
    send_out(0, parts0)
    send_back(1)
    parts1 = settle_stage(1)
    parts1 = [after(x, y) for x, y in zip(parts1, pieces[0][1:])]
    send_out(1, parts1)
    return place([x for j in range(2) for x in pieces[j]])


def solution(mesh):
    rows = P(("tm", "head"), None)
    return jax.shard_map(
        local,
        mesh=mesh,
        in_specs=(rows, rows, rows, rows, P("tm", None)),
        out_specs=(rows, rows, rows),
        check_vma=False,
    )
```

time: 310 us -> 140 us (0.45)
  matrix products: 79.4 us -> 0 us
  local copies, waits for them, and re-layouts: 57.8 us -> 2.41 us
  other arithmetic: 39.4 us -> 0 us
  Pallas kernels: 0 us -> 28.2 us
  waiting for transfers between devices: 68.1 us -> 53.1 us
  starting transfers between devices: 59 us -> 54.6 us
  loops' own time: 3.67 us -> 0 us
    dot_general x30 -> x0, matrix products: 79.4 us -> none  [the longest x5 21.3 us: head_pass(): part_v = jnp.dot(probs_b.T, g_head, preferred_element_type=jnp.float32)]
    all_to_all x7 -> x0, waiting for transfers between devices: 39.8 us -> none  [the longest x1 13.4 us: local(): lax.all_to_all(keys, 'head', split_axis=1, concat_axis=0, tiled=True)]
    all_to_all x7 -> x0, starting transfers between devices: 29.4 us -> none  [the longest x1 4.76 us: local(): lax.all_to_all(upstream, 'head', split_axis=1, concat_axis=0, tiled=True)]
    pallas_call x0 -> x10, Pallas kernels: none -> 28.2 us  [the longest x2 24.2 us: attend(): pl.pallas_call(functools.partial(attend_kernel, heads, base), in_specs=[p...]
    ppermute x8 -> x23, starting transfers between devices: 29.6 us -> 54.6 us  [the longest x8 32.7 us: tm_shift(): return lax.ppermute(block, 'tm', route)]
    ppermute x8 -> x23, waiting for transfers between devices: 28.3 us -> 53.1 us  [the longest x15 35.5 us: head_shift(): lax.ppermute(block, 'head', [(i, (i + distance) % n) for i in range(n)])]
    div x5 -> x0, other arithmetic: 17.5 us -> none  [head_pass(): probs = weights / row_total]
    all_to_all x7 -> x0, local copies, waits for them, and re-layouts: 10.9 us -> none  [the longest x1 2.31 us: local(): lax.all_to_all(keys, 'head', split_axis=1, concat_axis=0, tiled=True)]
  transfers between devices with their start and end apart: 15 -> 23, of which waited for: 7 -> 10; matrix products, arithmetic and copies ran while one was open for 11% -> 0% of each run, Pallas kernels for 0% -> 18%
where the time goes in v2:
time: 140 us; the launch traced here: 139 us
  starting transfers between devices  54.6 us (39%)
  waiting for transfers between devices  53.1 us (38%)
  Pallas kernels  28.2 us (20%)
  local copies, waits for them, and re-layouts  2.41 us (2%)
    ppermute x15, waiting for transfers between devices, head_shift(): lax.ppermute(block, 'head', [(i, (i + distance) % n) for i in range(n)])  35.5 us
    ppermute x8, starting transfers between devices, tm_shift(): return lax.ppermute(block, 'tm', route)  32.7 us
    pallas_call x2, Pallas kernels, attend(): pl.pallas_call(functools.partial(attend_kernel, heads, base), in_specs=[p...  24.2 us
    ppermute x15, starting transfers between devices, head_shift(): lax.ppermute(block, 'head', [(i, (i + distance) % n) for i in range(n)])  21.9 us
    ppermute x8, waiting for transfers between devices, tm_shift(): return lax.ppermute(block, 'tm', route)  17.6 us
  transfers between devices with their start and end apart: 23, of which 10 were waited for; matrix products, arithmetic and copies ran while one was open for 0% of the time, Pallas kernels for 18%

profile of v2, /device:TPU:6, one launch (start us, length us, event | category | flops | bytes accessed | tf_op | source)
XLA Modules:
  0.0 139.2 jit_solution(5302044613649869324)
XLA Ops:
  6.5 2.0 %collective-permute-start.2 = (bf16[4,192,128]{2,1,0:T(8,128)(2,1)S(1)}, bf16[4,192,128]{2,1,0:T(8,128)(2,1)S(1)}, u32[]{:S(2)}, u32[]{:S(2)}) collective-permute-start(bf16[4,192,128]{2,1,0:T(8,128)(2,1)S(1)} %get-tuple-element.49), channel_id=1, source_target_pairs={{0,2},{1,3},{2,0},{3,1},{4,6},{5,7},{6,4},{7,5},{8,10},{9,11},{10,... | collective-permute-start | bytes 589832 | tf_op jit(solution)/shard_map/ppermute | solution.py:41
  8.4 2.7 %collective-permute-done.r1 = bf16[4,192,128]{2,1,0:T(8,128)(2,1)S(1)} collective-permute-done((bf16[4,192,128]{2,1,0:T(8,128)(2,1)S(1)}, bf16[4,192,128]{2,1,0:T(8,128)(2,1)S(1)}, u32[]{:S(2)}, u32[]{:S(2)}) %collective-permute-start) | collective-permute-done | bytes 196640 | tf_op jit(solution)/shard_map/ppermute | solution.py:41
  11.1 3.6 %collective-permute-done.1.r2 = bf16[4,192,128]{2,1,0:T(8,128)(2,1)S(1)} collective-permute-done((bf16[4,192,128]{2,1,0:T(8,128)(2,1)S(1)}, bf16[4,192,128]{2,1,0:T(8,128)(2,1)S(1)}, u32[]{:S(2)}, u32[]{:S(2)}) %collective-permute-start.1) | collective-permute-done | bytes 196640 | tf_op jit(solution)/shard_map/ppermute | solution.py:41
  14.7 1.8 %collective-permute-done.2.r3 = bf16[4,192,128]{2,1,0:T(8,128)(2,1)S(1)} collective-permute-done((bf16[4,192,128]{2,1,0:T(8,128)(2,1)S(1)}, bf16[4,192,128]{2,1,0:T(8,128)(2,1)S(1)}, u32[]{:S(2)}, u32[]{:S(2)}) %collective-permute-start.2) | collective-permute-done | bytes 196640 | tf_op jit(solution)/shard_map/ppermute | solution.py:41
  16.6 1.9 %collective-permute-start.3 = (bf16[2,2,768,128]{3,2,1,0:T(8,128)(2,1)S(1)}, bf16[2,2,768,128]{3,2,1,0:T(8,128)(2,1)S(1)}, u32[]{:S(2)}, u32[]{:S(2)}) collective-permute-start(bf16[2,2,768,128]{3,2,1,0:T(8,128)(2,1)S(1)} %get-tuple-element.50.own_), channel_id=1, source_target_pairs={{0,4},{4,8},{8,12},{12,16},{16,20},{20,24},{24,28},{28,32},{32,36}... | collective-permute-start | bytes 2359304 | tf_op jit(solution)/shard_map/ppermute | solution.py:47
  20.1 2.1 %collective-permute-start.6 = (bf16[10,192,128]{2,1,0:T(8,128)(2,1)S(1)}, bf16[10,192,128]{2,1,0:T(8,128)(2,1)S(1)}, u32[]{:S(2)}, u32[]{:S(2)}) collective-permute-start(bf16[10,192,128]{2,1,0:T(8,128)(2,1)S(1)} %get-tuple-element.53), channel_id=1, source_target_pairs={{0,3},{1,0},{2,1},{3,2},{4,7},{5,4},{6,5},{7,6},{8,11},{9,8},{10,9... | collective-permute-start | bytes 1474568 | tf_op jit(solution)/shard_map/ppermute | solution.py:41
  22.3 3.8 %collective-permute-start.4 = (bf16[2,2,384,128]{3,2,1,0:T(8,128)(2,1)S(1)}, bf16[2,2,384,128]{3,2,1,0:T(8,128)(2,1)S(1)}, u32[]{:S(2)}, u32[]{:S(2)}) collective-permute-start(bf16[2,2,384,128]{3,2,1,0:T(8,128)(2,1)S(1)} %get-tuple-element.51), channel_id=1, source_target_pairs={{0,8},{4,12},{8,16},{12,20},{16,24},{20,28},{24,32},{28,36},{32,40... | collective-permute-start | bytes 1179656 | tf_op jit(solution)/shard_map/ppermute | solution.py:47
  26.1 7.1 %collective-permute-done.5.r1 = bf16[10,192,128]{2,1,0:T(8,128)(2,1)S(1)} collective-permute-done((bf16[10,192,128]{2,1,0:T(8,128)(2,1)S(1)}, bf16[10,192,128]{2,1,0:T(8,128)(2,1)S(1)}, u32[]{:S(2)}, u32[]{:S(2)}) %collective-permute-start.5) | collective-permute-done | bytes 491552 | tf_op jit(solution)/shard_map/ppermute | solution.py:41
  33.5 10.4 %collective-permute-done.7.r3 = bf16[10,192,128]{2,1,0:T(8,128)(2,1)S(1)} collective-permute-done((bf16[10,192,128]{2,1,0:T(8,128)(2,1)S(1)}, bf16[10,192,128]{2,1,0:T(8,128)(2,1)S(1)}, u32[]{:S(2)}, u32[]{:S(2)}) %collective-permute-start.7) | collective-permute-done | bytes 491552 | tf_op jit(solution)/shard_map/ppermute | solution.py:41
  44.0 2.8 %collective-permute-start.10 = (bf16[3,2,768,128]{3,2,1,0:T(8,128)(2,1)S(1)}, bf16[3,2,768,128]{3,2,1,0:T(8,128)(2,1)S(1)}, u32[]{:S(2)}, u32[]{:S(2)}) collective-permute-start(bf16[3,2,768,128]{3,2,1,0:T(8,128)(2,1)S(1)} %get-tuple-element.61.own_), channel_id=1, source_target_pairs={{0,4},{4,8},{8,12},{12,16},{16,20},{20,24},{24,28},{28,32},{32,36}... | collective-permute-start | bytes 3538952 | tf_op jit(solution)/shard_map/ppermute | solution.py:47
  47.0 3.8 %collective-permute-start.11 = (bf16[3,2,384,128]{3,2,1,0:T(8,128)(2,1)S(1)}, bf16[3,2,384,128]{3,2,1,0:T(8,128)(2,1)S(1)}, u32[]{:S(2)}, u32[]{:S(2)}) collective-permute-start(bf16[3,2,384,128]{3,2,1,0:T(8,128)(2,1)S(1)} %get-tuple-element.62), channel_id=1, source_target_pairs={{0,8},{4,12},{8,16},{12,20},{16,24},{20,28},{24,32},{28,36},{32,40... | collective-permute-start | bytes 1769480 | tf_op jit(solution)/shard_map/ppermute | solution.py:47
  52.3 1.8 %collective-permute-start.13 = (bf16[6,192,128]{2,1,0:T(8,128)(2,1)S(1)}, bf16[6,192,128]{2,1,0:T(8,128)(2,1)S(1)}, u32[]{:S(2)}, u32[]{:S(2)}) collective-permute-start(bf16[6,192,128]{2,1,0:T(8,128)(2,1)S(1)} %get-tuple-element.67), channel_id=1, source_target_pairs={{0,3},{1,0},{2,1},{3,2},{4,7},{5,4},{6,5},{7,6},{8,11},{9,8},{10,9... | collective-permute-start | bytes 884744 | tf_op jit(solution)/shard_map/ppermute | solution.py:41
  55.5 9.8 %attend.2 = (bf16[2,768,128]{2,1,0:T(8,128)(2,1)S(1)}, bf16[2,2,768,128]{3,2,1,0:T(8,128)(2,1)S(1)}, bf16[2,2,384,128]{3,2,1,0:T(8,128)(2,1)S(1)}, f32[2,2,768,128]{3,2,1,0:T(8,128)S(1)}) custom-call(s32[2,3]{1,0:T(2,128)S(1)} %copy-done.4, bf16[2,2,768,128]{3,2,1,0:T(8,128)(2,1)S(1)} %collective-permute-done.3.near_, ...), custom_call_target="tpu_custom_call" | custom-call | flops 11000000512 | bytes 6000000 | tf_op jit(solution)/shard_map/attend/pallas_call | solution.py:225
  65.3 4.1 %collective-permute-start.9 = (bf16[2,2,384,128]{3,2,1,0:T(8,128)(2,1)S(1)}, bf16[2,2,384,128]{3,2,1,0:T(8,128)(2,1)S(1)}, u32[]{:S(2)}, u32[]{:S(2)}) collective-permute-start(bf16[2,2,384,128]{3,2,1,0:T(8,128)(2,1)S(1)} %get-tuple-element.58), channel_id=1, source_target_pairs={{8,0},{12,4},{16,8},{20,12},{24,16},{28,20},{32,24},{36,28},{40,32... | collective-permute-start | bytes 1179656 | tf_op jit(solution)/shard_map/ppermute | solution.py:47
  69.4 3.7 %collective-permute-start.8 = (bf16[2,2,768,128]{3,2,1,0:T(8,128)(2,1)S(1)}, bf16[2,2,768,128]{3,2,1,0:T(8,128)(2,1)S(1)}, u32[]{:S(2)}, u32[]{:S(2)}) collective-permute-start(bf16[2,2,768,128]{3,2,1,0:T(8,128)(2,1)S(1)} %get-tuple-element.57), channel_id=1, source_target_pairs={{4,0},{8,4},{12,8},{16,12},{20,16},{24,20},{28,24},{32,28},{36,32}... | collective-permute-start | bytes 2359304 | tf_op jit(solution)/shard_map/ppermute | solution.py:47
  73.2 14.4 %attend.3 = (bf16[3,768,128]{2,1,0:T(8,128)(2,1)S(1)}, bf16[3,2,768,128]{3,2,1,0:T(8,128)(2,1)S(1)}, bf16[3,2,384,128]{3,2,1,0:T(8,128)(2,1)S(1)}, f32[3,2,768,128]{3,2,1,0:T(8,128)S(1)}) custom-call(s32[2,3]{1,0:T(2,128)S(1)} %copy-done.4, bf16[3,2,768,128]{3,2,1,0:T(8,128)(2,1)S(1)} %collective-permute-done.10.near_, ...), custom_call_target="tpu_custom_call" | custom-call | flops 16499999744 | bytes 9000000 | tf_op jit(solution)/shard_map/attend/pallas_call | solution.py:225
  87.7 8.6 %collective-permute-start.18 = (bf16[3,2,768,128]{3,2,1,0:T(8,128)(2,1)S(1)}, bf16[3,2,768,128]{3,2,1,0:T(8,128)(2,1)S(1)}, u32[]{:S(2)}, u32[]{:S(2)}) collective-permute-start(bf16[3,2,768,128]{3,2,1,0:T(8,128)(2,1)S(1)} %get-tuple-element.82), channel_id=1, source_target_pairs={{4,0},{8,4},{12,8},{16,12},{20,16},{24,20},{28,24},{32,28},{36,32}... | collective-permute-start | bytes 3538952 | tf_op jit(solution)/shard_map/ppermute | solution.py:47
  96.3 3.9 %collective-permute-start.19 = (bf16[3,2,384,128]{3,2,1,0:T(8,128)(2,1)S(1)}, bf16[3,2,384,128]{3,2,1,0:T(8,128)(2,1)S(1)}, u32[]{:S(2)}, u32[]{:S(2)}) collective-permute-start(bf16[3,2,384,128]{3,2,1,0:T(8,128)(2,1)S(1)} %get-tuple-element.83), channel_id=1, source_target_pairs={{8,0},{12,4},{16,8},{20,12},{24,16},{28,20},{32,24},{36,28},{40,32... | collective-permute-start | bytes 1769480 | tf_op jit(solution)/shard_map/ppermute | solution.py:47
  102.1 1.8 %collective-permute-start.16 = (bf16[9,192,128]{2,1,0:T(8,128)(2,1)S(1)}, bf16[9,192,128]{2,1,0:T(8,128)(2,1)S(1)}, u32[]{:S(2)}, u32[]{:S(2)}) collective-permute-start(bf16[9,192,128]{2,1,0:T(8,128)(2,1)S(1)} %get-tuple-element.79), channel_id=1, source_target_pairs={{0,3},{1,0},{2,1},{3,2},{4,7},{5,4},{6,5},{7,6},{8,11},{9,8},{10,9... | collective-permute-start | bytes 1327112 | tf_op jit(solution)/shard_map/ppermute | solution.py:41
  105.0 17.6 %collective-permute-done.19.refs_2_ = bf16[3,2,384,128]{3,2,1,0:T(8,128)(2,1)S(1)} collective-permute-done((bf16[3,2,384,128]{3,2,1,0:T(8,128)(2,1)S(1)}, bf16[3,2,384,128]{3,2,1,0:T(8,128)(2,1)S(1)}, u32[]{:S(2)}, u32[]{:S(2)}) %collective-permute-start.19) | collective-permute-done | bytes 589856 | tf_op jit(solution)/shard_map/ppermute | solution.py:47
  124.6 2.6 %collective-permute-start.21 = (bf16[6,192,128]{2,1,0:T(8,128)(2,1)S(1)}, bf16[6,192,128]{2,1,0:T(8,128)(2,1)S(1)}, u32[]{:S(2)}, u32[]{:S(2)}) collective-permute-start(bf16[6,192,128]{2,1,0:T(8,128)(2,1)S(1)} %get-tuple-element.88), channel_id=1, source_target_pairs={{0,3},{1,0},{2,1},{3,2},{4,7},{5,4},{6,5},{7,6},{8,11},{9,8},{10,9... | collective-permute-start | bytes 884744 | tf_op jit(solution)/shard_map/ppermute | solution.py:41
  127.2 6.6 %collective-permute-done.22.refs_7_ = bf16[6,192,128]{2,1,0:T(8,128)(2,1)S(1)} collective-permute-done((bf16[6,192,128]{2,1,0:T(8,128)(2,1)S(1)}, bf16[6,192,128]{2,1,0:T(8,128)(2,1)S(1)}, u32[]{:S(2)}, u32[]{:S(2)}) %collective-permute-start.22) | collective-permute-done | bytes 294944 | tf_op jit(solution)/shard_map/ppermute | solution.py:41
  135.0 1.9 %collective-permute-done.20.refs_5_ = bf16[6,192,128]{2,1,0:T(8,128)(2,1)S(1)} collective-permute-done((bf16[6,192,128]{2,1,0:T(8,128)(2,1)S(1)}, bf16[6,192,128]{2,1,0:T(8,128)(2,1)S(1)}, u32[]{:S(2)}, u32[]{:S(2)}) %collective-permute-start.20) | collective-permute-done | bytes 294944 | tf_op jit(solution)/shard_map/ppermute | solution.py:41
  136.9 2.3 %place.1 = (bf16[192,2560]{1,0:T(8,128)(2,1)}, bf16[192,2560]{1,0:T(8,128)(2,1)}, bf16[192,2560]{1,0:T(8,128)(2,1)}) custom-call(bf16[9,192,128]{2,1,0:T(8,128)(2,1)S(1)} %get-tuple-element.77.refs_0_, bf16[9,192,128]{2,1,0:T(8,128)(2,1)S(1)} %collective-permute-done.15.refs_1_, bf16[9,192,128]{2,1,0:T(8,128)(2,1)S(1)} %collective-permute-done.16.refs_2_, ...), custom_call_target="tpu_custom_call" | custom-call | bytes 5898240 | tf_op jit(solution)/shard_map/place/pallas_call | solution.py:298
  (42 shorter events, 17.2 us)
Async XLA Ops:
  3.1 8.0 %collective-permute-start = (bf16[4,192,128]{2,1,0:T(8,128)(2,1)S(1)}, bf16[4,192,128]{2,1,0:T(8,128)(2,1)S(1)}, u32[]{:S(2)}, u32[]{:S(2)}) collective-permute-start(bf16[4,192,128]{2,1,0:T(8,128)(2,1)S(1)} %get-tuple-element.47), channel_id=1, source_target_pairs={{0,1},{1,2},{2,3},{3,0},{4,5},{5,6},{6,7},{7,4},{8,9},{9,10},{10,1... | collective-permute-start | bytes 589832 | tf_op jit(solution)/shard_map/ppermute | solution.py:41
  4.8 9.9 %collective-permute-start.1 = (bf16[4,192,128]{2,1,0:T(8,128)(2,1)S(1)}, bf16[4,192,128]{2,1,0:T(8,128)(2,1)S(1)}, u32[]{:S(2)}, u32[]{:S(2)}) collective-permute-start(bf16[4,192,128]{2,1,0:T(8,128)(2,1)S(1)} %get-tuple-element.48), channel_id=1, source_target_pairs={{0,3},{1,0},{2,1},{3,2},{4,7},{5,4},{6,5},{7,6},{8,11},{9,8},{10,9... | collective-permute-start | bytes 589832 | tf_op jit(solution)/shard_map/ppermute | solution.py:41
  6.5 12.1 %copy-start.3 = (bf16[192,2560]{1,0:T(8,128)(2,1)S(1)}, bf16[192,2560]{1,0:T(8,128)(2,1)}, u32[]{:S(2)}) copy-start(bf16[192,2560]{1,0:T(8,128)(2,1)} %upstream.3) | copy-start | bytes 2949124
  6.5 10.1 %collective-permute-start.2 = (bf16[4,192,128]{2,1,0:T(8,128)(2,1)S(1)}, bf16[4,192,128]{2,1,0:T(8,128)(2,1)S(1)}, u32[]{:S(2)}, u32[]{:S(2)}) collective-permute-start(bf16[4,192,128]{2,1,0:T(8,128)(2,1)S(1)} %get-tuple-element.49), channel_id=1, source_target_pairs={{0,2},{1,3},{2,0},{3,1},{4,6},{5,7},{6,4},{7,5},{8,10},{9,11},{10,... | collective-permute-start | bytes 589832 | tf_op jit(solution)/shard_map/ppermute | solution.py:41
  16.6 27.4 %collective-permute-start.3 = (bf16[2,2,768,128]{3,2,1,0:T(8,128)(2,1)S(1)}, bf16[2,2,768,128]{3,2,1,0:T(8,128)(2,1)S(1)}, u32[]{:S(2)}, u32[]{:S(2)}) collective-permute-start(bf16[2,2,768,128]{3,2,1,0:T(8,128)(2,1)S(1)} %get-tuple-element.50.own_), channel_id=1, source_target_pairs={{0,4},{4,8},{8,12},{12,16},{16,20},{20,24},{24,28},{28,32},{32,36}... | collective-permute-start | bytes 2359304 | tf_op jit(solution)/shard_map/ppermute | solution.py:47
  18.9 14.3 %collective-permute-start.5 = (bf16[10,192,128]{2,1,0:T(8,128)(2,1)S(1)}, bf16[10,192,128]{2,1,0:T(8,128)(2,1)S(1)}, u32[]{:S(2)}, u32[]{:S(2)}) collective-permute-start(bf16[10,192,128]{2,1,0:T(8,128)(2,1)S(1)} %get-tuple-element.52), channel_id=1, source_target_pairs={{0,1},{1,2},{2,3},{3,0},{4,5},{5,6},{6,7},{7,4},{8,9},{9,10},{10,1... | collective-permute-start | bytes 1474568 | tf_op jit(solution)/shard_map/ppermute | solution.py:41
  20.1 13.4 %collective-permute-start.6 = (bf16[10,192,128]{2,1,0:T(8,128)(2,1)S(1)}, bf16[10,192,128]{2,1,0:T(8,128)(2,1)S(1)}, u32[]{:S(2)}, u32[]{:S(2)}) collective-permute-start(bf16[10,192,128]{2,1,0:T(8,128)(2,1)S(1)} %get-tuple-element.53), channel_id=1, source_target_pairs={{0,3},{1,0},{2,1},{3,2},{4,7},{5,4},{6,5},{7,6},{8,11},{9,8},{10,9... | collective-permute-start | bytes 1474568 | tf_op jit(solution)/shard_map/ppermute | solution.py:41
  22.2 21.6 %collective-permute-start.7 = (bf16[10,192,128]{2,1,0:T(8,128)(2,1)S(1)}, bf16[10,192,128]{2,1,0:T(8,128)(2,1)S(1)}, u32[]{:S(2)}, u32[]{:S(2)}) collective-permute-start(bf16[10,192,128]{2,1,0:T(8,128)(2,1)S(1)} %get-tuple-element.54), channel_id=1, source_target_pairs={{0,2},{1,3},{2,0},{3,1},{4,6},{5,7},{6,4},{7,5},{8,10},{9,11},{10,... | collective-permute-start | bytes 1474568 | tf_op jit(solution)/shard_map/ppermute | solution.py:41
  22.3 21.7 %collective-permute-start.4 = (bf16[2,2,384,128]{3,2,1,0:T(8,128)(2,1)S(1)}, bf16[2,2,384,128]{3,2,1,0:T(8,128)(2,1)S(1)}, u32[]{:S(2)}, u32[]{:S(2)}) collective-permute-start(bf16[2,2,384,128]{3,2,1,0:T(8,128)(2,1)S(1)} %get-tuple-element.51), channel_id=1, source_target_pairs={{0,8},{4,12},{8,16},{12,20},{16,24},{20,28},{24,32},{28,36},{32,40... | collective-permute-start | bytes 1179656 | tf_op jit(solution)/shard_map/ppermute | solution.py:47
  44.0 29.2 %collective-permute-start.10 = (bf16[3,2,768,128]{3,2,1,0:T(8,128)(2,1)S(1)}, bf16[3,2,768,128]{3,2,1,0:T(8,128)(2,1)S(1)}, u32[]{:S(2)}, u32[]{:S(2)}) collective-permute-start(bf16[3,2,768,128]{3,2,1,0:T(8,128)(2,1)S(1)} %get-tuple-element.61.own_), channel_id=1, source_target_pairs={{0,4},{4,8},{8,12},{12,16},{16,20},{20,24},{24,28},{28,32},{32,36}... | collective-permute-start | bytes 3538952 | tf_op jit(solution)/shard_map/ppermute | solution.py:47
  47.0 26.2 %collective-permute-start.11 = (bf16[3,2,384,128]{3,2,1,0:T(8,128)(2,1)S(1)}, bf16[3,2,384,128]{3,2,1,0:T(8,128)(2,1)S(1)}, u32[]{:S(2)}, u32[]{:S(2)}) collective-permute-start(bf16[3,2,384,128]{3,2,1,0:T(8,128)(2,1)S(1)} %get-tuple-element.62), channel_id=1, source_target_pairs={{0,8},{4,12},{8,16},{12,20},{16,24},{20,28},{24,32},{28,36},{32,40... | collective-permute-start | bytes 1769480 | tf_op jit(solution)/shard_map/ppermute | solution.py:47
  50.8 14.5 %collective-permute-start.12 = (bf16[6,192,128]{2,1,0:T(8,128)(2,1)S(1)}, bf16[6,192,128]{2,1,0:T(8,128)(2,1)S(1)}, u32[]{:S(2)}, u32[]{:S(2)}) collective-permute-start(bf16[6,192,128]{2,1,0:T(8,128)(2,1)S(1)} %get-tuple-element.66), channel_id=1, source_target_pairs={{0,1},{1,2},{2,3},{3,0},{4,5},{5,6},{6,7},{7,4},{8,9},{9,10},{10,1... | collective-permute-start | bytes 884744 | tf_op jit(solution)/shard_map/ppermute | solution.py:41
  52.3 17.1 %collective-permute-start.13 = (bf16[6,192,128]{2,1,0:T(8,128)(2,1)S(1)}, bf16[6,192,128]{2,1,0:T(8,128)(2,1)S(1)}, u32[]{:S(2)}, u32[]{:S(2)}) collective-permute-start(bf16[6,192,128]{2,1,0:T(8,128)(2,1)S(1)} %get-tuple-element.67), channel_id=1, source_target_pairs={{0,3},{1,0},{2,1},{3,2},{4,7},{5,4},{6,5},{7,6},{8,11},{9,8},{10,9... | collective-permute-start | bytes 884744 | tf_op jit(solution)/shard_map/ppermute | solution.py:41
  54.1 19.0 %collective-permute-start.14 = (bf16[6,192,128]{2,1,0:T(8,128)(2,1)S(1)}, bf16[6,192,128]{2,1,0:T(8,128)(2,1)S(1)}, u32[]{:S(2)}, u32[]{:S(2)}) collective-permute-start(bf16[6,192,128]{2,1,0:T(8,128)(2,1)S(1)} %get-tuple-element.68), channel_id=1, source_target_pairs={{0,2},{1,3},{2,0},{3,1},{4,6},{5,7},{6,4},{7,5},{8,10},{9,11},{10,... | collective-permute-start | bytes 884744 | tf_op jit(solution)/shard_map/ppermute | solution.py:41
  65.3 22.3 %collective-permute-start.9 = (bf16[2,2,384,128]{3,2,1,0:T(8,128)(2,1)S(1)}, bf16[2,2,384,128]{3,2,1,0:T(8,128)(2,1)S(1)}, u32[]{:S(2)}, u32[]{:S(2)}) collective-permute-start(bf16[2,2,384,128]{3,2,1,0:T(8,128)(2,1)S(1)} %get-tuple-element.58), channel_id=1, source_target_pairs={{8,0},{12,4},{16,8},{20,12},{24,16},{28,20},{32,24},{36,28},{40,32... | collective-permute-start | bytes 1179656 | tf_op jit(solution)/shard_map/ppermute | solution.py:47
  69.4 18.2 %collective-permute-start.8 = (bf16[2,2,768,128]{3,2,1,0:T(8,128)(2,1)S(1)}, bf16[2,2,768,128]{3,2,1,0:T(8,128)(2,1)S(1)}, u32[]{:S(2)}, u32[]{:S(2)}) collective-permute-start(bf16[2,2,768,128]{3,2,1,0:T(8,128)(2,1)S(1)} %get-tuple-element.57), channel_id=1, source_target_pairs={{4,0},{8,4},{12,8},{16,12},{20,16},{24,20},{28,24},{32,28},{36,32}... | collective-permute-start | bytes 2359304 | tf_op jit(solution)/shard_map/ppermute | solution.py:47
  87.7 35.0 %collective-permute-start.18 = (bf16[3,2,768,128]{3,2,1,0:T(8,128)(2,1)S(1)}, bf16[3,2,768,128]{3,2,1,0:T(8,128)(2,1)S(1)}, u32[]{:S(2)}, u32[]{:S(2)}) collective-permute-start(bf16[3,2,768,128]{3,2,1,0:T(8,128)(2,1)S(1)} %get-tuple-element.82), channel_id=1, source_target_pairs={{4,0},{8,4},{12,8},{16,12},{20,16},{24,20},{28,24},{32,28},{36,32}... | collective-permute-start | bytes 3538952 | tf_op jit(solution)/shard_map/ppermute | solution.py:47
  96.3 26.3 %collective-permute-start.19 = (bf16[3,2,384,128]{3,2,1,0:T(8,128)(2,1)S(1)}, bf16[3,2,384,128]{3,2,1,0:T(8,128)(2,1)S(1)}, u32[]{:S(2)}, u32[]{:S(2)}) collective-permute-start(bf16[3,2,384,128]{3,2,1,0:T(8,128)(2,1)S(1)} %get-tuple-element.83), channel_id=1, source_target_pairs={{8,0},{12,4},{16,8},{20,12},{24,16},{28,20},{32,24},{36,28},{40,32... | collective-permute-start | bytes 1769480 | tf_op jit(solution)/shard_map/ppermute | solution.py:47
  100.6 22.5 %collective-permute-start.15 = (bf16[9,192,128]{2,1,0:T(8,128)(2,1)S(1)}, bf16[9,192,128]{2,1,0:T(8,128)(2,1)S(1)}, u32[]{:S(2)}, u32[]{:S(2)}) collective-permute-start(bf16[9,192,128]{2,1,0:T(8,128)(2,1)S(1)} %get-tuple-element.78), channel_id=1, source_target_pairs={{0,1},{1,2},{2,3},{3,0},{4,5},{5,6},{6,7},{7,4},{8,9},{9,10},{10,1... | collective-permute-start | bytes 1327112 | tf_op jit(solution)/shard_map/ppermute | solution.py:41
  102.1 21.0 %collective-permute-start.16 = (bf16[9,192,128]{2,1,0:T(8,128)(2,1)S(1)}, bf16[9,192,128]{2,1,0:T(8,128)(2,1)S(1)}, u32[]{:S(2)}, u32[]{:S(2)}) collective-permute-start(bf16[9,192,128]{2,1,0:T(8,128)(2,1)S(1)} %get-tuple-element.79), channel_id=1, source_target_pairs={{0,3},{1,0},{2,1},{3,2},{4,7},{5,4},{6,5},{7,6},{8,11},{9,8},{10,9... | collective-permute-start | bytes 1327112 | tf_op jit(solution)/shard_map/ppermute | solution.py:41
  103.9 19.2 %collective-permute-start.17 = (bf16[9,192,128]{2,1,0:T(8,128)(2,1)S(1)}, bf16[9,192,128]{2,1,0:T(8,128)(2,1)S(1)}, u32[]{:S(2)}, u32[]{:S(2)}) collective-permute-start(bf16[9,192,128]{2,1,0:T(8,128)(2,1)S(1)} %get-tuple-element.80), channel_id=1, source_target_pairs={{0,2},{1,3},{2,0},{3,1},{4,6},{5,7},{6,4},{7,5},{8,10},{9,11},{10,... | collective-permute-start | bytes 1327112 | tf_op jit(solution)/shard_map/ppermute | solution.py:41
  123.2 10.7 %collective-permute-start.22 = (bf16[6,192,128]{2,1,0:T(8,128)(2,1)S(1)}, bf16[6,192,128]{2,1,0:T(8,128)(2,1)S(1)}, u32[]{:S(2)}, u32[]{:S(2)}) collective-permute-start(bf16[6,192,128]{2,1,0:T(8,128)(2,1)S(1)} %get-tuple-element.90), channel_id=1, source_target_pairs={{0,2},{1,3},{2,0},{3,1},{4,6},{5,7},{6,4},{7,5},{8,10},{9,11},{10,... | collective-permute-start | bytes 884744 | tf_op jit(solution)/shard_map/ppermute | solution.py:41
  124.6 10.4 %collective-permute-start.21 = (bf16[6,192,128]{2,1,0:T(8,128)(2,1)S(1)}, bf16[6,192,128]{2,1,0:T(8,128)(2,1)S(1)}, u32[]{:S(2)}, u32[]{:S(2)}) collective-permute-start(bf16[6,192,128]{2,1,0:T(8,128)(2,1)S(1)} %get-tuple-element.88), channel_id=1, source_target_pairs={{0,3},{1,0},{2,1},{3,2},{4,7},{5,4},{6,5},{7,6},{8,11},{9,8},{10,9... | collective-permute-start | bytes 884744 | tf_op jit(solution)/shard_map/ppermute | solution.py:41
  127.2 9.7 %collective-permute-start.20 = (bf16[6,192,128]{2,1,0:T(8,128)(2,1)S(1)}, bf16[6,192,128]{2,1,0:T(8,128)(2,1)S(1)}, u32[]{:S(2)}, u32[]{:S(2)}) collective-permute-start(bf16[6,192,128]{2,1,0:T(8,128)(2,1)S(1)} %get-tuple-element.86), channel_id=1, source_target_pairs={{0,1},{1,2},{2,3},{3,0},{4,5},{5,6},{6,7},{7,4},{8,9},{9,10},{10,1... | collective-permute-start | bytes 884744 | tf_op jit(solution)/shard_map/ppermute | solution.py:41
  (4 other events, 26.1 us)

commit v3 on v2

--- a/solution.py
+++ b/solution.py
@@ -127,7 +127,7 @@
             jax.ShapeDtypeStruct((n, 2, GR, HD), BF),
         ],
         compiler_params=small(),
-        cost_estimate=cost(0, 6 * 2 * GR * n * HD * 2),
+        cost_estimate=cost(0 if heads[0] == 0 else 3e10, 6 * 2 * GR * n * HD * 2),
         name="join",
     )(k, v, *r)
 
@@ -282,24 +282,25 @@
     )(*operands)
 
 
-def place_kernel(*refs):
-    outs = dict(zip("qkv", refs[-3:]))
+def place_kernel(names, *refs):
+    outs = dict(zip(names, refs[-len(names) :]))
     me = lax.axis_index("head")
-    for c, stage in enumerate(OUT_STAGES):
+    for c, stage in enumerate(OUT_STAGES[: len(refs) // 4]):
         for d, r in zip((0, 1, 3, 2), refs[4 * c : 4 * c + 4]):
             owner = lax.rem(me + 4 - d, 4)
             for u, (name, head) in enumerate(out_units(stage)):
-                outs[name][:, columns(owner, head)] = r[u]
-
-
-def place(pieces):
+                if name in names:
+                    outs[name][:, columns(owner, head)] = r[u]
+
+
+def place(names, pieces):
     out = jax.ShapeDtypeStruct((PR, 4 * HEADS_DEV * HD), BF)
     n = len(pieces)
     return pl.pallas_call(
-        place_kernel,
+        functools.partial(place_kernel, names),
         in_specs=[VM] * n,
-        out_specs=[VM] * 3,
-        out_shape=[out] * 3,
+        out_specs=[VM] * len(names),
+        out_shape=[out] * len(names),
         compiler_params=small(),
         cost_estimate=cost(0, 6 * PR * 2560 * 2),
         name="place",
@@ -366,6 +367,7 @@
         pieces[j] = [kept[j], *shift_all(parts)]
 
     send_in(0)
+    packed[1] = [after(x, y) for x, y in zip(packed[1], came[0])]
     send_in(1)
     join_chunk(0)
     send_near(0)
@@ -385,7 +387,9 @@
     parts1 = settle_stage(1)
     parts1 = [after(x, y) for x, y in zip(parts1, pieces[0][1:])]
     send_out(1, parts1)
-    return place([x for j in range(2) for x in pieces[j]])
+    (grad_q,) = place("q", pieces[0])
+    grad_k, grad_v = place("kv", pieces[0] + pieces[1])
+    return grad_q, grad_k, grad_v
 
 
 def solution(mesh):

time: 140 us -> 137 us (0.979)
  starting transfers between devices: 54.6 us -> 49.7 us
    ppermute x8, waiting for transfers between devices: 17.6 us -> 24.5 us  [tm_shift(): return lax.ppermute(block, 'tm', route)]
    ppermute x15, waiting for transfers between devices: 35.5 us -> 29.9 us  [head_shift(): lax.ppermute(block, 'head', [(i, (i + distance) % n) for i in range(n)])]
    ppermute x8, starting transfers between devices: 32.7 us -> 28.6 us  [tm_shift(): return lax.ppermute(block, 'tm', route)]
    pallas_call x1 -> x2, Pallas kernels: 2.29 us -> 2.99 us  [place(): pl.pallas_call(functools.partial(place_kernel, names), in_specs=[VM] * n,...]
  transfers between devices with their start and end apart: 23 -> 23, of which waited for: 10 -> 11; matrix products, arithmetic and copies ran while one was open for 0% -> 0% of each run, Pallas kernels for 18% -> 20%
where the time goes in v3:
time: 137 us; the launch traced here: 136 us
  waiting for transfers between devices  54.4 us (40%)
  starting transfers between devices  49.7 us (36%)
  Pallas kernels  28.8 us (21%)
  local copies, waits for them, and re-layouts  2.41 us (2%)
    ppermute x15, waiting for transfers between devices, head_shift(): lax.ppermute(block, 'head', [(i, (i + distance) % n) for i in range(n)])  29.9 us
    ppermute x8, starting transfers between devices, tm_shift(): return lax.ppermute(block, 'tm', route)  28.6 us
    ppermute x8, waiting for transfers between devices, tm_shift(): return lax.ppermute(block, 'tm', route)  24.5 us
    pallas_call x2, Pallas kernels, attend(): pl.pallas_call(functools.partial(attend_kernel, heads, base), in_specs=[p...  24.2 us
    ppermute x15, starting transfers between devices, head_shift(): lax.ppermute(block, 'head', [(i, (i + distance) % n) for i in range(n)])  21.1 us
    pallas_call x2, Pallas kernels, place(): pl.pallas_call(functools.partial(place_kernel, names), in_specs=[VM] * n,...  2.99 us
  transfers between devices with their start and end apart: 23, of which 11 were waited for; matrix products, arithmetic and copies ran while one was open for 0% of the time, Pallas kernels for 20%

profile of v3, /device:TPU:6, one launch (start us, length us, event | category | flops | bytes accessed | tf_op | source)
XLA Modules:
  0.0 136.2 jit_solution(2657764515674998059)
XLA Ops:
  6.5 2.0 %collective-permute-start.2 = (bf16[4,192,128]{2,1,0:T(8,128)(2,1)S(1)}, bf16[4,192,128]{2,1,0:T(8,128)(2,1)S(1)}, u32[]{:S(2)}, u32[]{:S(2)}) collective-permute-start(bf16[4,192,128]{2,1,0:T(8,128)(2,1)S(1)} %get-tuple-element.54), channel_id=1, source_target_pairs={{0,2},{1,3},{2,0},{3,1},{4,6},{5,7},{6,4},{7,5},{8,10},{9,11},{10,... | collective-permute-start | bytes 589832 | tf_op jit(solution)/shard_map/ppermute | solution.py:41
  8.7 2.4 %collective-permute-done.r1 = bf16[4,192,128]{2,1,0:T(8,128)(2,1)S(1)} collective-permute-done((bf16[4,192,128]{2,1,0:T(8,128)(2,1)S(1)}, bf16[4,192,128]{2,1,0:T(8,128)(2,1)S(1)}, u32[]{:S(2)}, u32[]{:S(2)}) %collective-permute-start) | collective-permute-done | bytes 196640 | tf_op jit(solution)/shard_map/ppermute | solution.py:41
  11.1 3.6 %collective-permute-done.1.r2 = bf16[4,192,128]{2,1,0:T(8,128)(2,1)S(1)} collective-permute-done((bf16[4,192,128]{2,1,0:T(8,128)(2,1)S(1)}, bf16[4,192,128]{2,1,0:T(8,128)(2,1)S(1)}, u32[]{:S(2)}, u32[]{:S(2)}) %collective-permute-start.1) | collective-permute-done | bytes 196640 | tf_op jit(solution)/shard_map/ppermute | solution.py:41
  14.7 1.8 %collective-permute-done.2.r3 = bf16[4,192,128]{2,1,0:T(8,128)(2,1)S(1)} collective-permute-done((bf16[4,192,128]{2,1,0:T(8,128)(2,1)S(1)}, bf16[4,192,128]{2,1,0:T(8,128)(2,1)S(1)}, u32[]{:S(2)}, u32[]{:S(2)}) %collective-permute-start.2) | collective-permute-done | bytes 196640 | tf_op jit(solution)/shard_map/ppermute | solution.py:41
  17.3 3.1 %collective-permute-start.6 = (bf16[10,192,128]{2,1,0:T(8,128)(2,1)S(1)}, bf16[10,192,128]{2,1,0:T(8,128)(2,1)S(1)}, u32[]{:S(2)}, u32[]{:S(2)}) collective-permute-start(bf16[10,192,128]{2,1,0:T(8,128)(2,1)S(1)} %get-tuple-element.60), channel_id=1, source_target_pairs={{0,3},{1,0},{2,1},{3,2},{4,7},{5,4},{6,5},{7,6},{8,11},{9,8},{10,9... | collective-permute-start | bytes 1474568 | tf_op jit(solution)/shard_map/ppermute | solution.py:41
  20.5 3.8 %collective-permute-start.4 = (bf16[2,2,384,128]{3,2,1,0:T(8,128)(2,1)S(1)}, bf16[2,2,384,128]{3,2,1,0:T(8,128)(2,1)S(1)}, u32[]{:S(2)}, u32[]{:S(2)}) collective-permute-start(bf16[2,2,384,128]{3,2,1,0:T(8,128)(2,1)S(1)} %get-tuple-element.56), channel_id=1, source_target_pairs={{0,8},{4,12},{8,16},{12,20},{16,24},{20,28},{24,32},{28,36},{32,40... | collective-permute-start | bytes 1179656 | tf_op jit(solution)/shard_map/ppermute | solution.py:47
  24.3 1.9 %collective-permute-start.3 = (bf16[2,2,768,128]{3,2,1,0:T(8,128)(2,1)S(1)}, bf16[2,2,768,128]{3,2,1,0:T(8,128)(2,1)S(1)}, u32[]{:S(2)}, u32[]{:S(2)}) collective-permute-start(bf16[2,2,768,128]{3,2,1,0:T(8,128)(2,1)S(1)} %get-tuple-element.55.own_), channel_id=1, source_target_pairs={{0,4},{4,8},{8,12},{12,16},{16,20},{20,24},{24,28},{28,32},{32,36}... | collective-permute-start | bytes 2359304 | tf_op jit(solution)/shard_map/ppermute | solution.py:47
  26.2 6.0 %collective-permute-done.7.r3 = bf16[10,192,128]{2,1,0:T(8,128)(2,1)S(1)} collective-permute-done((bf16[10,192,128]{2,1,0:T(8,128)(2,1)S(1)}, bf16[10,192,128]{2,1,0:T(8,128)(2,1)S(1)}, u32[]{:S(2)}, u32[]{:S(2)}) %collective-permute-start.7) | collective-permute-done | bytes 491552 | tf_op jit(solution)/shard_map/ppermute | solution.py:41
  32.2 7.0 %collective-permute-done.6.r2 = bf16[10,192,128]{2,1,0:T(8,128)(2,1)S(1)} collective-permute-done((bf16[10,192,128]{2,1,0:T(8,128)(2,1)S(1)}, bf16[10,192,128]{2,1,0:T(8,128)(2,1)S(1)}, u32[]{:S(2)}, u32[]{:S(2)}) %collective-permute-start.6) | collective-permute-done | bytes 491552 | tf_op jit(solution)/shard_map/ppermute | solution.py:41
  40.8 3.4 %collective-permute-done.3.near_ = bf16[2,2,768,128]{3,2,1,0:T(8,128)(2,1)S(1)} collective-permute-done((bf16[2,2,768,128]{3,2,1,0:T(8,128)(2,1)S(1)}, bf16[2,2,768,128]{3,2,1,0:T(8,128)(2,1)S(1)}, u32[]{:S(2)}, u32[]{:S(2)}) %collective-permute-start.3) | collective-permute-done | bytes 786464 | tf_op jit(solution)/shard_map/ppermute | solution.py:47
  44.3 1.9 %collective-permute-start.10 = (bf16[3,2,768,128]{3,2,1,0:T(8,128)(2,1)S(1)}, bf16[3,2,768,128]{3,2,1,0:T(8,128)(2,1)S(1)}, u32[]{:S(2)}, u32[]{:S(2)}) collective-permute-start(bf16[3,2,768,128]{3,2,1,0:T(8,128)(2,1)S(1)} %get-tuple-element.69.own_), channel_id=1, source_target_pairs={{0,4},{4,8},{8,12},{12,16},{16,20},{20,24},{24,28},{28,32},{32,36}... | collective-permute-start | bytes 3538952 | tf_op jit(solution)/shard_map/ppermute | solution.py:47
  46.4 1.9 %collective-permute-start.11 = (bf16[3,2,384,128]{3,2,1,0:T(8,128)(2,1)S(1)}, bf16[3,2,384,128]{3,2,1,0:T(8,128)(2,1)S(1)}, u32[]{:S(2)}, u32[]{:S(2)}) collective-permute-start(bf16[3,2,384,128]{3,2,1,0:T(8,128)(2,1)S(1)} %get-tuple-element.70), channel_id=1, source_target_pairs={{0,8},{4,12},{8,16},{12,20},{16,24},{20,28},{24,32},{28,36},{32,40... | collective-permute-start | bytes 1769480 | tf_op jit(solution)/shard_map/ppermute | solution.py:47
  48.7 2.9 %collective-permute-start.13 = (bf16[6,192,128]{2,1,0:T(8,128)(2,1)S(1)}, bf16[6,192,128]{2,1,0:T(8,128)(2,1)S(1)}, u32[]{:S(2)}, u32[]{:S(2)}) collective-permute-start(bf16[6,192,128]{2,1,0:T(8,128)(2,1)S(1)} %get-tuple-element.75), channel_id=1, source_target_pairs={{0,3},{1,0},{2,1},{3,2},{4,7},{5,4},{6,5},{7,6},{8,11},{9,8},{10,9... | collective-permute-start | bytes 884744 | tf_op jit(solution)/shard_map/ppermute | solution.py:41
  52.8 9.7 %attend.2 = (bf16[2,768,128]{2,1,0:T(8,128)(2,1)S(1)}, bf16[2,2,768,128]{3,2,1,0:T(8,128)(2,1)S(1)}, bf16[2,2,384,128]{3,2,1,0:T(8,128)(2,1)S(1)}, f32[2,2,768,128]{3,2,1,0:T(8,128)S(1)}) custom-call(s32[2,3]{1,0:T(2,128)S(1)} %copy-done.4, bf16[2,2,768,128]{3,2,1,0:T(8,128)(2,1)S(1)} %collective-permute-done.3.near_, ...), custom_call_target="tpu_custom_call" | custom-call | flops 11000000512 | bytes 6000000 | tf_op jit(solution)/shard_map/attend/pallas_call | solution.py:225
  62.5 6.0 %collective-permute-start.9 = (bf16[2,2,384,128]{3,2,1,0:T(8,128)(2,1)S(1)}, bf16[2,2,384,128]{3,2,1,0:T(8,128)(2,1)S(1)}, u32[]{:S(2)}, u32[]{:S(2)}) collective-permute-start(bf16[2,2,384,128]{3,2,1,0:T(8,128)(2,1)S(1)} %get-tuple-element.66), channel_id=1, source_target_pairs={{8,0},{12,4},{16,8},{20,12},{24,16},{28,20},{32,24},{36,28},{40,32... | collective-permute-start | bytes 1179656 | tf_op jit(solution)/shard_map/ppermute | solution.py:47
  68.6 2.5 %collective-permute-start.8 = (bf16[2,2,768,128]{3,2,1,0:T(8,128)(2,1)S(1)}, bf16[2,2,768,128]{3,2,1,0:T(8,128)(2,1)S(1)}, u32[]{:S(2)}, u32[]{:S(2)}) collective-permute-start(bf16[2,2,768,128]{3,2,1,0:T(8,128)(2,1)S(1)} %get-tuple-element.65), channel_id=1, source_target_pairs={{4,0},{8,4},{12,8},{16,12},{20,16},{24,20},{28,24},{32,28},{36,32}... | collective-permute-start | bytes 2359304 | tf_op jit(solution)/shard_map/ppermute | solution.py:47
  71.2 14.4 %attend.3 = (bf16[3,768,128]{2,1,0:T(8,128)(2,1)S(1)}, bf16[3,2,768,128]{3,2,1,0:T(8,128)(2,1)S(1)}, bf16[3,2,384,128]{3,2,1,0:T(8,128)(2,1)S(1)}, f32[3,2,768,128]{3,2,1,0:T(8,128)S(1)}) custom-call(s32[2,3]{1,0:T(2,128)S(1)} %copy-done.4, bf16[3,2,768,128]{3,2,1,0:T(8,128)(2,1)S(1)} %collective-permute-done.10.near_, ...), custom_call_target="tpu_custom_call" | custom-call | flops 16499999744 | bytes 9000000 | tf_op jit(solution)/shard_map/attend/pallas_call | solution.py:225
  85.6 7.6 %collective-permute-start.18 = (bf16[3,2,768,128]{3,2,1,0:T(8,128)(2,1)S(1)}, bf16[3,2,768,128]{3,2,1,0:T(8,128)(2,1)S(1)}, u32[]{:S(2)}, u32[]{:S(2)}) collective-permute-start(bf16[3,2,768,128]{3,2,1,0:T(8,128)(2,1)S(1)} %get-tuple-element.90), channel_id=1, source_target_pairs={{4,0},{8,4},{12,8},{16,12},{20,16},{24,20},{28,24},{32,28},{36,32}... | collective-permute-start | bytes 3538952 | tf_op jit(solution)/shard_map/ppermute | solution.py:47
  93.2 2.9 %collective-permute-start.19 = (bf16[3,2,384,128]{3,2,1,0:T(8,128)(2,1)S(1)}, bf16[3,2,384,128]{3,2,1,0:T(8,128)(2,1)S(1)}, u32[]{:S(2)}, u32[]{:S(2)}) collective-permute-start(bf16[3,2,384,128]{3,2,1,0:T(8,128)(2,1)S(1)} %get-tuple-element.91), channel_id=1, source_target_pairs={{8,0},{12,4},{16,8},{20,12},{24,16},{28,20},{32,24},{36,28},{40,32... | collective-permute-start | bytes 1769480 | tf_op jit(solution)/shard_map/ppermute | solution.py:47
  96.9 2.9 %collective-permute-start.16 = (bf16[9,192,128]{2,1,0:T(8,128)(2,1)S(1)}, bf16[9,192,128]{2,1,0:T(8,128)(2,1)S(1)}, u32[]{:S(2)}, u32[]{:S(2)}) collective-permute-start(bf16[9,192,128]{2,1,0:T(8,128)(2,1)S(1)} %get-tuple-element.87), channel_id=1, source_target_pairs={{0,3},{1,0},{2,1},{3,2},{4,7},{5,4},{6,5},{7,6},{8,11},{9,8},{10,9... | collective-permute-start | bytes 1327112 | tf_op jit(solution)/shard_map/ppermute | solution.py:41
  100.1 21.0 %collective-permute-done.19.refs_2_ = bf16[3,2,384,128]{3,2,1,0:T(8,128)(2,1)S(1)} collective-permute-done((bf16[3,2,384,128]{3,2,1,0:T(8,128)(2,1)S(1)}, bf16[3,2,384,128]{3,2,1,0:T(8,128)(2,1)S(1)}, u32[]{:S(2)}, u32[]{:S(2)}) %collective-permute-start.19) | collective-permute-done | bytes 589856 | tf_op jit(solution)/shard_map/ppermute | solution.py:47
  121.6 1.9 %collective-permute-start.22 = (bf16[6,192,128]{2,1,0:T(8,128)(2,1)S(1)}, bf16[6,192,128]{2,1,0:T(8,128)(2,1)S(1)}, u32[]{:S(2)}, u32[]{:S(2)}) collective-permute-start(bf16[6,192,128]{2,1,0:T(8,128)(2,1)S(1)} %get-tuple-element.98), channel_id=1, source_target_pairs={{0,2},{1,3},{2,0},{3,1},{4,6},{5,7},{6,4},{7,5},{8,10},{9,11},{10,... | collective-permute-start | bytes 884744 | tf_op jit(solution)/shard_map/ppermute | solution.py:41
  126.7 4.6 %collective-permute-done.22.refs_7_ = bf16[6,192,128]{2,1,0:T(8,128)(2,1)S(1)} collective-permute-done((bf16[6,192,128]{2,1,0:T(8,128)(2,1)S(1)}, bf16[6,192,128]{2,1,0:T(8,128)(2,1)S(1)}, u32[]{:S(2)}, u32[]{:S(2)}) %collective-permute-start.22) | collective-permute-done | bytes 294944 | tf_op jit(solution)/shard_map/ppermute | solution.py:41
  131.3 2.1 %collective-permute-done.21.refs_6_ = bf16[6,192,128]{2,1,0:T(8,128)(2,1)S(1)} collective-permute-done((bf16[6,192,128]{2,1,0:T(8,128)(2,1)S(1)}, bf16[6,192,128]{2,1,0:T(8,128)(2,1)S(1)}, u32[]{:S(2)}, u32[]{:S(2)}) %collective-permute-start.21) | collective-permute-done | bytes 294944 | tf_op jit(solution)/shard_map/ppermute | solution.py:41
  (43 shorter events, 17.7 us)
Async XLA Ops:
  3.1 8.0 %collective-permute-start = (bf16[4,192,128]{2,1,0:T(8,128)(2,1)S(1)}, bf16[4,192,128]{2,1,0:T(8,128)(2,1)S(1)}, u32[]{:S(2)}, u32[]{:S(2)}) collective-permute-start(bf16[4,192,128]{2,1,0:T(8,128)(2,1)S(1)} %get-tuple-element.52), channel_id=1, source_target_pairs={{0,1},{1,2},{2,3},{3,0},{4,5},{5,6},{6,7},{7,4},{8,9},{9,10},{10,1... | collective-permute-start | bytes 589832 | tf_op jit(solution)/shard_map/ppermute | solution.py:41
  4.8 9.9 %collective-permute-start.1 = (bf16[4,192,128]{2,1,0:T(8,128)(2,1)S(1)}, bf16[4,192,128]{2,1,0:T(8,128)(2,1)S(1)}, u32[]{:S(2)}, u32[]{:S(2)}) collective-permute-start(bf16[4,192,128]{2,1,0:T(8,128)(2,1)S(1)} %get-tuple-element.53), channel_id=1, source_target_pairs={{0,3},{1,0},{2,1},{3,2},{4,7},{5,4},{6,5},{7,6},{8,11},{9,8},{10,9... | collective-permute-start | bytes 589832 | tf_op jit(solution)/shard_map/ppermute | solution.py:41
  6.5 10.1 %collective-permute-start.2 = (bf16[4,192,128]{2,1,0:T(8,128)(2,1)S(1)}, bf16[4,192,128]{2,1,0:T(8,128)(2,1)S(1)}, u32[]{:S(2)}, u32[]{:S(2)}) collective-permute-start(bf16[4,192,128]{2,1,0:T(8,128)(2,1)S(1)} %get-tuple-element.54), channel_id=1, source_target_pairs={{0,2},{1,3},{2,0},{3,1},{4,6},{5,7},{6,4},{7,5},{8,10},{9,11},{10,... | collective-permute-start | bytes 589832 | tf_op jit(solution)/shard_map/ppermute | solution.py:41
  16.5 15.7 %collective-permute-start.7 = (bf16[10,192,128]{2,1,0:T(8,128)(2,1)S(1)}, bf16[10,192,128]{2,1,0:T(8,128)(2,1)S(1)}, u32[]{:S(2)}, u32[]{:S(2)}) collective-permute-start(bf16[10,192,128]{2,1,0:T(8,128)(2,1)S(1)} %get-tuple-element.62), channel_id=1, source_target_pairs={{0,2},{1,3},{2,0},{3,1},{4,6},{5,7},{6,4},{7,5},{8,10},{9,11},{10,... | collective-permute-start | bytes 1474568 | tf_op jit(solution)/shard_map/ppermute | solution.py:41
  17.3 22.0 %collective-permute-start.6 = (bf16[10,192,128]{2,1,0:T(8,128)(2,1)S(1)}, bf16[10,192,128]{2,1,0:T(8,128)(2,1)S(1)}, u32[]{:S(2)}, u32[]{:S(2)}) collective-permute-start(bf16[10,192,128]{2,1,0:T(8,128)(2,1)S(1)} %get-tuple-element.60), channel_id=1, source_target_pairs={{0,3},{1,0},{2,1},{3,2},{4,7},{5,4},{6,5},{7,6},{8,11},{9,8},{10,9... | collective-permute-start | bytes 1474568 | tf_op jit(solution)/shard_map/ppermute | solution.py:41
  20.3 20.3 %collective-permute-start.5 = (bf16[10,192,128]{2,1,0:T(8,128)(2,1)S(1)}, bf16[10,192,128]{2,1,0:T(8,128)(2,1)S(1)}, u32[]{:S(2)}, u32[]{:S(2)}) collective-permute-start(bf16[10,192,128]{2,1,0:T(8,128)(2,1)S(1)} %get-tuple-element.58), channel_id=1, source_target_pairs={{0,1},{1,2},{2,3},{3,0},{4,5},{5,6},{6,7},{7,4},{8,9},{9,10},{10,1... | collective-permute-start | bytes 1474568 | tf_op jit(solution)/shard_map/ppermute | solution.py:41
  20.5 20.4 %collective-permute-start.4 = (bf16[2,2,384,128]{3,2,1,0:T(8,128)(2,1)S(1)}, bf16[2,2,384,128]{3,2,1,0:T(8,128)(2,1)S(1)}, u32[]{:S(2)}, u32[]{:S(2)}) collective-permute-start(bf16[2,2,384,128]{3,2,1,0:T(8,128)(2,1)S(1)} %get-tuple-element.56), channel_id=1, source_target_pairs={{0,8},{4,12},{8,16},{12,20},{16,24},{20,28},{24,32},{28,36},{32,40... | collective-permute-start | bytes 1179656 | tf_op jit(solution)/shard_map/ppermute | solution.py:47
  24.3 20.0 %collective-permute-start.3 = (bf16[2,2,768,128]{3,2,1,0:T(8,128)(2,1)S(1)}, bf16[2,2,768,128]{3,2,1,0:T(8,128)(2,1)S(1)}, u32[]{:S(2)}, u32[]{:S(2)}) collective-permute-start(bf16[2,2,768,128]{3,2,1,0:T(8,128)(2,1)S(1)} %get-tuple-element.55.own_), channel_id=1, source_target_pairs={{0,4},{4,8},{8,12},{12,16},{16,20},{20,24},{24,28},{28,32},{32,36}... | collective-permute-start | bytes 2359304 | tf_op jit(solution)/shard_map/ppermute | solution.py:47
  40.8 12.0 %copy-start.4 = (s32[2,3]{1,0:T(2,128)S(1)}, s32[2,3]{1,0:T(2,128)}, u32[]{:S(2)}) copy-start(s32[2,3]{1,0:T(2,128)} %win.3) | copy-start | bytes 76
  44.3 26.9 %collective-permute-start.10 = (bf16[3,2,768,128]{3,2,1,0:T(8,128)(2,1)S(1)}, bf16[3,2,768,128]{3,2,1,0:T(8,128)(2,1)S(1)}, u32[]{:S(2)}, u32[]{:S(2)}) collective-permute-start(bf16[3,2,768,128]{3,2,1,0:T(8,128)(2,1)S(1)} %get-tuple-element.69.own_), channel_id=1, source_target_pairs={{0,4},{4,8},{8,12},{12,16},{16,20},{20,24},{24,28},{28,32},{32,36}... | collective-permute-start | bytes 3538952 | tf_op jit(solution)/shard_map/ppermute | solution.py:47
  46.4 24.8 %collective-permute-start.11 = (bf16[3,2,384,128]{3,2,1,0:T(8,128)(2,1)S(1)}, bf16[3,2,384,128]{3,2,1,0:T(8,128)(2,1)S(1)}, u32[]{:S(2)}, u32[]{:S(2)}) collective-permute-start(bf16[3,2,384,128]{3,2,1,0:T(8,128)(2,1)S(1)} %get-tuple-element.70), channel_id=1, source_target_pairs={{0,8},{4,12},{8,16},{12,20},{16,24},{20,28},{24,32},{28,36},{32,40... | collective-permute-start | bytes 1769480 | tf_op jit(solution)/shard_map/ppermute | solution.py:47
  48.3 14.2 %collective-permute-start.12 = (bf16[6,192,128]{2,1,0:T(8,128)(2,1)S(1)}, bf16[6,192,128]{2,1,0:T(8,128)(2,1)S(1)}, u32[]{:S(2)}, u32[]{:S(2)}) collective-permute-start(bf16[6,192,128]{2,1,0:T(8,128)(2,1)S(1)} %get-tuple-element.74), channel_id=1, source_target_pairs={{0,1},{1,2},{2,3},{3,0},{4,5},{5,6},{6,7},{7,4},{8,9},{9,10},{10,1... | collective-permute-start | bytes 884744 | tf_op jit(solution)/shard_map/ppermute | solution.py:41
  48.7 19.8 %collective-permute-start.13 = (bf16[6,192,128]{2,1,0:T(8,128)(2,1)S(1)}, bf16[6,192,128]{2,1,0:T(8,128)(2,1)S(1)}, u32[]{:S(2)}, u32[]{:S(2)}) collective-permute-start(bf16[6,192,128]{2,1,0:T(8,128)(2,1)S(1)} %get-tuple-element.75), channel_id=1, source_target_pairs={{0,3},{1,0},{2,1},{3,2},{4,7},{5,4},{6,5},{7,6},{8,11},{9,8},{10,9... | collective-permute-start | bytes 884744 | tf_op jit(solution)/shard_map/ppermute | solution.py:41
  51.6 19.5 %collective-permute-start.14 = (bf16[6,192,128]{2,1,0:T(8,128)(2,1)S(1)}, bf16[6,192,128]{2,1,0:T(8,128)(2,1)S(1)}, u32[]{:S(2)}, u32[]{:S(2)}) collective-permute-start(bf16[6,192,128]{2,1,0:T(8,128)(2,1)S(1)} %get-tuple-element.76), channel_id=1, source_target_pairs={{0,2},{1,3},{2,0},{3,1},{4,6},{5,7},{6,4},{7,5},{8,10},{9,11},{10,... | collective-permute-start | bytes 884744 | tf_op jit(solution)/shard_map/ppermute | solution.py:41
  62.5 23.1 %collective-permute-start.9 = (bf16[2,2,384,128]{3,2,1,0:T(8,128)(2,1)S(1)}, bf16[2,2,384,128]{3,2,1,0:T(8,128)(2,1)S(1)}, u32[]{:S(2)}, u32[]{:S(2)}) collective-permute-start(bf16[2,2,384,128]{3,2,1,0:T(8,128)(2,1)S(1)} %get-tuple-element.66), channel_id=1, source_target_pairs={{8,0},{12,4},{16,8},{20,12},{24,16},{28,20},{32,24},{36,28},{40,32... | collective-permute-start | bytes 1179656 | tf_op jit(solution)/shard_map/ppermute | solution.py:47
  68.6 17.0 %collective-permute-start.8 = (bf16[2,2,768,128]{3,2,1,0:T(8,128)(2,1)S(1)}, bf16[2,2,768,128]{3,2,1,0:T(8,128)(2,1)S(1)}, u32[]{:S(2)}, u32[]{:S(2)}) collective-permute-start(bf16[2,2,768,128]{3,2,1,0:T(8,128)(2,1)S(1)} %get-tuple-element.65), channel_id=1, source_target_pairs={{4,0},{8,4},{12,8},{16,12},{20,16},{24,20},{28,24},{32,28},{36,32}... | collective-permute-start | bytes 2359304 | tf_op jit(solution)/shard_map/ppermute | solution.py:47
  85.6 35.5 %collective-permute-start.18 = (bf16[3,2,768,128]{3,2,1,0:T(8,128)(2,1)S(1)}, bf16[3,2,768,128]{3,2,1,0:T(8,128)(2,1)S(1)}, u32[]{:S(2)}, u32[]{:S(2)}) collective-permute-start(bf16[3,2,768,128]{3,2,1,0:T(8,128)(2,1)S(1)} %get-tuple-element.90), channel_id=1, source_target_pairs={{4,0},{8,4},{12,8},{16,12},{20,16},{24,20},{28,24},{32,28},{36,32}... | collective-permute-start | bytes 3538952 | tf_op jit(solution)/shard_map/ppermute | solution.py:47
  93.2 27.9 %collective-permute-start.19 = (bf16[3,2,384,128]{3,2,1,0:T(8,128)(2,1)S(1)}, bf16[3,2,384,128]{3,2,1,0:T(8,128)(2,1)S(1)}, u32[]{:S(2)}, u32[]{:S(2)}) collective-permute-start(bf16[3,2,384,128]{3,2,1,0:T(8,128)(2,1)S(1)} %get-tuple-element.91), channel_id=1, source_target_pairs={{8,0},{12,4},{16,8},{20,12},{24,16},{28,20},{32,24},{36,28},{40,32... | collective-permute-start | bytes 1769480 | tf_op jit(solution)/shard_map/ppermute | solution.py:47
  96.5 25.0 %collective-permute-start.15 = (bf16[9,192,128]{2,1,0:T(8,128)(2,1)S(1)}, bf16[9,192,128]{2,1,0:T(8,128)(2,1)S(1)}, u32[]{:S(2)}, u32[]{:S(2)}) collective-permute-start(bf16[9,192,128]{2,1,0:T(8,128)(2,1)S(1)} %get-tuple-element.86), channel_id=1, source_target_pairs={{0,1},{1,2},{2,3},{3,0},{4,5},{5,6},{6,7},{7,4},{8,9},{9,10},{10,1... | collective-permute-start | bytes 1327112 | tf_op jit(solution)/shard_map/ppermute | solution.py:41
  96.9 24.7 %collective-permute-start.16 = (bf16[9,192,128]{2,1,0:T(8,128)(2,1)S(1)}, bf16[9,192,128]{2,1,0:T(8,128)(2,1)S(1)}, u32[]{:S(2)}, u32[]{:S(2)}) collective-permute-start(bf16[9,192,128]{2,1,0:T(8,128)(2,1)S(1)} %get-tuple-element.87), channel_id=1, source_target_pairs={{0,3},{1,0},{2,1},{3,2},{4,7},{5,4},{6,5},{7,6},{8,11},{9,8},{10,9... | collective-permute-start | bytes 1327112 | tf_op jit(solution)/shard_map/ppermute | solution.py:41
  99.9 21.8 %collective-permute-start.17 = (bf16[9,192,128]{2,1,0:T(8,128)(2,1)S(1)}, bf16[9,192,128]{2,1,0:T(8,128)(2,1)S(1)}, u32[]{:S(2)}, u32[]{:S(2)}) collective-permute-start(bf16[9,192,128]{2,1,0:T(8,128)(2,1)S(1)} %get-tuple-element.88), channel_id=1, source_target_pairs={{0,2},{1,3},{2,0},{3,1},{4,6},{5,7},{6,4},{7,5},{8,10},{9,11},{10,... | collective-permute-start | bytes 1327112 | tf_op jit(solution)/shard_map/ppermute | solution.py:41
  121.6 9.7 %collective-permute-start.22 = (bf16[6,192,128]{2,1,0:T(8,128)(2,1)S(1)}, bf16[6,192,128]{2,1,0:T(8,128)(2,1)S(1)}, u32[]{:S(2)}, u32[]{:S(2)}) collective-permute-start(bf16[6,192,128]{2,1,0:T(8,128)(2,1)S(1)} %get-tuple-element.98), channel_id=1, source_target_pairs={{0,2},{1,3},{2,0},{3,1},{4,6},{5,7},{6,4},{7,5},{8,10},{9,11},{10,... | collective-permute-start | bytes 884744 | tf_op jit(solution)/shard_map/ppermute | solution.py:41
  123.5 9.9 %collective-permute-start.21 = (bf16[6,192,128]{2,1,0:T(8,128)(2,1)S(1)}, bf16[6,192,128]{2,1,0:T(8,128)(2,1)S(1)}, u32[]{:S(2)}, u32[]{:S(2)}) collective-permute-start(bf16[6,192,128]{2,1,0:T(8,128)(2,1)S(1)} %get-tuple-element.96), channel_id=1, source_target_pairs={{0,3},{1,0},{2,1},{3,2},{4,7},{5,4},{6,5},{7,6},{8,11},{9,8},{10,9... | collective-permute-start | bytes 884744 | tf_op jit(solution)/shard_map/ppermute | solution.py:41
  124.7 9.6 %collective-permute-start.20 = (bf16[6,192,128]{2,1,0:T(8,128)(2,1)S(1)}, bf16[6,192,128]{2,1,0:T(8,128)(2,1)S(1)}, u32[]{:S(2)}, u32[]{:S(2)}) collective-permute-start(bf16[6,192,128]{2,1,0:T(8,128)(2,1)S(1)} %get-tuple-element.94), channel_id=1, source_target_pairs={{0,1},{1,2},{2,3},{3,0},{4,5},{5,6},{6,7},{7,4},{8,9},{9,10},{10,1... | collective-permute-start | bytes 884744 | tf_op jit(solution)/shard_map/ppermute | solution.py:41
  (4 other events, 13.2 us)

commit v4 on v3

--- a/solution.py
+++ b/solution.py
@@ -385,7 +385,6 @@
     send_out(0, parts0)
     send_back(1)
     parts1 = settle_stage(1)
-    parts1 = [after(x, y) for x, y in zip(parts1, pieces[0][1:])]
     send_out(1, parts1)
     (grad_q,) = place("q", pieces[0])
     grad_k, grad_v = place("kv", pieces[0] + pieces[1])

time: 137 us -> 136 us (level)
  no operation moved by 1% of the time
where the time goes in v4:
time: 136 us
  waiting for transfers between devices  53.4 us (39%)
  starting transfers between devices  50.3 us (37%)
  Pallas kernels  28.8 us (21%)
  local copies, waits for them, and re-layouts  2.41 us (2%)
    ppermute x15, waiting for transfers between devices, head_shift(): lax.ppermute(block, 'head', [(i, (i + distance) % n) for i in range(n)])  28.9 us
    ppermute x8, starting transfers between devices, tm_shift(): return lax.ppermute(block, 'tm', route)  28.6 us
    ppermute x8, waiting for transfers between devices, tm_shift(): return lax.ppermute(block, 'tm', route)  24.5 us
    pallas_call x2, Pallas kernels, attend(): pl.pallas_call(functools.partial(attend_kernel, heads, base), in_specs=[p...  24.2 us
    ppermute x15, starting transfers between devices, head_shift(): lax.ppermute(block, 'head', [(i, (i + distance) % n) for i in range(n)])  21.7 us
    pallas_call x2, Pallas kernels, place(): pl.pallas_call(functools.partial(place_kernel, names), in_specs=[VM] * n,...  2.99 us
  transfers between devices with their start and end apart: 23, of which 11 were waited for; matrix products, arithmetic and copies ran while one was open for 0% of the time, Pallas kernels for 20%

profile of v4, /device:TPU:6, one launch (start us, length us, event | category | flops | bytes accessed | tf_op | source)
XLA Modules:
  0.0 135.7 jit_solution(3291200802559469971)
XLA Ops:
  6.5 2.0 %collective-permute-start.2 = (bf16[4,192,128]{2,1,0:T(8,128)(2,1)S(1)}, bf16[4,192,128]{2,1,0:T(8,128)(2,1)S(1)}, u32[]{:S(2)}, u32[]{:S(2)}) collective-permute-start(bf16[4,192,128]{2,1,0:T(8,128)(2,1)S(1)} %get-tuple-element.51), channel_id=1, source_target_pairs={{0,2},{1,3},{2,0},{3,1},{4,6},{5,7},{6,4},{7,5},{8,10},{9,11},{10,... | collective-permute-start | bytes 589832 | tf_op jit(solution)/shard_map/ppermute | solution.py:41
  8.7 2.4 %collective-permute-done.r1 = bf16[4,192,128]{2,1,0:T(8,128)(2,1)S(1)} collective-permute-done((bf16[4,192,128]{2,1,0:T(8,128)(2,1)S(1)}, bf16[4,192,128]{2,1,0:T(8,128)(2,1)S(1)}, u32[]{:S(2)}, u32[]{:S(2)}) %collective-permute-start) | collective-permute-done | bytes 196640 | tf_op jit(solution)/shard_map/ppermute | solution.py:41
  11.1 3.6 %collective-permute-done.1.r2 = bf16[4,192,128]{2,1,0:T(8,128)(2,1)S(1)} collective-permute-done((bf16[4,192,128]{2,1,0:T(8,128)(2,1)S(1)}, bf16[4,192,128]{2,1,0:T(8,128)(2,1)S(1)}, u32[]{:S(2)}, u32[]{:S(2)}) %collective-permute-start.1) | collective-permute-done | bytes 196640 | tf_op jit(solution)/shard_map/ppermute | solution.py:41
  14.7 1.8 %collective-permute-done.2.r3 = bf16[4,192,128]{2,1,0:T(8,128)(2,1)S(1)} collective-permute-done((bf16[4,192,128]{2,1,0:T(8,128)(2,1)S(1)}, bf16[4,192,128]{2,1,0:T(8,128)(2,1)S(1)}, u32[]{:S(2)}, u32[]{:S(2)}) %collective-permute-start.2) | collective-permute-done | bytes 196640 | tf_op jit(solution)/shard_map/ppermute | solution.py:41
  17.3 3.1 %collective-permute-start.6 = (bf16[10,192,128]{2,1,0:T(8,128)(2,1)S(1)}, bf16[10,192,128]{2,1,0:T(8,128)(2,1)S(1)}, u32[]{:S(2)}, u32[]{:S(2)}) collective-permute-start(bf16[10,192,128]{2,1,0:T(8,128)(2,1)S(1)} %get-tuple-element.57), channel_id=1, source_target_pairs={{0,3},{1,0},{2,1},{3,2},{4,7},{5,4},{6,5},{7,6},{8,11},{9,8},{10,9... | collective-permute-start | bytes 1474568 | tf_op jit(solution)/shard_map/ppermute | solution.py:41
  20.5 3.8 %collective-permute-start.4 = (bf16[2,2,384,128]{3,2,1,0:T(8,128)(2,1)S(1)}, bf16[2,2,384,128]{3,2,1,0:T(8,128)(2,1)S(1)}, u32[]{:S(2)}, u32[]{:S(2)}) collective-permute-start(bf16[2,2,384,128]{3,2,1,0:T(8,128)(2,1)S(1)} %get-tuple-element.53), channel_id=1, source_target_pairs={{0,8},{4,12},{8,16},{12,20},{16,24},{20,28},{24,32},{28,36},{32,40... | collective-permute-start | bytes 1179656 | tf_op jit(solution)/shard_map/ppermute | solution.py:47
  24.3 1.9 %collective-permute-start.3 = (bf16[2,2,768,128]{3,2,1,0:T(8,128)(2,1)S(1)}, bf16[2,2,768,128]{3,2,1,0:T(8,128)(2,1)S(1)}, u32[]{:S(2)}, u32[]{:S(2)}) collective-permute-start(bf16[2,2,768,128]{3,2,1,0:T(8,128)(2,1)S(1)} %get-tuple-element.52.own_), channel_id=1, source_target_pairs={{0,4},{4,8},{8,12},{12,16},{16,20},{20,24},{24,28},{28,32},{32,36}... | collective-permute-start | bytes 2359304 | tf_op jit(solution)/shard_map/ppermute | solution.py:47
  26.2 6.0 %collective-permute-done.7.r3 = bf16[10,192,128]{2,1,0:T(8,128)(2,1)S(1)} collective-permute-done((bf16[10,192,128]{2,1,0:T(8,128)(2,1)S(1)}, bf16[10,192,128]{2,1,0:T(8,128)(2,1)S(1)}, u32[]{:S(2)}, u32[]{:S(2)}) %collective-permute-start.7) | collective-permute-done | bytes 491552 | tf_op jit(solution)/shard_map/ppermute | solution.py:41
  32.2 7.0 %collective-permute-done.6.r2 = bf16[10,192,128]{2,1,0:T(8,128)(2,1)S(1)} collective-permute-done((bf16[10,192,128]{2,1,0:T(8,128)(2,1)S(1)}, bf16[10,192,128]{2,1,0:T(8,128)(2,1)S(1)}, u32[]{:S(2)}, u32[]{:S(2)}) %collective-permute-start.6) | collective-permute-done | bytes 491552 | tf_op jit(solution)/shard_map/ppermute | solution.py:41
  40.8 3.4 %collective-permute-done.3.near_ = bf16[2,2,768,128]{3,2,1,0:T(8,128)(2,1)S(1)} collective-permute-done((bf16[2,2,768,128]{3,2,1,0:T(8,128)(2,1)S(1)}, bf16[2,2,768,128]{3,2,1,0:T(8,128)(2,1)S(1)}, u32[]{:S(2)}, u32[]{:S(2)}) %collective-permute-start.3) | collective-permute-done | bytes 786464 | tf_op jit(solution)/shard_map/ppermute | solution.py:47
  44.3 1.9 %collective-permute-start.10 = (bf16[3,2,768,128]{3,2,1,0:T(8,128)(2,1)S(1)}, bf16[3,2,768,128]{3,2,1,0:T(8,128)(2,1)S(1)}, u32[]{:S(2)}, u32[]{:S(2)}) collective-permute-start(bf16[3,2,768,128]{3,2,1,0:T(8,128)(2,1)S(1)} %get-tuple-element.66.own_), channel_id=1, source_target_pairs={{0,4},{4,8},{8,12},{12,16},{16,20},{20,24},{24,28},{28,32},{32,36}... | collective-permute-start | bytes 3538952 | tf_op jit(solution)/shard_map/ppermute | solution.py:47
  46.4 1.9 %collective-permute-start.11 = (bf16[3,2,384,128]{3,2,1,0:T(8,128)(2,1)S(1)}, bf16[3,2,384,128]{3,2,1,0:T(8,128)(2,1)S(1)}, u32[]{:S(2)}, u32[]{:S(2)}) collective-permute-start(bf16[3,2,384,128]{3,2,1,0:T(8,128)(2,1)S(1)} %get-tuple-element.67), channel_id=1, source_target_pairs={{0,8},{4,12},{8,16},{12,20},{16,24},{20,28},{24,32},{28,36},{32,40... | collective-permute-start | bytes 1769480 | tf_op jit(solution)/shard_map/ppermute | solution.py:47
  48.7 2.9 %collective-permute-start.13 = (bf16[6,192,128]{2,1,0:T(8,128)(2,1)S(1)}, bf16[6,192,128]{2,1,0:T(8,128)(2,1)S(1)}, u32[]{:S(2)}, u32[]{:S(2)}) collective-permute-start(bf16[6,192,128]{2,1,0:T(8,128)(2,1)S(1)} %get-tuple-element.72), channel_id=1, source_target_pairs={{0,3},{1,0},{2,1},{3,2},{4,7},{5,4},{6,5},{7,6},{8,11},{9,8},{10,9... | collective-permute-start | bytes 884744 | tf_op jit(solution)/shard_map/ppermute | solution.py:41
  52.8 9.7 %attend.2 = (bf16[2,768,128]{2,1,0:T(8,128)(2,1)S(1)}, bf16[2,2,768,128]{3,2,1,0:T(8,128)(2,1)S(1)}, bf16[2,2,384,128]{3,2,1,0:T(8,128)(2,1)S(1)}, f32[2,2,768,128]{3,2,1,0:T(8,128)S(1)}) custom-call(s32[2,3]{1,0:T(2,128)S(1)} %copy-done.4, bf16[2,2,768,128]{3,2,1,0:T(8,128)(2,1)S(1)} %collective-permute-done.3.near_, ...), custom_call_target="tpu_custom_call" | custom-call | flops 11000000512 | bytes 6000000 | tf_op jit(solution)/shard_map/attend/pallas_call | solution.py:225
  62.5 6.0 %collective-permute-start.9 = (bf16[2,2,384,128]{3,2,1,0:T(8,128)(2,1)S(1)}, bf16[2,2,384,128]{3,2,1,0:T(8,128)(2,1)S(1)}, u32[]{:S(2)}, u32[]{:S(2)}) collective-permute-start(bf16[2,2,384,128]{3,2,1,0:T(8,128)(2,1)S(1)} %get-tuple-element.63), channel_id=1, source_target_pairs={{8,0},{12,4},{16,8},{20,12},{24,16},{28,20},{32,24},{36,28},{40,32... | collective-permute-start | bytes 1179656 | tf_op jit(solution)/shard_map/ppermute | solution.py:47
  68.6 2.5 %collective-permute-start.8 = (bf16[2,2,768,128]{3,2,1,0:T(8,128)(2,1)S(1)}, bf16[2,2,768,128]{3,2,1,0:T(8,128)(2,1)S(1)}, u32[]{:S(2)}, u32[]{:S(2)}) collective-permute-start(bf16[2,2,768,128]{3,2,1,0:T(8,128)(2,1)S(1)} %get-tuple-element.62), channel_id=1, source_target_pairs={{4,0},{8,4},{12,8},{16,12},{20,16},{24,20},{28,24},{32,28},{36,32}... | collective-permute-start | bytes 2359304 | tf_op jit(solution)/shard_map/ppermute | solution.py:47
  71.2 14.4 %attend.3 = (bf16[3,768,128]{2,1,0:T(8,128)(2,1)S(1)}, bf16[3,2,768,128]{3,2,1,0:T(8,128)(2,1)S(1)}, bf16[3,2,384,128]{3,2,1,0:T(8,128)(2,1)S(1)}, f32[3,2,768,128]{3,2,1,0:T(8,128)S(1)}) custom-call(s32[2,3]{1,0:T(2,128)S(1)} %copy-done.4, bf16[3,2,768,128]{3,2,1,0:T(8,128)(2,1)S(1)} %collective-permute-done.10.near_, ...), custom_call_target="tpu_custom_call" | custom-call | flops 16499999744 | bytes 9000000 | tf_op jit(solution)/shard_map/attend/pallas_call | solution.py:225
  85.6 7.6 %collective-permute-start.18 = (bf16[3,2,768,128]{3,2,1,0:T(8,128)(2,1)S(1)}, bf16[3,2,768,128]{3,2,1,0:T(8,128)(2,1)S(1)}, u32[]{:S(2)}, u32[]{:S(2)}) collective-permute-start(bf16[3,2,768,128]{3,2,1,0:T(8,128)(2,1)S(1)} %get-tuple-element.87), channel_id=1, source_target_pairs={{4,0},{8,4},{12,8},{16,12},{20,16},{24,20},{28,24},{32,28},{36,32}... | collective-permute-start | bytes 3538952 | tf_op jit(solution)/shard_map/ppermute | solution.py:47
  93.2 2.9 %collective-permute-start.19 = (bf16[3,2,384,128]{3,2,1,0:T(8,128)(2,1)S(1)}, bf16[3,2,384,128]{3,2,1,0:T(8,128)(2,1)S(1)}, u32[]{:S(2)}, u32[]{:S(2)}) collective-permute-start(bf16[3,2,384,128]{3,2,1,0:T(8,128)(2,1)S(1)} %get-tuple-element.88), channel_id=1, source_target_pairs={{8,0},{12,4},{16,8},{20,12},{24,16},{28,20},{32,24},{36,28},{40,32... | collective-permute-start | bytes 1769480 | tf_op jit(solution)/shard_map/ppermute | solution.py:47
  96.9 2.9 %collective-permute-start.16 = (bf16[9,192,128]{2,1,0:T(8,128)(2,1)S(1)}, bf16[9,192,128]{2,1,0:T(8,128)(2,1)S(1)}, u32[]{:S(2)}, u32[]{:S(2)}) collective-permute-start(bf16[9,192,128]{2,1,0:T(8,128)(2,1)S(1)} %get-tuple-element.84), channel_id=1, source_target_pairs={{0,3},{1,0},{2,1},{3,2},{4,7},{5,4},{6,5},{7,6},{8,11},{9,8},{10,9... | collective-permute-start | bytes 1327112 | tf_op jit(solution)/shard_map/ppermute | solution.py:41
  100.1 21.0 %collective-permute-done.19.refs_2_ = bf16[3,2,384,128]{3,2,1,0:T(8,128)(2,1)S(1)} collective-permute-done((bf16[3,2,384,128]{3,2,1,0:T(8,128)(2,1)S(1)}, bf16[3,2,384,128]{3,2,1,0:T(8,128)(2,1)S(1)}, u32[]{:S(2)}, u32[]{:S(2)}) %collective-permute-start.19) | collective-permute-done | bytes 589856 | tf_op jit(solution)/shard_map/ppermute | solution.py:47
  122.0 2.9 %collective-permute-start.21 = (bf16[6,192,128]{2,1,0:T(8,128)(2,1)S(1)}, bf16[6,192,128]{2,1,0:T(8,128)(2,1)S(1)}, u32[]{:S(2)}, u32[]{:S(2)}) collective-permute-start(bf16[6,192,128]{2,1,0:T(8,128)(2,1)S(1)} %get-tuple-element.91), channel_id=1, source_target_pairs={{0,3},{1,0},{2,1},{3,2},{4,7},{5,4},{6,5},{7,6},{8,11},{9,8},{10,9... | collective-permute-start | bytes 884744 | tf_op jit(solution)/shard_map/ppermute | solution.py:41
  127.3 2.6 %collective-permute-done.20.refs_5_ = bf16[6,192,128]{2,1,0:T(8,128)(2,1)S(1)} collective-permute-done((bf16[6,192,128]{2,1,0:T(8,128)(2,1)S(1)}, bf16[6,192,128]{2,1,0:T(8,128)(2,1)S(1)}, u32[]{:S(2)}, u32[]{:S(2)}) %collective-permute-start.20) | collective-permute-done | bytes 294944 | tf_op jit(solution)/shard_map/ppermute | solution.py:41
  129.9 2.4 %collective-permute-done.21.refs_6_ = bf16[6,192,128]{2,1,0:T(8,128)(2,1)S(1)} collective-permute-done((bf16[6,192,128]{2,1,0:T(8,128)(2,1)S(1)}, bf16[6,192,128]{2,1,0:T(8,128)(2,1)S(1)}, u32[]{:S(2)}, u32[]{:S(2)}) %collective-permute-start.21) | collective-permute-done | bytes 294944 | tf_op jit(solution)/shard_map/ppermute | solution.py:41
  (43 shorter events, 17.9 us)
Async XLA Ops:
  3.1 8.0 %collective-permute-start = (bf16[4,192,128]{2,1,0:T(8,128)(2,1)S(1)}, bf16[4,192,128]{2,1,0:T(8,128)(2,1)S(1)}, u32[]{:S(2)}, u32[]{:S(2)}) collective-permute-start(bf16[4,192,128]{2,1,0:T(8,128)(2,1)S(1)} %get-tuple-element.49), channel_id=1, source_target_pairs={{0,1},{1,2},{2,3},{3,0},{4,5},{5,6},{6,7},{7,4},{8,9},{9,10},{10,1... | collective-permute-start | bytes 589832 | tf_op jit(solution)/shard_map/ppermute | solution.py:41
  4.8 9.9 %collective-permute-start.1 = (bf16[4,192,128]{2,1,0:T(8,128)(2,1)S(1)}, bf16[4,192,128]{2,1,0:T(8,128)(2,1)S(1)}, u32[]{:S(2)}, u32[]{:S(2)}) collective-permute-start(bf16[4,192,128]{2,1,0:T(8,128)(2,1)S(1)} %get-tuple-element.50), channel_id=1, source_target_pairs={{0,3},{1,0},{2,1},{3,2},{4,7},{5,4},{6,5},{7,6},{8,11},{9,8},{10,9... | collective-permute-start | bytes 589832 | tf_op jit(solution)/shard_map/ppermute | solution.py:41
  6.5 10.1 %collective-permute-start.2 = (bf16[4,192,128]{2,1,0:T(8,128)(2,1)S(1)}, bf16[4,192,128]{2,1,0:T(8,128)(2,1)S(1)}, u32[]{:S(2)}, u32[]{:S(2)}) collective-permute-start(bf16[4,192,128]{2,1,0:T(8,128)(2,1)S(1)} %get-tuple-element.51), channel_id=1, source_target_pairs={{0,2},{1,3},{2,0},{3,1},{4,6},{5,7},{6,4},{7,5},{8,10},{9,11},{10,... | collective-permute-start | bytes 589832 | tf_op jit(solution)/shard_map/ppermute | solution.py:41
  16.5 15.7 %collective-permute-start.7 = (bf16[10,192,128]{2,1,0:T(8,128)(2,1)S(1)}, bf16[10,192,128]{2,1,0:T(8,128)(2,1)S(1)}, u32[]{:S(2)}, u32[]{:S(2)}) collective-permute-start(bf16[10,192,128]{2,1,0:T(8,128)(2,1)S(1)} %get-tuple-element.59), channel_id=1, source_target_pairs={{0,2},{1,3},{2,0},{3,1},{4,6},{5,7},{6,4},{7,5},{8,10},{9,11},{10,... | collective-permute-start | bytes 1474568 | tf_op jit(solution)/shard_map/ppermute | solution.py:41
  17.3 22.0 %collective-permute-start.6 = (bf16[10,192,128]{2,1,0:T(8,128)(2,1)S(1)}, bf16[10,192,128]{2,1,0:T(8,128)(2,1)S(1)}, u32[]{:S(2)}, u32[]{:S(2)}) collective-permute-start(bf16[10,192,128]{2,1,0:T(8,128)(2,1)S(1)} %get-tuple-element.57), channel_id=1, source_target_pairs={{0,3},{1,0},{2,1},{3,2},{4,7},{5,4},{6,5},{7,6},{8,11},{9,8},{10,9... | collective-permute-start | bytes 1474568 | tf_op jit(solution)/shard_map/ppermute | solution.py:41
  20.3 20.3 %collective-permute-start.5 = (bf16[10,192,128]{2,1,0:T(8,128)(2,1)S(1)}, bf16[10,192,128]{2,1,0:T(8,128)(2,1)S(1)}, u32[]{:S(2)}, u32[]{:S(2)}) collective-permute-start(bf16[10,192,128]{2,1,0:T(8,128)(2,1)S(1)} %get-tuple-element.55), channel_id=1, source_target_pairs={{0,1},{1,2},{2,3},{3,0},{4,5},{5,6},{6,7},{7,4},{8,9},{9,10},{10,1... | collective-permute-start | bytes 1474568 | tf_op jit(solution)/shard_map/ppermute | solution.py:41
  20.5 20.4 %collective-permute-start.4 = (bf16[2,2,384,128]{3,2,1,0:T(8,128)(2,1)S(1)}, bf16[2,2,384,128]{3,2,1,0:T(8,128)(2,1)S(1)}, u32[]{:S(2)}, u32[]{:S(2)}) collective-permute-start(bf16[2,2,384,128]{3,2,1,0:T(8,128)(2,1)S(1)} %get-tuple-element.53), channel_id=1, source_target_pairs={{0,8},{4,12},{8,16},{12,20},{16,24},{20,28},{24,32},{28,36},{32,40... | collective-permute-start | bytes 1179656 | tf_op jit(solution)/shard_map/ppermute | solution.py:47
  24.3 20.0 %collective-permute-start.3 = (bf16[2,2,768,128]{3,2,1,0:T(8,128)(2,1)S(1)}, bf16[2,2,768,128]{3,2,1,0:T(8,128)(2,1)S(1)}, u32[]{:S(2)}, u32[]{:S(2)}) collective-permute-start(bf16[2,2,768,128]{3,2,1,0:T(8,128)(2,1)S(1)} %get-tuple-element.52.own_), channel_id=1, source_target_pairs={{0,4},{4,8},{8,12},{12,16},{16,20},{20,24},{24,28},{28,32},{32,36}... | collective-permute-start | bytes 2359304 | tf_op jit(solution)/shard_map/ppermute | solution.py:47
  40.8 12.0 %copy-start.4 = (s32[2,3]{1,0:T(2,128)S(1)}, s32[2,3]{1,0:T(2,128)}, u32[]{:S(2)}) copy-start(s32[2,3]{1,0:T(2,128)} %win.3) | copy-start | bytes 76
  44.3 26.9 %collective-permute-start.10 = (bf16[3,2,768,128]{3,2,1,0:T(8,128)(2,1)S(1)}, bf16[3,2,768,128]{3,2,1,0:T(8,128)(2,1)S(1)}, u32[]{:S(2)}, u32[]{:S(2)}) collective-permute-start(bf16[3,2,768,128]{3,2,1,0:T(8,128)(2,1)S(1)} %get-tuple-element.66.own_), channel_id=1, source_target_pairs={{0,4},{4,8},{8,12},{12,16},{16,20},{20,24},{24,28},{28,32},{32,36}... | collective-permute-start | bytes 3538952 | tf_op jit(solution)/shard_map/ppermute | solution.py:47
  46.4 24.8 %collective-permute-start.11 = (bf16[3,2,384,128]{3,2,1,0:T(8,128)(2,1)S(1)}, bf16[3,2,384,128]{3,2,1,0:T(8,128)(2,1)S(1)}, u32[]{:S(2)}, u32[]{:S(2)}) collective-permute-start(bf16[3,2,384,128]{3,2,1,0:T(8,128)(2,1)S(1)} %get-tuple-element.67), channel_id=1, source_target_pairs={{0,8},{4,12},{8,16},{12,20},{16,24},{20,28},{24,32},{28,36},{32,40... | collective-permute-start | bytes 1769480 | tf_op jit(solution)/shard_map/ppermute | solution.py:47
  48.3 14.2 %collective-permute-start.12 = (bf16[6,192,128]{2,1,0:T(8,128)(2,1)S(1)}, bf16[6,192,128]{2,1,0:T(8,128)(2,1)S(1)}, u32[]{:S(2)}, u32[]{:S(2)}) collective-permute-start(bf16[6,192,128]{2,1,0:T(8,128)(2,1)S(1)} %get-tuple-element.71), channel_id=1, source_target_pairs={{0,1},{1,2},{2,3},{3,0},{4,5},{5,6},{6,7},{7,4},{8,9},{9,10},{10,1... | collective-permute-start | bytes 884744 | tf_op jit(solution)/shard_map/ppermute | solution.py:41
  48.7 19.8 %collective-permute-start.13 = (bf16[6,192,128]{2,1,0:T(8,128)(2,1)S(1)}, bf16[6,192,128]{2,1,0:T(8,128)(2,1)S(1)}, u32[]{:S(2)}, u32[]{:S(2)}) collective-permute-start(bf16[6,192,128]{2,1,0:T(8,128)(2,1)S(1)} %get-tuple-element.72), channel_id=1, source_target_pairs={{0,3},{1,0},{2,1},{3,2},{4,7},{5,4},{6,5},{7,6},{8,11},{9,8},{10,9... | collective-permute-start | bytes 884744 | tf_op jit(solution)/shard_map/ppermute | solution.py:41
  51.6 19.5 %collective-permute-start.14 = (bf16[6,192,128]{2,1,0:T(8,128)(2,1)S(1)}, bf16[6,192,128]{2,1,0:T(8,128)(2,1)S(1)}, u32[]{:S(2)}, u32[]{:S(2)}) collective-permute-start(bf16[6,192,128]{2,1,0:T(8,128)(2,1)S(1)} %get-tuple-element.73), channel_id=1, source_target_pairs={{0,2},{1,3},{2,0},{3,1},{4,6},{5,7},{6,4},{7,5},{8,10},{9,11},{10,... | collective-permute-start | bytes 884744 | tf_op jit(solution)/shard_map/ppermute | solution.py:41
  62.5 23.1 %collective-permute-start.9 = (bf16[2,2,384,128]{3,2,1,0:T(8,128)(2,1)S(1)}, bf16[2,2,384,128]{3,2,1,0:T(8,128)(2,1)S(1)}, u32[]{:S(2)}, u32[]{:S(2)}) collective-permute-start(bf16[2,2,384,128]{3,2,1,0:T(8,128)(2,1)S(1)} %get-tuple-element.63), channel_id=1, source_target_pairs={{8,0},{12,4},{16,8},{20,12},{24,16},{28,20},{32,24},{36,28},{40,32... | collective-permute-start | bytes 1179656 | tf_op jit(solution)/shard_map/ppermute | solution.py:47
  68.6 17.0 %collective-permute-start.8 = (bf16[2,2,768,128]{3,2,1,0:T(8,128)(2,1)S(1)}, bf16[2,2,768,128]{3,2,1,0:T(8,128)(2,1)S(1)}, u32[]{:S(2)}, u32[]{:S(2)}) collective-permute-start(bf16[2,2,768,128]{3,2,1,0:T(8,128)(2,1)S(1)} %get-tuple-element.62), channel_id=1, source_target_pairs={{4,0},{8,4},{12,8},{16,12},{20,16},{24,20},{28,24},{32,28},{36,32}... | collective-permute-start | bytes 2359304 | tf_op jit(solution)/shard_map/ppermute | solution.py:47
  85.6 35.5 %collective-permute-start.18 = (bf16[3,2,768,128]{3,2,1,0:T(8,128)(2,1)S(1)}, bf16[3,2,768,128]{3,2,1,0:T(8,128)(2,1)S(1)}, u32[]{:S(2)}, u32[]{:S(2)}) collective-permute-start(bf16[3,2,768,128]{3,2,1,0:T(8,128)(2,1)S(1)} %get-tuple-element.87), channel_id=1, source_target_pairs={{4,0},{8,4},{12,8},{16,12},{20,16},{24,20},{28,24},{32,28},{36,32}... | collective-permute-start | bytes 3538952 | tf_op jit(solution)/shard_map/ppermute | solution.py:47
  93.2 27.9 %collective-permute-start.19 = (bf16[3,2,384,128]{3,2,1,0:T(8,128)(2,1)S(1)}, bf16[3,2,384,128]{3,2,1,0:T(8,128)(2,1)S(1)}, u32[]{:S(2)}, u32[]{:S(2)}) collective-permute-start(bf16[3,2,384,128]{3,2,1,0:T(8,128)(2,1)S(1)} %get-tuple-element.88), channel_id=1, source_target_pairs={{8,0},{12,4},{16,8},{20,12},{24,16},{28,20},{32,24},{36,28},{40,32... | collective-permute-start | bytes 1769480 | tf_op jit(solution)/shard_map/ppermute | solution.py:47
  96.5 28.4 %collective-permute-start.15 = (bf16[9,192,128]{2,1,0:T(8,128)(2,1)S(1)}, bf16[9,192,128]{2,1,0:T(8,128)(2,1)S(1)}, u32[]{:S(2)}, u32[]{:S(2)}) collective-permute-start(bf16[9,192,128]{2,1,0:T(8,128)(2,1)S(1)} %get-tuple-element.83), channel_id=1, source_target_pairs={{0,1},{1,2},{2,3},{3,0},{4,5},{5,6},{6,7},{7,4},{8,9},{9,10},{10,1... | collective-permute-start | bytes 1327112 | tf_op jit(solution)/shard_map/ppermute | solution.py:41
  96.9 29.2 %collective-permute-start.16 = (bf16[9,192,128]{2,1,0:T(8,128)(2,1)S(1)}, bf16[9,192,128]{2,1,0:T(8,128)(2,1)S(1)}, u32[]{:S(2)}, u32[]{:S(2)}) collective-permute-start(bf16[9,192,128]{2,1,0:T(8,128)(2,1)S(1)} %get-tuple-element.84), channel_id=1, source_target_pairs={{0,3},{1,0},{2,1},{3,2},{4,7},{5,4},{6,5},{7,6},{8,11},{9,8},{10,9... | collective-permute-start | bytes 1327112 | tf_op jit(solution)/shard_map/ppermute | solution.py:41
  99.9 26.2 %collective-permute-start.17 = (bf16[9,192,128]{2,1,0:T(8,128)(2,1)S(1)}, bf16[9,192,128]{2,1,0:T(8,128)(2,1)S(1)}, u32[]{:S(2)}, u32[]{:S(2)}) collective-permute-start(bf16[9,192,128]{2,1,0:T(8,128)(2,1)S(1)} %get-tuple-element.85), channel_id=1, source_target_pairs={{0,2},{1,3},{2,0},{3,1},{4,6},{5,7},{6,4},{7,5},{8,10},{9,11},{10,... | collective-permute-start | bytes 1327112 | tf_op jit(solution)/shard_map/ppermute | solution.py:41
  121.6 8.3 %collective-permute-start.20 = (bf16[6,192,128]{2,1,0:T(8,128)(2,1)S(1)}, bf16[6,192,128]{2,1,0:T(8,128)(2,1)S(1)}, u32[]{:S(2)}, u32[]{:S(2)}) collective-permute-start(bf16[6,192,128]{2,1,0:T(8,128)(2,1)S(1)} %get-tuple-element.90), channel_id=1, source_target_pairs={{0,1},{1,2},{2,3},{3,0},{4,5},{5,6},{6,7},{7,4},{8,9},{9,10},{10,1... | collective-permute-start | bytes 884744 | tf_op jit(solution)/shard_map/ppermute | solution.py:41
  122.0 10.4 %collective-permute-start.21 = (bf16[6,192,128]{2,1,0:T(8,128)(2,1)S(1)}, bf16[6,192,128]{2,1,0:T(8,128)(2,1)S(1)}, u32[]{:S(2)}, u32[]{:S(2)}) collective-permute-start(bf16[6,192,128]{2,1,0:T(8,128)(2,1)S(1)} %get-tuple-element.91), channel_id=1, source_target_pairs={{0,3},{1,0},{2,1},{3,2},{4,7},{5,4},{6,5},{7,6},{8,11},{9,8},{10,9... | collective-permute-start | bytes 884744 | tf_op jit(solution)/shard_map/ppermute | solution.py:41
  124.9 9.0 %collective-permute-start.22 = (bf16[6,192,128]{2,1,0:T(8,128)(2,1)S(1)}, bf16[6,192,128]{2,1,0:T(8,128)(2,1)S(1)}, u32[]{:S(2)}, u32[]{:S(2)}) collective-permute-start(bf16[6,192,128]{2,1,0:T(8,128)(2,1)S(1)} %get-tuple-element.92), channel_id=1, source_target_pairs={{0,2},{1,3},{2,0},{3,1},{4,6},{5,7},{6,4},{7,5},{8,10},{9,11},{10,... | collective-permute-start | bytes 884744 | tf_op jit(solution)/shard_map/ppermute | solution.py:41
  (4 other events, 13.2 us)

commit v5 on v4

--- a/solution.py
+++ b/solution.py
@@ -134,7 +134,7 @@
 
 def attend_kernel(
     heads, base, win, near_, far_, own_, queries, upstream, r1, r2, r3,
-    dq_, nearg_, farg_, owng_, q_ref, g_ref, s_ref, d_ref,
+    dq_, nearg_, farg_, owng_, q_two, g_two, s_two, d_two,
 ):
     me = lax.axis_index("head")
 
@@ -162,7 +162,8 @@
         mid = op(op(x[1], x[2]), x[3])
         return jnp.concatenate([op(mid[:, :GR], x[0]), op(mid[:, GR:], x[4])], axis=1)
 
-    def head(n, carry):
+    def head(n):
+        q_ref, g_ref, s_ref, d_ref = [x.at[n % 2] for x in (q_two, g_two, s_two, d_two)]
         near, far, own = near_.at[n], far_.at[n], own_.at[n]
         nearg, farg, owng = nearg_.at[n], farg_.at[n], owng_.at[n]
         q_ref[piece_rows(me), :] = queries[:, columns(me, heads[0] + n)]
@@ -211,12 +212,9 @@
         for i in range(2):
             factor = inverse[:, rows_of(i)] * SCALE
             dq_[n, rows_of(i), :] = (dq[i] * factor).T.astype(BF)
-        return carry
-
-    if len(heads) == 1:
-        head(0, 0)
-    else:
-        lax.fori_loop(0, len(heads), head, 0)
+
+    for n in range(len(heads)):
+        head(n)
 
 
 def attend(window, near, far, own, queries, upstream, r, heads, base):
@@ -233,10 +231,10 @@
             sd((n, 2, 2 * GR, HD), F32),
         ],
         scratch_shapes=[
-            pltpu.VMEM((2 * GR, HD), BF),
-            pltpu.VMEM((2 * GR, HD), BF),
-            pltpu.VMEM((5 * GR, 2 * GR), F32),
-            pltpu.VMEM((5 * GR, 2 * GR), F32),
+            pltpu.VMEM((2, 2 * GR, HD), BF),
+            pltpu.VMEM((2, 2 * GR, HD), BF),
+            pltpu.VMEM((2, 5 * GR, 2 * GR), F32),
+            pltpu.VMEM((2, 5 * GR, 2 * GR), F32),
         ],
         compiler_params=pltpu.CompilerParams(vmem_limit_bytes=32 << 20),
         cost_estimate=cost(n * 5.5e9, n * 3e6),

time: 136 us -> 136 us (level)
  transfers between devices with their start and end apart: 23 -> 23, of which waited for: 11 -> 11; matrix products, arithmetic and copies ran while one was open for 0% -> 0% of each run, Pallas kernels for 20% -> 19%
where the time goes in v5:
time: 136 us; the launch traced here: 135 us
  waiting for transfers between devices  53.4 us (39%)
  starting transfers between devices  50.7 us (37%)
  Pallas kernels  28 us (21%)
  local copies, waits for them, and re-layouts  2.41 us (2%)
    ppermute x8, starting transfers between devices, tm_shift(): return lax.ppermute(block, 'tm', route)  29 us
    ppermute x15, waiting for transfers between devices, head_shift(): lax.ppermute(block, 'head', [(i, (i + distance) % n) for i in range(n)])  28.9 us
    ppermute x8, waiting for transfers between devices, tm_shift(): return lax.ppermute(block, 'tm', route)  24.5 us
    pallas_call x2, Pallas kernels, attend(): pl.pallas_call(functools.partial(attend_kernel, heads, base), in_specs=[p...  23.4 us
    ppermute x15, starting transfers between devices, head_shift(): lax.ppermute(block, 'head', [(i, (i + distance) % n) for i in range(n)])  21.7 us
    pallas_call x2, Pallas kernels, place(): pl.pallas_call(functools.partial(place_kernel, names), in_specs=[VM] * n,...  2.99 us
  transfers between devices with their start and end apart: 23, of which 11 were waited for; matrix products, arithmetic and copies ran while one was open for 0% of the time, Pallas kernels for 19%

profile of v5, /device:TPU:6, one launch (start us, length us, event | category | flops | bytes accessed | tf_op | source)
XLA Modules:
  0.0 135.3 jit_solution(12853497253378600940)
XLA Ops:
  6.5 2.0 %collective-permute-start.2 = (bf16[4,192,128]{2,1,0:T(8,128)(2,1)S(1)}, bf16[4,192,128]{2,1,0:T(8,128)(2,1)S(1)}, u32[]{:S(2)}, u32[]{:S(2)}) collective-permute-start(bf16[4,192,128]{2,1,0:T(8,128)(2,1)S(1)} %get-tuple-element.51), channel_id=1, source_target_pairs={{0,2},{1,3},{2,0},{3,1},{4,6},{5,7},{6,4},{7,5},{8,10},{9,11},{10,... | collective-permute-start | bytes 589832 | tf_op jit(solution)/shard_map/ppermute | solution.py:41
  8.7 2.4 %collective-permute-done.r1 = bf16[4,192,128]{2,1,0:T(8,128)(2,1)S(1)} collective-permute-done((bf16[4,192,128]{2,1,0:T(8,128)(2,1)S(1)}, bf16[4,192,128]{2,1,0:T(8,128)(2,1)S(1)}, u32[]{:S(2)}, u32[]{:S(2)}) %collective-permute-start) | collective-permute-done | bytes 196640 | tf_op jit(solution)/shard_map/ppermute | solution.py:41
  11.1 3.6 %collective-permute-done.1.r2 = bf16[4,192,128]{2,1,0:T(8,128)(2,1)S(1)} collective-permute-done((bf16[4,192,128]{2,1,0:T(8,128)(2,1)S(1)}, bf16[4,192,128]{2,1,0:T(8,128)(2,1)S(1)}, u32[]{:S(2)}, u32[]{:S(2)}) %collective-permute-start.1) | collective-permute-done | bytes 196640 | tf_op jit(solution)/shard_map/ppermute | solution.py:41
  14.7 1.8 %collective-permute-done.2.r3 = bf16[4,192,128]{2,1,0:T(8,128)(2,1)S(1)} collective-permute-done((bf16[4,192,128]{2,1,0:T(8,128)(2,1)S(1)}, bf16[4,192,128]{2,1,0:T(8,128)(2,1)S(1)}, u32[]{:S(2)}, u32[]{:S(2)}) %collective-permute-start.2) | collective-permute-done | bytes 196640 | tf_op jit(solution)/shard_map/ppermute | solution.py:41
  17.3 3.1 %collective-permute-start.6 = (bf16[10,192,128]{2,1,0:T(8,128)(2,1)S(1)}, bf16[10,192,128]{2,1,0:T(8,128)(2,1)S(1)}, u32[]{:S(2)}, u32[]{:S(2)}) collective-permute-start(bf16[10,192,128]{2,1,0:T(8,128)(2,1)S(1)} %get-tuple-element.57), channel_id=1, source_target_pairs={{0,3},{1,0},{2,1},{3,2},{4,7},{5,4},{6,5},{7,6},{8,11},{9,8},{10,9... | collective-permute-start | bytes 1474568 | tf_op jit(solution)/shard_map/ppermute | solution.py:41
  20.5 3.8 %collective-permute-start.4 = (bf16[2,2,384,128]{3,2,1,0:T(8,128)(2,1)S(1)}, bf16[2,2,384,128]{3,2,1,0:T(8,128)(2,1)S(1)}, u32[]{:S(2)}, u32[]{:S(2)}) collective-permute-start(bf16[2,2,384,128]{3,2,1,0:T(8,128)(2,1)S(1)} %get-tuple-element.53), channel_id=1, source_target_pairs={{0,8},{4,12},{8,16},{12,20},{16,24},{20,28},{24,32},{28,36},{32,40... | collective-permute-start | bytes 1179656 | tf_op jit(solution)/shard_map/ppermute | solution.py:47
  24.3 1.9 %collective-permute-start.3 = (bf16[2,2,768,128]{3,2,1,0:T(8,128)(2,1)S(1)}, bf16[2,2,768,128]{3,2,1,0:T(8,128)(2,1)S(1)}, u32[]{:S(2)}, u32[]{:S(2)}) collective-permute-start(bf16[2,2,768,128]{3,2,1,0:T(8,128)(2,1)S(1)} %get-tuple-element.52.own_), channel_id=1, source_target_pairs={{0,4},{4,8},{8,12},{12,16},{16,20},{20,24},{24,28},{28,32},{32,36}... | collective-permute-start | bytes 2359304 | tf_op jit(solution)/shard_map/ppermute | solution.py:47
  26.2 6.0 %collective-permute-done.7.r3 = bf16[10,192,128]{2,1,0:T(8,128)(2,1)S(1)} collective-permute-done((bf16[10,192,128]{2,1,0:T(8,128)(2,1)S(1)}, bf16[10,192,128]{2,1,0:T(8,128)(2,1)S(1)}, u32[]{:S(2)}, u32[]{:S(2)}) %collective-permute-start.7) | collective-permute-done | bytes 491552 | tf_op jit(solution)/shard_map/ppermute | solution.py:41
  32.2 7.0 %collective-permute-done.6.r2 = bf16[10,192,128]{2,1,0:T(8,128)(2,1)S(1)} collective-permute-done((bf16[10,192,128]{2,1,0:T(8,128)(2,1)S(1)}, bf16[10,192,128]{2,1,0:T(8,128)(2,1)S(1)}, u32[]{:S(2)}, u32[]{:S(2)}) %collective-permute-start.6) | collective-permute-done | bytes 491552 | tf_op jit(solution)/shard_map/ppermute | solution.py:41
  40.8 3.4 %collective-permute-done.3.near_ = bf16[2,2,768,128]{3,2,1,0:T(8,128)(2,1)S(1)} collective-permute-done((bf16[2,2,768,128]{3,2,1,0:T(8,128)(2,1)S(1)}, bf16[2,2,768,128]{3,2,1,0:T(8,128)(2,1)S(1)}, u32[]{:S(2)}, u32[]{:S(2)}) %collective-permute-start.3) | collective-permute-done | bytes 786464 | tf_op jit(solution)/shard_map/ppermute | solution.py:47
  44.3 1.9 %collective-permute-start.10 = (bf16[3,2,768,128]{3,2,1,0:T(8,128)(2,1)S(1)}, bf16[3,2,768,128]{3,2,1,0:T(8,128)(2,1)S(1)}, u32[]{:S(2)}, u32[]{:S(2)}) collective-permute-start(bf16[3,2,768,128]{3,2,1,0:T(8,128)(2,1)S(1)} %get-tuple-element.66.own_), channel_id=1, source_target_pairs={{0,4},{4,8},{8,12},{12,16},{16,20},{20,24},{24,28},{28,32},{32,36}... | collective-permute-start | bytes 3538952 | tf_op jit(solution)/shard_map/ppermute | solution.py:47
  46.4 1.9 %collective-permute-start.11 = (bf16[3,2,384,128]{3,2,1,0:T(8,128)(2,1)S(1)}, bf16[3,2,384,128]{3,2,1,0:T(8,128)(2,1)S(1)}, u32[]{:S(2)}, u32[]{:S(2)}) collective-permute-start(bf16[3,2,384,128]{3,2,1,0:T(8,128)(2,1)S(1)} %get-tuple-element.67), channel_id=1, source_target_pairs={{0,8},{4,12},{8,16},{12,20},{16,24},{20,28},{24,32},{28,36},{32,40... | collective-permute-start | bytes 1769480 | tf_op jit(solution)/shard_map/ppermute | solution.py:47
  48.7 2.9 %collective-permute-start.13 = (bf16[6,192,128]{2,1,0:T(8,128)(2,1)S(1)}, bf16[6,192,128]{2,1,0:T(8,128)(2,1)S(1)}, u32[]{:S(2)}, u32[]{:S(2)}) collective-permute-start(bf16[6,192,128]{2,1,0:T(8,128)(2,1)S(1)} %get-tuple-element.72), channel_id=1, source_target_pairs={{0,3},{1,0},{2,1},{3,2},{4,7},{5,4},{6,5},{7,6},{8,11},{9,8},{10,9... | collective-permute-start | bytes 884744 | tf_op jit(solution)/shard_map/ppermute | solution.py:41
  52.8 9.4 %attend.2 = (bf16[2,768,128]{2,1,0:T(8,128)(2,1)S(1)}, bf16[2,2,768,128]{3,2,1,0:T(8,128)(2,1)S(1)}, bf16[2,2,384,128]{3,2,1,0:T(8,128)(2,1)S(1)}, f32[2,2,768,128]{3,2,1,0:T(8,128)S(1)}) custom-call(s32[2,3]{1,0:T(2,128)S(1)} %copy-done.4, bf16[2,2,768,128]{3,2,1,0:T(8,128)(2,1)S(1)} %collective-permute-done.3.near_, ...), custom_call_target="tpu_custom_call" | custom-call | flops 11000000512 | bytes 6000000 | tf_op jit(solution)/shard_map/attend/pallas_call | solution.py:223
  62.2 6.0 %collective-permute-start.9 = (bf16[2,2,384,128]{3,2,1,0:T(8,128)(2,1)S(1)}, bf16[2,2,384,128]{3,2,1,0:T(8,128)(2,1)S(1)}, u32[]{:S(2)}, u32[]{:S(2)}) collective-permute-start(bf16[2,2,384,128]{3,2,1,0:T(8,128)(2,1)S(1)} %get-tuple-element.63), channel_id=1, source_target_pairs={{8,0},{12,4},{16,8},{20,12},{24,16},{28,20},{32,24},{36,28},{40,32... | collective-permute-start | bytes 1179656 | tf_op jit(solution)/shard_map/ppermute | solution.py:47
  68.2 2.8 %collective-permute-start.8 = (bf16[2,2,768,128]{3,2,1,0:T(8,128)(2,1)S(1)}, bf16[2,2,768,128]{3,2,1,0:T(8,128)(2,1)S(1)}, u32[]{:S(2)}, u32[]{:S(2)}) collective-permute-start(bf16[2,2,768,128]{3,2,1,0:T(8,128)(2,1)S(1)} %get-tuple-element.62), channel_id=1, source_target_pairs={{4,0},{8,4},{12,8},{16,12},{20,16},{24,20},{28,24},{32,28},{36,32}... | collective-permute-start | bytes 2359304 | tf_op jit(solution)/shard_map/ppermute | solution.py:47
  71.0 14.0 %attend.3 = (bf16[3,768,128]{2,1,0:T(8,128)(2,1)S(1)}, bf16[3,2,768,128]{3,2,1,0:T(8,128)(2,1)S(1)}, bf16[3,2,384,128]{3,2,1,0:T(8,128)(2,1)S(1)}, f32[3,2,768,128]{3,2,1,0:T(8,128)S(1)}) custom-call(s32[2,3]{1,0:T(2,128)S(1)} %copy-done.4, bf16[3,2,768,128]{3,2,1,0:T(8,128)(2,1)S(1)} %collective-permute-done.10.near_, ...), custom_call_target="tpu_custom_call" | custom-call | flops 16499999744 | bytes 9000000 | tf_op jit(solution)/shard_map/attend/pallas_call | solution.py:223
  85.1 7.7 %collective-permute-start.18 = (bf16[3,2,768,128]{3,2,1,0:T(8,128)(2,1)S(1)}, bf16[3,2,768,128]{3,2,1,0:T(8,128)(2,1)S(1)}, u32[]{:S(2)}, u32[]{:S(2)}) collective-permute-start(bf16[3,2,768,128]{3,2,1,0:T(8,128)(2,1)S(1)} %get-tuple-element.87), channel_id=1, source_target_pairs={{4,0},{8,4},{12,8},{16,12},{20,16},{24,20},{28,24},{32,28},{36,32}... | collective-permute-start | bytes 3538952 | tf_op jit(solution)/shard_map/ppermute | solution.py:47
  92.8 2.9 %collective-permute-start.19 = (bf16[3,2,384,128]{3,2,1,0:T(8,128)(2,1)S(1)}, bf16[3,2,384,128]{3,2,1,0:T(8,128)(2,1)S(1)}, u32[]{:S(2)}, u32[]{:S(2)}) collective-permute-start(bf16[3,2,384,128]{3,2,1,0:T(8,128)(2,1)S(1)} %get-tuple-element.88), channel_id=1, source_target_pairs={{8,0},{12,4},{16,8},{20,12},{24,16},{28,20},{32,24},{36,28},{40,32... | collective-permute-start | bytes 1769480 | tf_op jit(solution)/shard_map/ppermute | solution.py:47
  96.5 2.9 %collective-permute-start.16 = (bf16[9,192,128]{2,1,0:T(8,128)(2,1)S(1)}, bf16[9,192,128]{2,1,0:T(8,128)(2,1)S(1)}, u32[]{:S(2)}, u32[]{:S(2)}) collective-permute-start(bf16[9,192,128]{2,1,0:T(8,128)(2,1)S(1)} %get-tuple-element.84), channel_id=1, source_target_pairs={{0,3},{1,0},{2,1},{3,2},{4,7},{5,4},{6,5},{7,6},{8,11},{9,8},{10,9... | collective-permute-start | bytes 1327112 | tf_op jit(solution)/shard_map/ppermute | solution.py:41
  99.7 21.0 %collective-permute-done.19.refs_2_ = bf16[3,2,384,128]{3,2,1,0:T(8,128)(2,1)S(1)} collective-permute-done((bf16[3,2,384,128]{3,2,1,0:T(8,128)(2,1)S(1)}, bf16[3,2,384,128]{3,2,1,0:T(8,128)(2,1)S(1)}, u32[]{:S(2)}, u32[]{:S(2)}) %collective-permute-start.19) | collective-permute-done | bytes 589856 | tf_op jit(solution)/shard_map/ppermute | solution.py:47
  121.6 2.9 %collective-permute-start.21 = (bf16[6,192,128]{2,1,0:T(8,128)(2,1)S(1)}, bf16[6,192,128]{2,1,0:T(8,128)(2,1)S(1)}, u32[]{:S(2)}, u32[]{:S(2)}) collective-permute-start(bf16[6,192,128]{2,1,0:T(8,128)(2,1)S(1)} %get-tuple-element.91), channel_id=1, source_target_pairs={{0,3},{1,0},{2,1},{3,2},{4,7},{5,4},{6,5},{7,6},{8,11},{9,8},{10,9... | collective-permute-start | bytes 884744 | tf_op jit(solution)/shard_map/ppermute | solution.py:41
  126.9 2.6 %collective-permute-done.20.refs_5_ = bf16[6,192,128]{2,1,0:T(8,128)(2,1)S(1)} collective-permute-done((bf16[6,192,128]{2,1,0:T(8,128)(2,1)S(1)}, bf16[6,192,128]{2,1,0:T(8,128)(2,1)S(1)}, u32[]{:S(2)}, u32[]{:S(2)}) %collective-permute-start.20) | collective-permute-done | bytes 294944 | tf_op jit(solution)/shard_map/ppermute | solution.py:41
  129.5 2.4 %collective-permute-done.21.refs_6_ = bf16[6,192,128]{2,1,0:T(8,128)(2,1)S(1)} collective-permute-done((bf16[6,192,128]{2,1,0:T(8,128)(2,1)S(1)}, bf16[6,192,128]{2,1,0:T(8,128)(2,1)S(1)}, u32[]{:S(2)}, u32[]{:S(2)}) %collective-permute-start.21) | collective-permute-done | bytes 294944 | tf_op jit(solution)/shard_map/ppermute | solution.py:41
  (43 shorter events, 17.9 us)
Async XLA Ops:
  3.1 8.0 %collective-permute-start = (bf16[4,192,128]{2,1,0:T(8,128)(2,1)S(1)}, bf16[4,192,128]{2,1,0:T(8,128)(2,1)S(1)}, u32[]{:S(2)}, u32[]{:S(2)}) collective-permute-start(bf16[4,192,128]{2,1,0:T(8,128)(2,1)S(1)} %get-tuple-element.49), channel_id=1, source_target_pairs={{0,1},{1,2},{2,3},{3,0},{4,5},{5,6},{6,7},{7,4},{8,9},{9,10},{10,1... | collective-permute-start | bytes 589832 | tf_op jit(solution)/shard_map/ppermute | solution.py:41
  4.8 9.9 %collective-permute-start.1 = (bf16[4,192,128]{2,1,0:T(8,128)(2,1)S(1)}, bf16[4,192,128]{2,1,0:T(8,128)(2,1)S(1)}, u32[]{:S(2)}, u32[]{:S(2)}) collective-permute-start(bf16[4,192,128]{2,1,0:T(8,128)(2,1)S(1)} %get-tuple-element.50), channel_id=1, source_target_pairs={{0,3},{1,0},{2,1},{3,2},{4,7},{5,4},{6,5},{7,6},{8,11},{9,8},{10,9... | collective-permute-start | bytes 589832 | tf_op jit(solution)/shard_map/ppermute | solution.py:41
  6.5 10.1 %collective-permute-start.2 = (bf16[4,192,128]{2,1,0:T(8,128)(2,1)S(1)}, bf16[4,192,128]{2,1,0:T(8,128)(2,1)S(1)}, u32[]{:S(2)}, u32[]{:S(2)}) collective-permute-start(bf16[4,192,128]{2,1,0:T(8,128)(2,1)S(1)} %get-tuple-element.51), channel_id=1, source_target_pairs={{0,2},{1,3},{2,0},{3,1},{4,6},{5,7},{6,4},{7,5},{8,10},{9,11},{10,... | collective-permute-start | bytes 589832 | tf_op jit(solution)/shard_map/ppermute | solution.py:41
  16.5 15.7 %collective-permute-start.7 = (bf16[10,192,128]{2,1,0:T(8,128)(2,1)S(1)}, bf16[10,192,128]{2,1,0:T(8,128)(2,1)S(1)}, u32[]{:S(2)}, u32[]{:S(2)}) collective-permute-start(bf16[10,192,128]{2,1,0:T(8,128)(2,1)S(1)} %get-tuple-element.59), channel_id=1, source_target_pairs={{0,2},{1,3},{2,0},{3,1},{4,6},{5,7},{6,4},{7,5},{8,10},{9,11},{10,... | collective-permute-start | bytes 1474568 | tf_op jit(solution)/shard_map/ppermute | solution.py:41
  17.3 22.0 %collective-permute-start.6 = (bf16[10,192,128]{2,1,0:T(8,128)(2,1)S(1)}, bf16[10,192,128]{2,1,0:T(8,128)(2,1)S(1)}, u32[]{:S(2)}, u32[]{:S(2)}) collective-permute-start(bf16[10,192,128]{2,1,0:T(8,128)(2,1)S(1)} %get-tuple-element.57), channel_id=1, source_target_pairs={{0,3},{1,0},{2,1},{3,2},{4,7},{5,4},{6,5},{7,6},{8,11},{9,8},{10,9... | collective-permute-start | bytes 1474568 | tf_op jit(solution)/shard_map/ppermute | solution.py:41
  20.3 20.3 %collective-permute-start.5 = (bf16[10,192,128]{2,1,0:T(8,128)(2,1)S(1)}, bf16[10,192,128]{2,1,0:T(8,128)(2,1)S(1)}, u32[]{:S(2)}, u32[]{:S(2)}) collective-permute-start(bf16[10,192,128]{2,1,0:T(8,128)(2,1)S(1)} %get-tuple-element.55), channel_id=1, source_target_pairs={{0,1},{1,2},{2,3},{3,0},{4,5},{5,6},{6,7},{7,4},{8,9},{9,10},{10,1... | collective-permute-start | bytes 1474568 | tf_op jit(solution)/shard_map/ppermute | solution.py:41
  20.5 20.4 %collective-permute-start.4 = (bf16[2,2,384,128]{3,2,1,0:T(8,128)(2,1)S(1)}, bf16[2,2,384,128]{3,2,1,0:T(8,128)(2,1)S(1)}, u32[]{:S(2)}, u32[]{:S(2)}) collective-permute-start(bf16[2,2,384,128]{3,2,1,0:T(8,128)(2,1)S(1)} %get-tuple-element.53), channel_id=1, source_target_pairs={{0,8},{4,12},{8,16},{12,20},{16,24},{20,28},{24,32},{28,36},{32,40... | collective-permute-start | bytes 1179656 | tf_op jit(solution)/shard_map/ppermute | solution.py:47
  24.3 20.0 %collective-permute-start.3 = (bf16[2,2,768,128]{3,2,1,0:T(8,128)(2,1)S(1)}, bf16[2,2,768,128]{3,2,1,0:T(8,128)(2,1)S(1)}, u32[]{:S(2)}, u32[]{:S(2)}) collective-permute-start(bf16[2,2,768,128]{3,2,1,0:T(8,128)(2,1)S(1)} %get-tuple-element.52.own_), channel_id=1, source_target_pairs={{0,4},{4,8},{8,12},{12,16},{16,20},{20,24},{24,28},{28,32},{32,36}... | collective-permute-start | bytes 2359304 | tf_op jit(solution)/shard_map/ppermute | solution.py:47
  40.8 12.0 %copy-start.4 = (s32[2,3]{1,0:T(2,128)S(1)}, s32[2,3]{1,0:T(2,128)}, u32[]{:S(2)}) copy-start(s32[2,3]{1,0:T(2,128)} %win.3) | copy-start | bytes 76
  44.3 26.7 %collective-permute-start.10 = (bf16[3,2,768,128]{3,2,1,0:T(8,128)(2,1)S(1)}, bf16[3,2,768,128]{3,2,1,0:T(8,128)(2,1)S(1)}, u32[]{:S(2)}, u32[]{:S(2)}) collective-permute-start(bf16[3,2,768,128]{3,2,1,0:T(8,128)(2,1)S(1)} %get-tuple-element.66.own_), channel_id=1, source_target_pairs={{0,4},{4,8},{8,12},{12,16},{16,20},{20,24},{24,28},{28,32},{32,36}... | collective-permute-start | bytes 3538952 | tf_op jit(solution)/shard_map/ppermute | solution.py:47
  46.4 24.6 %collective-permute-start.11 = (bf16[3,2,384,128]{3,2,1,0:T(8,128)(2,1)S(1)}, bf16[3,2,384,128]{3,2,1,0:T(8,128)(2,1)S(1)}, u32[]{:S(2)}, u32[]{:S(2)}) collective-permute-start(bf16[3,2,384,128]{3,2,1,0:T(8,128)(2,1)S(1)} %get-tuple-element.67), channel_id=1, source_target_pairs={{0,8},{4,12},{8,16},{12,20},{16,24},{20,28},{24,32},{28,36},{32,40... | collective-permute-start | bytes 1769480 | tf_op jit(solution)/shard_map/ppermute | solution.py:47
  48.3 13.9 %collective-permute-start.12 = (bf16[6,192,128]{2,1,0:T(8,128)(2,1)S(1)}, bf16[6,192,128]{2,1,0:T(8,128)(2,1)S(1)}, u32[]{:S(2)}, u32[]{:S(2)}) collective-permute-start(bf16[6,192,128]{2,1,0:T(8,128)(2,1)S(1)} %get-tuple-element.71), channel_id=1, source_target_pairs={{0,1},{1,2},{2,3},{3,0},{4,5},{5,6},{6,7},{7,4},{8,9},{9,10},{10,1... | collective-permute-start | bytes 884744 | tf_op jit(solution)/shard_map/ppermute | solution.py:41
  48.7 19.5 %collective-permute-start.13 = (bf16[6,192,128]{2,1,0:T(8,128)(2,1)S(1)}, bf16[6,192,128]{2,1,0:T(8,128)(2,1)S(1)}, u32[]{:S(2)}, u32[]{:S(2)}) collective-permute-start(bf16[6,192,128]{2,1,0:T(8,128)(2,1)S(1)} %get-tuple-element.72), channel_id=1, source_target_pairs={{0,3},{1,0},{2,1},{3,2},{4,7},{5,4},{6,5},{7,6},{8,11},{9,8},{10,9... | collective-permute-start | bytes 884744 | tf_op jit(solution)/shard_map/ppermute | solution.py:41
  51.6 19.4 %collective-permute-start.14 = (bf16[6,192,128]{2,1,0:T(8,128)(2,1)S(1)}, bf16[6,192,128]{2,1,0:T(8,128)(2,1)S(1)}, u32[]{:S(2)}, u32[]{:S(2)}) collective-permute-start(bf16[6,192,128]{2,1,0:T(8,128)(2,1)S(1)} %get-tuple-element.73), channel_id=1, source_target_pairs={{0,2},{1,3},{2,0},{3,1},{4,6},{5,7},{6,4},{7,5},{8,10},{9,11},{10,... | collective-permute-start | bytes 884744 | tf_op jit(solution)/shard_map/ppermute | solution.py:41
  62.2 22.9 %collective-permute-start.9 = (bf16[2,2,384,128]{3,2,1,0:T(8,128)(2,1)S(1)}, bf16[2,2,384,128]{3,2,1,0:T(8,128)(2,1)S(1)}, u32[]{:S(2)}, u32[]{:S(2)}) collective-permute-start(bf16[2,2,384,128]{3,2,1,0:T(8,128)(2,1)S(1)} %get-tuple-element.63), channel_id=1, source_target_pairs={{8,0},{12,4},{16,8},{20,12},{24,16},{28,20},{32,24},{36,28},{40,32... | collective-permute-start | bytes 1179656 | tf_op jit(solution)/shard_map/ppermute | solution.py:47
  68.2 16.8 %collective-permute-start.8 = (bf16[2,2,768,128]{3,2,1,0:T(8,128)(2,1)S(1)}, bf16[2,2,768,128]{3,2,1,0:T(8,128)(2,1)S(1)}, u32[]{:S(2)}, u32[]{:S(2)}) collective-permute-start(bf16[2,2,768,128]{3,2,1,0:T(8,128)(2,1)S(1)} %get-tuple-element.62), channel_id=1, source_target_pairs={{4,0},{8,4},{12,8},{16,12},{20,16},{24,20},{28,24},{32,28},{36,32}... | collective-permute-start | bytes 2359304 | tf_op jit(solution)/shard_map/ppermute | solution.py:47
  85.1 35.7 %collective-permute-start.18 = (bf16[3,2,768,128]{3,2,1,0:T(8,128)(2,1)S(1)}, bf16[3,2,768,128]{3,2,1,0:T(8,128)(2,1)S(1)}, u32[]{:S(2)}, u32[]{:S(2)}) collective-permute-start(bf16[3,2,768,128]{3,2,1,0:T(8,128)(2,1)S(1)} %get-tuple-element.87), channel_id=1, source_target_pairs={{4,0},{8,4},{12,8},{16,12},{20,16},{24,20},{28,24},{32,28},{36,32}... | collective-permute-start | bytes 3538952 | tf_op jit(solution)/shard_map/ppermute | solution.py:47
  92.8 27.9 %collective-permute-start.19 = (bf16[3,2,384,128]{3,2,1,0:T(8,128)(2,1)S(1)}, bf16[3,2,384,128]{3,2,1,0:T(8,128)(2,1)S(1)}, u32[]{:S(2)}, u32[]{:S(2)}) collective-permute-start(bf16[3,2,384,128]{3,2,1,0:T(8,128)(2,1)S(1)} %get-tuple-element.88), channel_id=1, source_target_pairs={{8,0},{12,4},{16,8},{20,12},{24,16},{28,20},{32,24},{36,28},{40,32... | collective-permute-start | bytes 1769480 | tf_op jit(solution)/shard_map/ppermute | solution.py:47
  96.1 28.4 %collective-permute-start.15 = (bf16[9,192,128]{2,1,0:T(8,128)(2,1)S(1)}, bf16[9,192,128]{2,1,0:T(8,128)(2,1)S(1)}, u32[]{:S(2)}, u32[]{:S(2)}) collective-permute-start(bf16[9,192,128]{2,1,0:T(8,128)(2,1)S(1)} %get-tuple-element.83), channel_id=1, source_target_pairs={{0,1},{1,2},{2,3},{3,0},{4,5},{5,6},{6,7},{7,4},{8,9},{9,10},{10,1... | collective-permute-start | bytes 1327112 | tf_op jit(solution)/shard_map/ppermute | solution.py:41
  96.5 29.1 %collective-permute-start.16 = (bf16[9,192,128]{2,1,0:T(8,128)(2,1)S(1)}, bf16[9,192,128]{2,1,0:T(8,128)(2,1)S(1)}, u32[]{:S(2)}, u32[]{:S(2)}) collective-permute-start(bf16[9,192,128]{2,1,0:T(8,128)(2,1)S(1)} %get-tuple-element.84), channel_id=1, source_target_pairs={{0,3},{1,0},{2,1},{3,2},{4,7},{5,4},{6,5},{7,6},{8,11},{9,8},{10,9... | collective-permute-start | bytes 1327112 | tf_op jit(solution)/shard_map/ppermute | solution.py:41
  99.5 26.2 %collective-permute-start.17 = (bf16[9,192,128]{2,1,0:T(8,128)(2,1)S(1)}, bf16[9,192,128]{2,1,0:T(8,128)(2,1)S(1)}, u32[]{:S(2)}, u32[]{:S(2)}) collective-permute-start(bf16[9,192,128]{2,1,0:T(8,128)(2,1)S(1)} %get-tuple-element.85), channel_id=1, source_target_pairs={{0,2},{1,3},{2,0},{3,1},{4,6},{5,7},{6,4},{7,5},{8,10},{9,11},{10,... | collective-permute-start | bytes 1327112 | tf_op jit(solution)/shard_map/ppermute | solution.py:41
  121.2 8.3 %collective-permute-start.20 = (bf16[6,192,128]{2,1,0:T(8,128)(2,1)S(1)}, bf16[6,192,128]{2,1,0:T(8,128)(2,1)S(1)}, u32[]{:S(2)}, u32[]{:S(2)}) collective-permute-start(bf16[6,192,128]{2,1,0:T(8,128)(2,1)S(1)} %get-tuple-element.90), channel_id=1, source_target_pairs={{0,1},{1,2},{2,3},{3,0},{4,5},{5,6},{6,7},{7,4},{8,9},{9,10},{10,1... | collective-permute-start | bytes 884744 | tf_op jit(solution)/shard_map/ppermute | solution.py:41
  121.6 10.3 %collective-permute-start.21 = (bf16[6,192,128]{2,1,0:T(8,128)(2,1)S(1)}, bf16[6,192,128]{2,1,0:T(8,128)(2,1)S(1)}, u32[]{:S(2)}, u32[]{:S(2)}) collective-permute-start(bf16[6,192,128]{2,1,0:T(8,128)(2,1)S(1)} %get-tuple-element.91), channel_id=1, source_target_pairs={{0,3},{1,0},{2,1},{3,2},{4,7},{5,4},{6,5},{7,6},{8,11},{9,8},{10,9... | collective-permute-start | bytes 884744 | tf_op jit(solution)/shard_map/ppermute | solution.py:41
  124.5 9.0 %collective-permute-start.22 = (bf16[6,192,128]{2,1,0:T(8,128)(2,1)S(1)}, bf16[6,192,128]{2,1,0:T(8,128)(2,1)S(1)}, u32[]{:S(2)}, u32[]{:S(2)}) collective-permute-start(bf16[6,192,128]{2,1,0:T(8,128)(2,1)S(1)} %get-tuple-element.92), channel_id=1, source_target_pairs={{0,2},{1,3},{2,0},{3,1},{4,6},{5,7},{6,4},{7,5},{8,10},{9,11},{10,... | collective-permute-start | bytes 884744 | tf_op jit(solution)/shard_map/ppermute | solution.py:41
  (4 other events, 13.2 us)
